TPU v7x, 32 devices: a whole 2x2x4 slice. The times are simulated.
32 devices in a mesh: dp: 8 (over y, x, core), tensor: 4 (over z).
Axes of the slice: x: 2, y: 2, z: 4, core: 2. Of those that a mesh axis runs over, the one named last changes fastest.
Arguments:
- hidden_in: bfloat16 [5632, 1024], P('dp', 'tensor'), may hold values from -9 to 9
- lengths: int32 [8], P('dp'), may hold values from 176 to 704, as said below
- w_query: bfloat16 [1024, 2048], P(None, 'tensor'), may hold values from -0.1875 to 0.1875
- w_key: bfloat16 [1024, 1024], P(None, 'tensor'), may hold values from -0.1875 to 0.1875
- w_value: bfloat16 [1024, 1024], P(None, 'tensor'), may hold values from -0.1875 to 0.1875
- w_out: bfloat16 [2048, 1024], P('tensor'), may hold values from -1 to 1
- attn_gain: float32 [1024], P('tensor'), may hold values from 0.5 to 1.5
- ffn_gain: float32 [1024], P('tensor'), may hold values from 0.5 to 1.5
- query_gain: float32 [128], replicated, may hold values from 0.5 to 1.5
- key_gain: float32 [128], replicated, may hold values from 0.5 to 1.5
- w_gate: bfloat16 [1024, 3072], P(None, 'tensor'), may hold values from -0.1875 to 0.1875
- w_up: bfloat16 [1024, 3072], P(None, 'tensor'), may hold values from -0.1875 to 0.1875
- w_down: bfloat16 [3072, 1024], P('tensor'), may hold values from -0.109375 to 0.109375
- cotangent: bfloat16 [5632, 1024], P('dp', 'tensor'), may hold values from -6 to 6
Outputs:
- out_rows: bfloat16 [5632, 1024], P('dp', 'tensor')
- input_grad: bfloat16 [5632, 1024], P('dp', 'tensor')
- grad_query: float32 [1024, 2048], P(None, 'tensor')
- grad_key: float32 [1024, 1024], P(None, 'tensor')
- grad_value: float32 [1024, 1024], P(None, 'tensor')
- grad_out: float32 [2048, 1024], P('tensor')
- grad_attn_gain: float32 [1024], P('tensor')
- grad_ffn_gain: float32 [1024], P('tensor')
- grad_query_gain: float32 [128], replicated
- grad_key_gain: float32 [128], replicated
- grad_gate: float32 [1024, 3072], P(None, 'tensor')
- grad_up: float32 [1024, 3072], P(None, 'tensor')
- grad_down: float32 [3072, 1024], P('tensor')
- stat_rms: float32 [3], replicated
Inputs may be any that keep to these rules, and one draw needn't show every extreme that they name: `lengths`: some sequence is full, with 704 valid tokens, and some has 176.
All inputs are finite; a program needn't handle non-finite values.
Results may differ from a plain program's by a relative error of at most 0.015.
Values may be sent and summed in bfloat16 or wider, within the bound.
No kernel may reach another device: no remote copies, remote signals or barrier semaphores. Data moves between devices by JAX's collectives and lax.ppermute only.
A program may use at most 128 MiB of HBM per device.

v0:
```python
import jax
import jax.numpy as jnp
from jax import lax
from jax.sharding import PartitionSpec as P

BLOCK = 256


NORM_EPSILON = 1e-06
ROPE_THETA = 1000000.0


def rope_tables(length, width):
    half_width = width // 2
    frequency = ROPE_THETA ** (-(jnp.arange(half_width, dtype=jnp.float32) * (2.0 / width)))
    angles = jnp.arange(length, dtype=jnp.float32)[:, None] * frequency[None, :]
    angles = jnp.concatenate([angles, angles], axis=1)
    return (jnp.cos(angles), jnp.sin(angles))


def rotate(values, cos_table, sin_table):
    half_width = values.shape[-1] // 2
    turned = jnp.concatenate([-values[..., half_width:], values[..., :half_width]], axis=-1)
    return values * cos_table[:, None, :] + turned * sin_table[:, None, :]


def unrotate(grad_rows, cos_table, sin_table):
    half_width = grad_rows.shape[-1] // 2
    turned = grad_rows * sin_table[:, None, :]
    back_turn = jnp.concatenate([turned[..., half_width:], -turned[..., :half_width]], axis=-1)
    return grad_rows * cos_table[:, None, :] + back_turn


def widen(local_rows):
    return lax.all_gather(local_rows, "tensor", axis=1, tiled=True)


def narrow(part_sums):
    return lax.psum_scatter(part_sums, "tensor", scatter_dimension=1, tiled=True)


def norm_scale(local_rows):
    total_sq = lax.psum(jnp.sum(local_rows * local_rows, axis=1), "tensor")
    full_width = local_rows.shape[1] * lax.axis_size("tensor")
    return lax.rsqrt(total_sq / full_width + NORM_EPSILON)[:, None]


def norm_back(local_rows, row_scale, gain_vec, grad_normed):
    weighted = grad_normed * gain_vec
    inner_sum = lax.psum(jnp.sum(weighted * local_rows, axis=1), "tensor")
    full_width = local_rows.shape[1] * lax.axis_size("tensor")
    grad_in = row_scale * weighted - local_rows * row_scale**3 * (inner_sum[:, None] / full_width)
    grad_gain = jnp.sum(grad_normed * local_rows * row_scale, axis=0)
    return (grad_in, grad_gain)


def head_scale(values):
    return lax.rsqrt(jnp.mean(values * values, axis=-1, keepdims=True) + NORM_EPSILON)


def head_back(values, row_scale, gain_vec, grad_rows):
    weighted = grad_rows * gain_vec
    inner_sum = jnp.mean(weighted * values, axis=-1, keepdims=True)
    return row_scale * weighted - values * row_scale**3 * inner_sum


def masked_scores(query_rows, key_rows, visible, scale_factor):
    scores = (
        jnp.einsum("sgrd,tgd->grst", query_rows, key_rows, preferred_element_type=jnp.float32)
        * scale_factor
    )
    return jnp.where(visible, scores, -1e30)


def per_device(
    hidden_in,
    lengths,
    w_query,
    w_key,
    w_value,
    w_out,
    attn_gain,
    ffn_gain,
    query_gain,
    key_gain,
    w_gate,
    w_up,
    w_down,
    cotangent,
):
    bf16 = jnp.bfloat16
    f32 = jnp.float32
    seq_len = hidden_in.shape[0]
    head_dim = query_gain.shape[0]
    head_count = w_query.shape[1] // head_dim
    kv_count = w_key.shape[1] // head_dim
    group_size = head_count // kv_count
    scale_factor = head_dim ** (-0.5)
    positions = jnp.arange(seq_len, dtype=jnp.int32)
    valid_rows = (positions < lengths[0]).astype(f32)[:, None]
    block_ids = positions // BLOCK
    visible = (block_ids[None, :] <= block_ids[:, None]) & (positions[None, :] < lengths[0])
    cos_table, sin_table = rope_tables(seq_len, head_dim)
    resid = hidden_in.astype(f32)
    scale_one = norm_scale(resid)
    full_one = widen((resid * scale_one * attn_gain).astype(bf16))
    query_pre = jnp.dot(full_one, w_query, preferred_element_type=f32).reshape(
        seq_len, head_count, head_dim
    )
    key_pre = jnp.dot(full_one, w_key, preferred_element_type=f32).reshape(
        seq_len, kv_count, head_dim
    )
    value_rows = (
        jnp.dot(full_one, w_value, preferred_element_type=f32)
        .astype(bf16)
        .reshape(seq_len, kv_count, head_dim)
    )
    query_scale = head_scale(query_pre)
    key_scale = head_scale(key_pre)
    query_rows = rotate(query_pre * query_scale * query_gain, cos_table, sin_table).astype(bf16)
    query_rows = query_rows.reshape(seq_len, kv_count, group_size, head_dim)
    key_rows = rotate(key_pre * key_scale * key_gain, cos_table, sin_table).astype(bf16)
    scores = masked_scores(query_rows, key_rows, visible, scale_factor)
    row_top = jnp.max(scores, axis=-1, keepdims=True)
    log_total = row_top + jnp.log(jnp.sum(jnp.exp(scores - row_top), axis=-1, keepdims=True))
    attn_probs = jnp.exp(scores - log_total)
    mixed_rows = jnp.einsum(
        "grst,tgd->sgrd", attn_probs.astype(bf16), value_rows, preferred_element_type=f32
    )
    mixed_rows = mixed_rows.reshape(seq_len, head_count * head_dim).astype(bf16)
    attn_local = narrow(jnp.dot(mixed_rows, w_out, preferred_element_type=f32))
    middle = resid + attn_local
    scale_two = norm_scale(middle)
    full_two = widen((middle * scale_two * ffn_gain).astype(bf16))
    gate_rows = jnp.dot(full_two, w_gate, preferred_element_type=f32)
    up_rows = jnp.dot(full_two, w_up, preferred_element_type=f32)
    gate_sig = jax.nn.sigmoid(gate_rows)
    silu_gate = gate_rows * gate_sig
    hidden = (silu_gate * up_rows).astype(bf16)
    ffn_local = narrow(jnp.dot(hidden, w_down, preferred_element_type=f32))
    out_full = middle + ffn_local
    first_rank = (lax.axis_index("tensor") == 0).astype(f32)
    full_width = hidden_in.shape[1] * lax.axis_size("tensor")
    local_totals = jnp.stack(
        [
            jnp.sum(valid_rows * out_full * out_full),
            jnp.sum(valid_rows * attn_local * attn_local),
            jnp.sum(valid_rows * ffn_local * ffn_local),
            first_rank * jnp.sum(valid_rows) * full_width,
        ]
    )
    grad_top = cotangent.astype(f32) * valid_rows
    grad_ffn_full = widen(grad_top.astype(bf16))
    grad_w_down = jnp.einsum("sf,sd->fd", hidden, grad_ffn_full, preferred_element_type=f32)
    grad_hidden = jnp.einsum("sd,fd->sf", grad_ffn_full, w_down, preferred_element_type=f32)
    grad_gate_rows = (
        grad_hidden * up_rows * (gate_sig * (1.0 + gate_rows * (1.0 - gate_sig)))
    ).astype(bf16)
    grad_up_rows = (grad_hidden * silu_gate).astype(bf16)
    grad_w_gate = jnp.einsum("sd,sf->df", full_two, grad_gate_rows, preferred_element_type=f32)
    grad_w_up = jnp.einsum("sd,sf->df", full_two, grad_up_rows, preferred_element_type=f32)
    grad_full_two = jnp.einsum("sf,df->sd", grad_gate_rows, w_gate, preferred_element_type=f32)
    grad_full_two = grad_full_two + jnp.einsum(
        "sf,df->sd", grad_up_rows, w_up, preferred_element_type=f32
    )
    grad_mid_norm, grad_ffn_gain = norm_back(middle, scale_two, ffn_gain, narrow(grad_full_two))
    grad_middle = grad_top + grad_mid_norm
    grad_attn_full = widen(grad_middle.astype(bf16))
    grad_w_out = jnp.einsum("sh,sd->hd", mixed_rows, grad_attn_full, preferred_element_type=f32)
    grad_mixed = jnp.einsum("sd,hd->sh", grad_attn_full, w_out, preferred_element_type=f32).astype(
        bf16
    )
    grad_mixed = grad_mixed.reshape(seq_len, kv_count, group_size, head_dim)
    again_probs = jnp.exp(masked_scores(query_rows, key_rows, visible, scale_factor) - log_total)
    grad_value_rows = jnp.einsum(
        "grst,sgrd->tgd", again_probs.astype(bf16), grad_mixed, preferred_element_type=f32
    ).astype(bf16)
    grad_probs = jnp.einsum("sgrd,tgd->grst", grad_mixed, value_rows, preferred_element_type=f32)
    grad_scores = (
        again_probs * (grad_probs - jnp.sum(again_probs * grad_probs, axis=-1, keepdims=True))
    ).astype(bf16)
    grad_query_rot = (
        jnp.einsum("grst,tgd->sgrd", grad_scores, key_rows, preferred_element_type=f32)
        * scale_factor
    )
    grad_key_rot = (
        jnp.einsum("grst,sgrd->tgd", grad_scores, query_rows, preferred_element_type=f32)
        * scale_factor
    )
    grad_query_norm = unrotate(
        grad_query_rot.reshape(seq_len, head_count, head_dim), cos_table, sin_table
    )
    grad_key_norm = unrotate(grad_key_rot, cos_table, sin_table)
    grad_query_gain = jnp.sum(grad_query_norm * query_pre * query_scale, axis=(0, 1))
    grad_key_gain = jnp.sum(grad_key_norm * key_pre * key_scale, axis=(0, 1))
    grad_query_pre = (
        head_back(query_pre, query_scale, query_gain, grad_query_norm)
        .reshape(seq_len, head_count * head_dim)
        .astype(bf16)
    )
    grad_key_pre = (
        head_back(key_pre, key_scale, key_gain, grad_key_norm)
        .reshape(seq_len, kv_count * head_dim)
        .astype(bf16)
    )
    grad_value_flat = grad_value_rows.reshape(seq_len, kv_count * head_dim)
    grad_w_query = jnp.einsum("sd,sh->dh", full_one, grad_query_pre, preferred_element_type=f32)
    grad_w_key = jnp.einsum("sd,sh->dh", full_one, grad_key_pre, preferred_element_type=f32)
    grad_w_value = jnp.einsum("sd,sh->dh", full_one, grad_value_flat, preferred_element_type=f32)
    grad_full_one = jnp.einsum("sh,dh->sd", grad_query_pre, w_query, preferred_element_type=f32)
    grad_full_one = grad_full_one + jnp.einsum(
        "sh,dh->sd", grad_key_pre, w_key, preferred_element_type=f32
    )
    grad_full_one = grad_full_one + jnp.einsum(
        "sh,dh->sd", grad_value_flat, w_value, preferred_element_type=f32
    )
    grad_in_norm, grad_attn_gain = norm_back(resid, scale_one, attn_gain, narrow(grad_full_one))
    input_grad = (grad_middle + grad_in_norm).astype(bf16)
    (
        grad_w_query,
        grad_w_key,
        grad_w_value,
        grad_w_out,
        grad_attn_gain,
        grad_ffn_gain,
        grad_w_gate,
        grad_w_up,
        grad_w_down,
        local_totals,
        grad_query_gain,
        grad_key_gain,
    ) = lax.psum(
        (
            grad_w_query,
            grad_w_key,
            grad_w_value,
            grad_w_out,
            grad_attn_gain,
            grad_ffn_gain,
            grad_w_gate,
            grad_w_up,
            grad_w_down,
            local_totals,
            grad_query_gain,
            grad_key_gain,
        ),
        "dp",
    )
    totals, grad_query_gain, grad_key_gain = lax.psum(
        (local_totals, grad_query_gain, grad_key_gain), "tensor"
    )
    stat_rms = jnp.sqrt(totals[:3] / totals[3])
    return (
        out_full.astype(bf16),
        input_grad,
        grad_w_query,
        grad_w_key,
        grad_w_value,
        grad_w_out,
        grad_attn_gain,
        grad_ffn_gain,
        grad_query_gain,
        grad_key_gain,
        grad_w_gate,
        grad_w_up,
        grad_w_down,
        stat_rms,
    )


def solution(mesh):
    return jax.shard_map(
        per_device,
        mesh=mesh,
        in_specs=(
            P("dp", "tensor"),
            P("dp"),
            P(None, "tensor"),
            P(None, "tensor"),
            P(None, "tensor"),
            P("tensor", None),
            P("tensor"),
            P("tensor"),
            P(),
            P(),
            P(None, "tensor"),
            P(None, "tensor"),
            P("tensor", None),
            P("dp", "tensor"),
        ),
        out_specs=(
            P("dp", "tensor"),
            P("dp", "tensor"),
            P(None, "tensor"),
            P(None, "tensor"),
            P(None, "tensor"),
            P("tensor", None),
            P("tensor"),
            P("tensor"),
            P(),
            P(),
            P(None, "tensor"),
            P(None, "tensor"),
            P("tensor", None),
            P(),
        ),
        check_vma=False,
    )
```

profile of v0, /device:TPU:0, one launch (start us, length us, event | category | flops | bytes accessed | tf_op | source)
XLA Modules:
  0.0 777.5 jit_solution(4223319322410031584)
XLA Ops:
  8.5 13.5 %psum.133 = f32[704]{0:T(1024)S(1)} all-reduce(f32[704]{0:T(1024)S(1)} %fusion.23), channel_id=1, replica_groups=mesh['dp'=8,'tensor'=4] {'tensor'}, use_global_device_ids=true, to_apply=%region_1.2 | all-reduce | flops 704 | bytes 5632 | tf_op jit(solution)/shard_map/psum | solution.py:43
  28.5 29.4 %all-gather.5.cloned.1.call-done = bf16[704,1024]{1,0:T(8,128)(2,1)} async-done(((bf16[704,256]{1,0:T(8,128)(2,1)}), bf16[704,1024]{1,0:T(8,128)(2,1)}) %all-gather.5.cloned.1.call-update) | async-done | bytes 1441808 | tf_op jit(solution)/shard_map/all_gather | solution.py:35
  57.9 3.7 fusion.73
  98.3 6.5 fusion.17
  109.4 3.9 fusion.74
  113.4 54.5 %reduce-scatter.5.cloned.1.call-done = f32[704,256]{1,0:T(8,128)} async-done(((f32[704,1024]{1,0:T(8,128)}), f32[704,256]{1,0:T(8,128)}) %reduce-scatter.5.cloned.1.call-update) | async-done | bytes 720912 | tf_op jit(solution)/shard_map/reduce_scatter | solution.py:39
  170.0 10.2 %psum.134 = f32[704]{0:T(1024)S(1)} all-reduce(f32[704]{0:T(1024)S(1)} %get-tuple-element.44), channel_id=1, replica_groups=mesh['dp'=8,'tensor'=4] {'tensor'}, use_global_device_ids=true, to_apply=%region_8.9 | all-reduce | flops 704 | bytes 5632 | tf_op jit(solution)/shard_map/psum | solution.py:43
  184.5 31.9 %all-gather.7.cloned.1.call-done = bf16[704,1024]{1,0:T(8,128)(2,1)} async-done(((bf16[704,256]{1,0:T(8,128)(2,1)}), bf16[704,1024]{1,0:T(8,128)(2,1)}) %all-gather.7.cloned.1.call-update) | async-done | bytes 1441808 | tf_op jit(solution)/shard_map/all_gather | solution.py:35
  216.4 4.6 fusion.75
  223.6 28.6 %all-gather.9.cloned.1.call-done = bf16[704,1024]{1,0:T(8,128)(2,1)} async-done(((bf16[704,256]{1,0:T(8,128)(2,1)}), bf16[704,1024]{1,0:T(8,128)(2,1)}) %all-gather.9.cloned.1.call-update) | async-done | bytes 1441808 | tf_op jit(solution)/shard_map/all_gather | solution.py:35
  252.2 5.8 multiply_convert_fusion
  263.2 4.1 fusion.77
  267.3 50.3 %reduce-scatter.9.cloned.1.call-done = f32[704,256]{1,0:T(8,128)} async-done(((f32[704,1024]{1,0:T(8,128)}), f32[704,256]{1,0:T(8,128)}) %reduce-scatter.9.cloned.1.call-update) | async-done | bytes 720912 | tf_op jit(solution)/shard_map/reduce_scatter | solution.py:39
  317.7 58.8 %reduce-scatter.7.cloned.1.call-done = f32[704,256]{1,0:T(8,128)} async-done(((f32[704,1024]{1,0:T(8,128)}), f32[704,256]{1,0:T(8,128)}) %reduce-scatter.7.cloned.1.call-update) | async-done | bytes 720912 | tf_op jit(solution)/shard_map/reduce_scatter | solution.py:39
  379.7 10.2 %psum.135 = f32[704]{0:T(1024)S(1)} all-reduce(f32[704]{0:T(1024)S(1)} %get-tuple-element.22), channel_id=1, replica_groups=mesh['dp'=8,'tensor'=4] {'tensor'}, use_global_device_ids=true, to_apply=%region_12.13 | all-reduce | flops 704 | bytes 5632 | tf_op jit(solution)/shard_map/psum | solution.py:50
  401.6 25.1 %all-gather.11.cloned.1.call-done = bf16[704,1024]{1,0:T(8,128)(2,1)} async-done(((bf16[704,256]{1,0:T(8,128)(2,1)}), bf16[704,1024]{1,0:T(8,128)(2,1)}) %all-gather.11.cloned.1.call-update) | async-done | bytes 1441808 | tf_op jit(solution)/shard_map/all_gather | solution.py:35
  429.6 6.9 fusion.19
  449.3 4.2 copy.150
  453.5 3.5 broadcast_multiply_fusion
  484.7 4.3 fusion.82
  506.4 31.5 %reduce-scatter.11.cloned.1.call-done = f32[704,256]{1,0:T(8,128)} async-done(((f32[704,1024]{1,0:T(8,128)}), f32[704,256]{1,0:T(8,128)}) %reduce-scatter.11.cloned.1.call-update) | async-done | bytes 720912 | tf_op jit(solution)/shard_map/reduce_scatter | solution.py:39
  539.5 14.1 %all-reduce = (f32[256]{0:T(256)}, f32[256]{0:T(256)}, f32[128]{0:T(128)S(1)}, f32[128]{0:T(128)S(1)}, f32[4]{0:T(128)S(1)}) all-reduce(f32[256]{0:T(256)S(1)} %get-tuple-element.18, f32[256]{0:T(256)S(1)} %get-tuple-element.23, f32[128]{0:T(128)S(1)} %bitcast_reduce_fusion, ...), channel_id=1, replica_groups=mesh['dp'=8,'tensor'=4] {'dp'}, use_global_device_ids=true, to_apply=%region_24.25 | all-reduce | flops 772 | bytes 6176 | tf_op jit(solution)/shard_map/psum | solution.py:232
  553.6 11.4 %all-reduce.2 = (f32[704]{0:T(1024)S(1)}, f32[128]{0:T(128)}, f32[128]{0:T(128)}, f32[4]{0:T(128)S(1)}) all-reduce(f32[704]{0:T(1024)S(1)} %get-tuple-element.19, f32[128]{0:T(128)S(1)} %get-tuple-element.27, f32[128]{0:T(128)S(1)} %get-tuple-element.28, f32[4]{0:T(128)S(1)} %get-tuple-element.29), channel_id=1, replica_groups=mesh['dp'=8,'tensor'=4] {'tensor'}, use_global_device_ids=true, to_apply=%region_18.19 | all-reduce | flops 964 | bytes 7712 | tf_op jit(solution)/shard_map/psum | solution.py:50
  567.8 185.0 %all-reduce.5.cloned.1.call-done = (f32[1024,512]{1,0:T(8,128)}, f32[1024,256]{1,0:T(8,128)}, f32[1024,256]{1,0:T(8,128)}, f32[512,1024]{1,0:T(8,128)}, f32[1024...) async-done(((f32[1024,512]{1,0:T(8,128)}, f32[1024,256]{1,0:T(8,128)}, f32[1024,256]{1,0:T(8,128)}, f32[512,1024]{1,0:T(8,128)}, f32[1024,768]{1,0:T(8,128)}, ...) | async-done | bytes 15728656 | tf_op jit(solution)/shard_map/psum | solution.py:232
  (262 shorter events, 159.4 us)
Async XLA Ops:
  7.2 245.0 %copy-start = (bf16[768,1024]{1,0:T(8,128)(2,1)S(1)}, bf16[768,1024]{1,0:T(8,128)(2,1)}, u32[]{:S(2)}) copy-start(bf16[768,1024]{1,0:T(8,128)(2,1)} %param.26) | copy-start | bytes 4718596
  7.2 50.7 %all-gather.5.cloned.1.call-start = ((), (), s32[]{:S(2)}) async-start(), calls=%async_computation.4 | async-start | bytes 1802240 | tf_op jit(solution)/shard_map/all_gather | solution.py:35
  23.9 144.0 %reduce-scatter.5.cloned.1.call-start = ((), (), s32[]{:S(2)}) async-start(), calls=%async_computation.5 | async-start | bytes 3604480 | tf_op jit(solution)/shard_map/reduce_scatter | solution.py:39
  26.3 35.2 %copy-start.12 = (f32[704,128]{0,1:T(8,128)}, f32[704,128]{0,1:T(8,128)S(1)}, u32[]{:S(2)}) copy-start(f32[704,128]{0,1:T(8,128)S(1)} %get-tuple-element.65) | copy-start | bytes 1081348
  26.3 35.2 %copy-start.21 = (f32[704,128]{0,1:T(8,128)}, f32[704,128]{0,1:T(8,128)S(1)}, u32[]{:S(2)}) copy-start(f32[704,128]{0,1:T(8,128)S(1)} %get-tuple-element.64) | copy-start | bytes 1081348
  113.3 54.6 %copy-start.11 = (bf16[704,256]{1,0:T(8,128)(2,1)S(1)}, bf16[704,256]{1,0:T(8,128)(2,1)}, u32[]{:S(2)}) copy-start(bf16[704,256]{1,0:T(8,128)(2,1)} %param.14) | copy-start | bytes 1081348
  113.3 66.9 %copy-start.58 = (f32[256]{0:T(256)S(1)}, f32[256]{0:T(256)}, u32[]{:S(2)}) copy-start(f32[256]{0:T(256)} %param.21) | copy-start | bytes 3076
  113.4 103.0 %all-gather.7.cloned.1.call-start = ((), (), s32[]{:S(2)}) async-start(), calls=%async_computation.6 | async-start | bytes 1802240 | tf_op jit(solution)/shard_map/all_gather | solution.py:35
  182.3 70.0 %all-gather.9.cloned.1.call-start = ((), (), s32[]{:S(2)}) async-start(), calls=%async_computation.8 | async-start | bytes 1802240 | tf_op jit(solution)/shard_map/all_gather | solution.py:35
  184.2 133.5 %reduce-scatter.9.cloned.1.call-start = ((), (), s32[]{:S(2)}) async-start(), calls=%async_computation.9 | async-start | bytes 3604480 | tf_op jit(solution)/shard_map/reduce_scatter | solution.py:39
  263.1 113.4 %reduce-scatter.7.cloned.1.call-start = ((), (), s32[]{:S(2)}) async-start(), calls=%async_computation.7 | async-start | bytes 3604480 | tf_op jit(solution)/shard_map/reduce_scatter | solution.py:39
  267.3 109.2 %copy-start.9 = (f32[704,256]{1,0:T(8,128)S(1)}, f32[704,256]{1,0:T(8,128)}, u32[]{:S(2)}) copy-start(f32[704,256]{1,0:T(8,128)} %get-tuple-element.45) | copy-start | bytes 2162692
  267.3 109.2 %copy-start.32 = (f32[704,256]{1,0:T(8,128)S(1)}, f32[704,256]{1,0:T(8,128)}, u32[]{:S(2)}) copy-start(f32[704,256]{1,0:T(8,128)} %reduce-scatter.5.cloned.1.call-done) | copy-start | bytes 2162692
  267.3 159.4 %all-gather.11.cloned.1.call-start = ((), (), s32[]{:S(2)}) async-start(), calls=%async_computation.10 | async-start | bytes 1802240 | tf_op jit(solution)/shard_map/all_gather | solution.py:35
  392.6 145.3 %reduce-scatter.11.cloned.1.call-start = ((), (), s32[]{:S(2)}) async-start(), calls=%async_computation.11 | async-start | bytes 3604480 | tf_op jit(solution)/shard_map/reduce_scatter | solution.py:39
  429.3 7.1 slice-start
  429.5 6.9 slice-start.1
  429.5 6.9 slice-start.2
  429.5 6.9 copy-start.48
  449.3 12.7 %copy-start.6 = (f32[704,2,2,128]{0,3,2,1:T(8,128)}, f32[704,2,2,128]{0,3,2,1:T(8,128)S(1)}, u32[]{:S(2)}) copy-start(f32[704,2,2,128]{0,3,2,1:T(8,128)S(1)} %copy.152) | copy-start | bytes 4325380
  483.3 269.5 %all-reduce.5.cloned.1.call-start = ((), (), s32[]{:S(2)}) async-start(), calls=%async_computation.12 | async-start | bytes 31457280 | tf_op jit(solution)/shard_map/psum | solution.py:232
  503.0 34.8 %copy-start.59 = (f32[256]{0:T(256)S(1)}, f32[256]{0:T(256)}, u32[]{:S(2)}) copy-start(f32[256]{0:T(256)} %param.20) | copy-start | bytes 3076
  503.0 63.7 %copy-start.34 = (f32[704,256]{1,0:T(8,128)S(1)}, f32[704,256]{1,0:T(8,128)}, u32[]{:S(2)}) copy-start(f32[704,256]{1,0:T(8,128)} %get-tuple-element.43) | copy-start | bytes 2162692
  537.9 28.9 %copy-start.33 = (f32[704,256]{1,0:T(8,128)S(1)}, f32[704,256]{1,0:T(8,128)}, u32[]{:S(2)}) copy-start(f32[704,256]{1,0:T(8,128)} %reduce-scatter.11.cloned.1.call-done) | copy-start | bytes 2162692
  (57 other events, 162.7 us)
Sparse Core Ops, SparseCore 0:
  24.0 33.7 all-gather.4
  113.5 54.4 reduce-scatter.4
  182.4 33.9 all-gather.6
  218.4 33.7 all-gather.8
  263.2 54.4 reduce-scatter.8
  320.4 56.0 reduce-scatter.6
  392.7 33.9 all-gather.10
  483.4 54.4 reduce-scatter.10
  543.9 208.8 all-reduce.4
where the time goes:
time: 786 us; the launch traced here: 778 us
  waiting for transfers between devices  495 us (63%)
  matrix products  83.9 us (11%)
  local copies, waits for them, and re-layouts  75 us (10%)
  blocking collectives  59.4 us (8%)
  other arithmetic  47.1 us (6%)
  between operations  16.1 us (2%)
    reduce_scatter x4, waiting for transfers between devices, narrow(): lax.psum_scatter(part_sums, 'tensor', scatter_dimension=1, tiled=True)  195 us
    psum x1, waiting for transfers between devices, per_device(): lax.psum((grad_w_query, grad_w_key, grad_w_value, grad_w_out, grad_attn_g...  185 us
    all_gather x4, waiting for transfers between devices, widen(): return lax.all_gather(local_rows, 'tensor', axis=1, tiled=True)  115 us
    unnamed x151, local copies, waits for them, and re-layouts  28.9 us
    psum x2, blocking collectives, norm_scale(): total_sq = lax.psum(jnp.sum(local_rows * local_rows, axis=1), 'tensor')  23.7 us
    psum x2, blocking collectives, norm_back(): inner_sum = lax.psum(jnp.sum(weighted * local_rows, axis=1), 'tensor')  21.6 us
  transfers between devices with their start and end apart: 9, of which 9 were waited for; matrix products, arithmetic and copies ran while one was open for 7% of the time, Pallas kernels for 0%

commit v1 on v0

v1 whole, which is shorter than its diff:
```python
import functools

import jax
import jax.numpy as jnp
from jax import lax
from jax.experimental import pallas as pl
from jax.experimental.pallas import tpu as pltpu
from jax.sharding import PartitionSpec as P

BLOCK = 256
NORM_EPSILON = 1e-06
ROPE_THETA = 1000000.0
LOG2E = 1.4426950408889634
NEG = -1e30
ROWS = 64
VMEM_BYTES = 48 * 1024 * 1024

bf16 = jnp.bfloat16
f32 = jnp.float32


def dot(a, b):
    return jnp.dot(a, b, preferred_element_type=f32)


def dot_t(a, b):
    return lax.dot_general(a, b, (((1,), (1,)), ((), ())), preferred_element_type=f32)


def t_dot(a, b):
    return lax.dot_general(a, b, (((0,), (0,)), ((), ())), preferred_element_type=f32)


def row_loop(count, step, body):
    def run(i, carry):
        body(pl.ds(pl.multiple_of(i * step, step), step))
        return carry

    lax.fori_loop(0, count // step, run, 0)


def rope_tables(length, width):
    half_width = width // 2
    frequency = ROPE_THETA ** (-(jnp.arange(half_width, dtype=f32) * (2.0 / width)))
    angles = jnp.arange(length, dtype=f32)[:, None] * frequency[None, :]
    cos, sin = jnp.cos(angles), jnp.sin(angles)
    return jnp.concatenate([cos, cos], axis=1), jnp.concatenate([-sin, sin], axis=1)


def query_units(seq_len):
    units = []
    start = 0
    while start < seq_len:
        rows = min(128, seq_len - start)
        keys = (start // BLOCK + 1) * BLOCK
        units.append((start, rows, keys))
        start += rows
    return units


def roles(z):
    low = z < 2
    return jnp.where(low, 2, 1), jnp.where(low, 3, 0), z + 1 - 2 * lax.rem(z, 2), z


def shard_slices(z, width):
    return [pl.ds(pl.multiple_of(shard * width, width), width) for shard in roles(z)]


def assemble(z, pieces, body):
    own, pair, across_mid, across_end, far_mid, far_end = pieces
    end = (z == 0) | (z == 3)

    @pl.when(end)
    def _():
        body((across_end, far_end, pair, own))

    @pl.when(jnp.logical_not(end))
    def _():
        body((across_mid, far_mid, pair, own))


def key_bias(length, keys):
    slot = lax.broadcasted_iota(jnp.int32, (1, keys), 1)
    return jnp.where(slot < length, 0.0, NEG).astype(f32)


def attn_forward_kernel(
    info_ref, x0, x1, x2, x3, x4, x5, gain_ref, wq_ref, wk_ref, wv_ref, wo_ref, qg_ref, kg_ref, cos_ref, sin_ref,
    n1_ref, qpre_ref, kpre_ref, qrot_ref, krot_ref, val_ref, mixed_ref, stat_ref, p_across, p_far, p_pair, p_own,
):
    seq_len, width = n1_ref.shape
    hd = qg_ref.shape[1]
    heads = wq_ref.shape[1] // hd
    kvs = wk_ref.shape[1] // hd
    group = heads // kvs
    padded = krot_ref.shape[0]
    length, z = info_ref[0], info_ref[1]
    scale = hd ** (-0.5) * LOG2E
    slices = shard_slices(z, width // 4)

    def normalise(refs):
        def norm(rows):
            xs = [ref[rows, :].astype(f32) for ref in refs]
            r1 = lax.rsqrt(sum(jnp.sum(x * x, axis=1, keepdims=True) for x in xs) / width + NORM_EPSILON)
            stat_ref[rows, heads : heads + 1] = r1
            for x, cols in zip(xs, slices):
                n1_ref[rows, cols] = (x * r1 * gain_ref[:, cols]).astype(bf16)

        row_loop(seq_len, ROWS, norm)

    assemble(z, (x0, x1, x2, x3, x4, x5), normalise)

    def project(w_ref, pre_ref, rot_ref, g_ref):
        count = w_ref.shape[1]
        for c in range(0, count, 2 * hd):
            pre_ref[:, c : c + 2 * hd] = dot(n1_ref[...], w_ref[:, c : c + 2 * hd])

        def rotate(rows):
            cos, sin = cos_ref[rows, :], sin_ref[rows, :]
            for c in range(0, count, hd):
                v = pre_ref[rows, c : c + hd]
                r = lax.rsqrt(jnp.mean(v * v, axis=1, keepdims=True) + NORM_EPSILON)
                v = v * r * g_ref[...]
                rot_ref[rows, c : c + hd] = (v * cos + pltpu.roll(v, hd // 2, 1) * sin).astype(bf16)

        row_loop(seq_len, ROWS, rotate)

    project(wk_ref, kpre_ref, krot_ref, kg_ref)
    val_ref[0:seq_len, :] = dot(n1_ref[...], wv_ref[...]).astype(bf16)
    if padded > seq_len:
        krot_ref[seq_len:padded, :] = jnp.zeros((padded - seq_len, kvs * hd), bf16)
        val_ref[seq_len:padded, :] = jnp.zeros((padded - seq_len, kvs * hd), bf16)
    project(wq_ref, qpre_ref, qrot_ref, qg_ref)

    for start, rows, keys in query_units(seq_len):
        bias = key_bias(length, keys)
        for g in range(kvs):
            key = krot_ref[0:keys, g * hd : (g + 1) * hd]
            val = val_ref[0:keys, g * hd : (g + 1) * hd]
            first = g * group
            q = jnp.concatenate(
                [qrot_ref[start : start + rows, h * hd : (h + 1) * hd] for h in range(first, first + group)], axis=0
            )
            e = jnp.exp2(dot_t(q, key) * scale + bias)
            total = jnp.sum(e, axis=1, keepdims=True)
            mixed = dot(e.astype(bf16), val) * (1.0 / total)
            lse = jnp.log2(total)
            for r in range(group):
                h = first + r
                mixed_ref[start : start + rows, h * hd : (h + 1) * hd] = mixed[r * rows : (r + 1) * rows].astype(bf16)
                stat_ref[start : start + rows, h : h + 1] = lse[r * rows : (r + 1) * rows]

    for part_ref, cols in zip((p_across, p_far, p_pair, p_own), slices):
        part_ref[...] = dot(mixed_ref[...], wo_ref[:, cols]).astype(part_ref.dtype)


def norm_back(grad_s, normed_ref, row_scale, inner_s, gain_ref, part_ref, gain_grad_ref, cols, width):
    seq_len, step = grad_s.shape
    gain = gain_ref[:, cols]
    inverse = 1.0 / gain

    def finish(i, acc):
        rows = pl.ds(pl.multiple_of(i * ROWS, ROWS), ROWS)
        grad = grad_s[rows, :]
        unit = normed_ref[rows, cols].astype(f32) * inverse
        coef = inner_s[rows, 0:1] * (1.0 / width)
        part_ref[rows, :] = (row_scale(rows) * (grad * gain - unit * coef)).astype(part_ref.dtype)
        return acc + jnp.sum((grad * unit).reshape(ROWS // 8, 8, step), axis=0)

    gain_grad_ref[:, cols] = lax.fori_loop(0, seq_len // ROWS, finish, jnp.zeros((8, step), f32))


def ffn_kernel(
    info_ref, m0, m1, m2, m3, m4, m5, gain_ref, wg_ref, wu_ref, wd_ref, c0, c1, c2, c3, c4, c5,
    n2_ref, cotm_ref, hid_ref, dgu_ref, p_across, p_far, p_pair, p_own, gfg_ref,
    gate_s, up_s, gh_s, inner_s, r2_s,
):
    seq_len, width = n2_ref.shape
    hidden = wg_ref.shape[1]
    length, z = info_ref[0], info_ref[1]
    step = gate_s.shape[1]
    slices = shard_slices(z, width // 4)

    def normalise(refs):
        def norm(rows):
            ms = [ref[rows, :].astype(f32) for ref in refs]
            r2 = lax.rsqrt(sum(jnp.sum(m * m, axis=1, keepdims=True) for m in ms) / width + NORM_EPSILON)
            r2_s[rows, :] = jnp.broadcast_to(r2, (ROWS, 128))
            inner_s[rows, :] = jnp.zeros((ROWS, 128), f32)
            for m, cols in zip(ms, slices):
                n2_ref[rows, cols] = (m * r2 * gain_ref[:, cols]).astype(bf16)

        row_loop(seq_len, ROWS, norm)

    def mask(refs):
        def one(rows):
            slot = rows.start + lax.broadcasted_iota(jnp.int32, (ROWS, 1), 0)
            for ref, cols in zip(refs, slices):
                cotm_ref[rows, cols] = jnp.where(slot < length, ref[rows, :].astype(f32), 0.0).astype(bf16)

        row_loop(seq_len, ROWS, one)

    assemble(z, (m0, m1, m2, m3, m4, m5), normalise)
    assemble(z, (c0, c1, c2, c3, c4, c5), mask)

    for j in range(0, hidden, step):
        gate_s[...] = dot(n2_ref[...], wg_ref[:, j : j + step])
        up_s[...] = dot(n2_ref[...], wu_ref[:, j : j + step])
        gh_s[...] = dot_t(cotm_ref[...], wd_ref[j : j + step, :])

        def elementwise(rows):
            gate, up, gh = gate_s[rows, :], up_s[rows, :], gh_s[rows, :]
            sig = jax.nn.sigmoid(gate)
            silu = gate * sig
            hid_ref[rows, j : j + step] = (silu * up).astype(bf16)
            dg = (gh * up * (sig * (1.0 + gate * (1.0 - sig)))).astype(bf16)
            du = (gh * silu).astype(bf16)
            dgu_ref[rows, j : j + step] = dg
            dgu_ref[rows, hidden + j : hidden + j + step] = du
            inner = jnp.sum(dg.astype(f32) * gate + du.astype(f32) * up, axis=1, keepdims=True)
            inner_s[rows, :] += jnp.broadcast_to(inner, (ROWS, 128))

        row_loop(seq_len, ROWS, elementwise)

    for part_ref, cols in zip((p_across, p_far, p_pair, p_own), slices):
        gate_s[...] = dot_t(dgu_ref[:, 0:hidden], wg_ref[cols, :]) + dot_t(
            dgu_ref[:, hidden : 2 * hidden], wu_ref[cols, :]
        )
        norm_back(
            gate_s, n2_ref, lambda rows: r2_s[rows, 0:1], inner_s, gain_ref, part_ref, gfg_ref, cols, width
        )


def attn_backward_kernel(
    info_ref, g0, g1, g2, g3, g4, g5, n1_ref, gain_ref, wq_ref, wk_ref, wv_ref, wo_ref, qg_ref, kg_ref, cos_ref,
    sin_ref, qpre_ref, kpre_ref, qrot_ref, krot_ref, val_ref, mixed_ref, stat_ref,
    ga_ref, dqkv_ref, p_across, p_far, p_pair, p_own, gag_ref, qgg_ref, kgg_ref,
    gm_s, dq_s, dk_s, dv_s, acc_s, inner_s,
):
    seq_len, width = n1_ref.shape
    hd = qg_ref.shape[1]
    heads = wq_ref.shape[1] // hd
    kvs = wk_ref.shape[1] // hd
    group = heads // kvs
    length, z = info_ref[0], info_ref[1]
    scale = hd ** (-0.5)
    qw, kw = heads * hd, kvs * hd
    slices = shard_slices(z, width // 4)

    def collect(refs):
        for ref, cols in zip(refs, slices):
            ga_ref[:, cols] = ref[...]

    assemble(z, (g0, g1, g2, g3, g4, g5), collect)

    for c in range(0, qw, 256):
        gm_s[:, c : c + 256] = dot_t(ga_ref[...], wo_ref[c : c + 256, :]).astype(bf16)
    dk_s[...] = jnp.zeros_like(dk_s)
    dv_s[...] = jnp.zeros_like(dv_s)

    for start, rows, keys in query_units(seq_len):
        bias = key_bias(length, keys)
        for g in range(kvs):
            first = g * group
            cols = slice(g * hd, (g + 1) * hd)
            key, val = krot_ref[0:keys, cols], val_ref[0:keys, cols]

            def stacked(ref):
                return jnp.concatenate(
                    [ref[start : start + rows, h * hd : (h + 1) * hd] for h in range(first, first + group)], axis=0
                )

            q, gm, mixed = stacked(qrot_ref), stacked(gm_s), stacked(mixed_ref)
            lse = jnp.concatenate(
                [stat_ref[start : start + rows, h : h + 1] for h in range(first, first + group)], axis=0
            )
            p = jnp.exp2(dot_t(q, key) * (scale * LOG2E) + bias - lse)
            delta = jnp.sum(gm.astype(f32) * mixed.astype(f32), axis=1, keepdims=True)
            ds = (p * (dot_t(gm, val) - delta)).astype(bf16)
            dv_s[0:keys, cols] += t_dot(p.astype(bf16), gm)
            dk_s[0:keys, cols] += t_dot(ds, q)
            dq = dot(ds, key)
            for r in range(group):
                h = first + r
                dq_s[start : start + rows, h * hd : (h + 1) * hd] = dq[r * rows : (r + 1) * rows]

    def unrotate(rows, rot_s, pre_ref, g_ref, count, base):
        cos, sin = cos_ref[rows, :], sin_ref[rows, :]
        inner = jnp.zeros((ROWS, 1), f32)
        gain_sum = jnp.zeros((8, hd), f32)
        for c in range(0, count, hd):
            g = rot_s[rows, c : c + hd] * scale
            u = g * cos + pltpu.roll(g * sin, hd // 2, 1)
            v = pre_ref[rows, c : c + hd]
            r = lax.rsqrt(jnp.mean(v * v, axis=1, keepdims=True) + NORM_EPSILON)
            gain_sum = gain_sum + jnp.sum((u * v * r).reshape(ROWS // 8, 8, hd), axis=0)
            w = u * g_ref[...]
            mean = jnp.mean(w * v, axis=1, keepdims=True)
            d = (r * w - v * (r * r * r * mean)).astype(bf16)
            dqkv_ref[rows, base + c : base + c + hd] = d
            inner = inner + jnp.sum(d.astype(f32) * v, axis=1, keepdims=True)
        return inner, gain_sum

    def heads_back(i, carry):
        rows = pl.ds(pl.multiple_of(i * ROWS, ROWS), ROWS)
        qi, qgs = unrotate(rows, dq_s, qpre_ref, qg_ref, qw, 0)
        ki, kgs = unrotate(rows, dk_s, kpre_ref, kg_ref, kw, qw)
        dv = dv_s[rows, :].astype(bf16)
        dqkv_ref[rows, qw + kw : qw + 2 * kw] = dv
        vi = jnp.sum(dv.astype(f32) * val_ref[rows, :].astype(f32), axis=1, keepdims=True)
        inner_s[rows, :] = jnp.broadcast_to(qi + ki + vi, (ROWS, 128))
        return carry[0] + qgs, carry[1] + kgs

    zero = jnp.zeros((8, hd), f32)
    qgs, kgs = lax.fori_loop(0, seq_len // ROWS, heads_back, (zero, zero))
    qgg_ref[...] = qgs
    kgg_ref[...] = kgs

    for part_ref, cols in zip((p_across, p_far, p_pair, p_own), slices):
        acc_s[...] = (
            dot_t(dqkv_ref[:, 0:qw], wq_ref[cols, :])
            + dot_t(dqkv_ref[:, qw : qw + kw], wk_ref[cols, :])
            + dot_t(dqkv_ref[:, qw + kw : qw + 2 * kw], wv_ref[cols, :])
        )
        norm_back(
            acc_s, n1_ref, lambda rows: stat_ref[rows, heads : heads + 1], inner_s, gain_ref, part_ref, gag_ref,
            cols, width,
        )


def call(body, outs, args, scratch=(), flops=0, bytes_accessed=0):
    spec = pl.BlockSpec(memory_space=pltpu.VMEM)
    return pl.pallas_call(
        body,
        out_shape=[jax.ShapeDtypeStruct(s, d) for s, d in outs],
        in_specs=[pl.BlockSpec(memory_space=pltpu.SMEM)] + [spec] * (len(args) - 1),
        out_specs=[spec] * len(outs),
        scratch_shapes=[pltpu.VMEM(s, d) for s, d in scratch],
        compiler_params=pltpu.CompilerParams(vmem_limit_bytes=VMEM_BYTES),
        cost_estimate=pl.CostEstimate(flops=flops, bytes_accessed=bytes_accessed, transcendentals=0),
    )(*args)


PAIRS = ((0, 1), (1, 0), (2, 3), (3, 2))
MIDDLE = ((1, 2), (2, 1))
OUTWARD = ((1, 0), (2, 3))
INWARD = ((0, 1), (3, 2))
OUTWARD_TWO = ((2, 0), (1, 3))
INWARD_TWO = ((0, 2), (3, 1))


def send(rows, pairs):
    return lax.ppermute(rows, "tensor", pairs)


def gather_line(own):
    pair = send(own, PAIRS)
    across_mid = send(own, MIDDLE)
    across_end = send(across_mid, OUTWARD)
    far_end = send(pair, OUTWARD_TWO)
    far_mid = send(pair, MIDDLE)
    return own, pair, across_mid, across_end, far_mid, far_end


def scatter_line(across, far, pair, own):
    one = send(across, INWARD)
    two = send(far, INWARD_TWO)
    three = send(far, MIDDLE)
    to_pair = (pair.astype(f32) + (two.astype(f32) + three.astype(f32))).astype(bf16)
    to_across = (across.astype(f32) + one.astype(f32)).astype(bf16)
    from_pair = send(to_pair, PAIRS)
    from_across = send(to_across, MIDDLE)
    return own.astype(f32) + (from_pair.astype(f32) + from_across.astype(f32))


def per_device(
    hidden_in, lengths, w_query, w_key, w_value, w_out, attn_gain, ffn_gain,
    query_gain, key_gain, w_gate, w_up, w_down, cotangent,
):
    seq_len, shard = hidden_in.shape
    width = w_query.shape[0]
    hd = query_gain.shape[0]
    qw, kw = w_query.shape[1], w_key.shape[1]
    hidden = w_gate.shape[1]
    padded = -(-seq_len // BLOCK) * BLOCK
    z = lax.axis_index("tensor").astype(jnp.int32)
    info = jnp.stack([lengths[0], z])
    parts = [((seq_len, shard), bf16)] * 4

    x_parts = gather_line(hidden_in)
    gains = lax.all_gather(jnp.stack([attn_gain, ffn_gain]), "tensor", axis=1, tiled=True)
    gain_one, gain_two = gains[0:1], gains[1:2]
    cot_parts = gather_line(cotangent)
    cos, sin = rope_tables(seq_len, hd)
    qg, kg = query_gain[None], key_gain[None]
    resid = hidden_in.astype(f32)
    valid = (jnp.arange(seq_len, dtype=jnp.int32) < lengths[0]).astype(f32)[:, None]

    n1, qpre, kpre, qrot, krot, val, mixed, stat, *attn_parts = call(
        attn_forward_kernel,
        [
            ((seq_len, width), bf16), ((seq_len, qw), f32), ((seq_len, kw), f32), ((seq_len, qw), bf16),
            ((padded, kw), bf16), ((padded, kw), bf16), ((seq_len, qw), bf16), ((seq_len, 128), f32),
        ] + parts,
        (info, *x_parts, gain_one, w_query, w_key, w_value, w_out, qg, kg, cos, sin),
        flops=2 * seq_len * width * (2 * qw + 2 * kw) + 4 * seq_len * seq_len * qw,
        bytes_accessed=14_000_000,
    )
    attn_local = scatter_line(*attn_parts)
    middle = resid + attn_local
    m_parts = gather_line(middle.astype(bf16))

    n2, cotm, hid, dgu, *ffn_parts, gfg = call(
        ffn_kernel,
        [
            ((seq_len, width), bf16), ((seq_len, width), bf16), ((seq_len, hidden), bf16),
            ((seq_len, 2 * hidden), bf16),
        ] + parts + [((8, width), f32)],
        (info, *m_parts, gain_two, w_gate, w_up, w_down, *cot_parts),
        scratch=[((seq_len, 256), f32)] * 3 + [((seq_len, 128), f32)] * 2,
        flops=2 * seq_len * width * hidden * 5,
        bytes_accessed=16_000_000,
    )
    grad_top = cotangent.astype(f32) * valid
    grad_middle = grad_top + scatter_line(*ffn_parts)
    ga_parts = gather_line(grad_middle.astype(bf16))

    down = [
        dot(hid, lax.dynamic_slice(w_down, (0, s * shard), (hidden, shard))).astype(bf16) for s in roles(z)
    ]
    ffn_local = scatter_line(*down)
    out_full = middle + ffn_local
    g_down = t_dot(hid, cotm).astype(bf16)
    g_gu = t_dot(n2, dgu).astype(bf16)
    g_down, g_gu = lax.psum((g_down, g_gu), "dp")

    ga, dqkv, *back_parts, gag, qgg, kgg = call(
        attn_backward_kernel,
        [((seq_len, width), bf16), ((seq_len, qw + 2 * kw), bf16)] + parts
        + [((8, width), f32), ((8, hd), f32), ((8, hd), f32)],
        (
            info, *ga_parts, n1, gain_one, w_query, w_key, w_value, w_out, qg, kg, cos, sin,
            qpre, kpre, qrot, krot, val, mixed, stat,
        ),
        scratch=[
            ((seq_len, qw), bf16), ((seq_len, qw), f32), ((padded, kw), f32), ((padded, kw), f32),
            ((seq_len, shard), f32), ((seq_len, 128), f32),
        ],
        flops=2 * seq_len * width * (2 * qw + 2 * kw) + 10 * seq_len * seq_len * qw,
        bytes_accessed=16_000_000,
    )
    input_grad = (grad_middle + scatter_line(*back_parts)).astype(bf16)
    g_out = t_dot(mixed, ga).astype(bf16)
    g_qkv = t_dot(n1, dqkv).astype(bf16)
    (g_down, g_gu, g_out, g_qkv) = lax.optimization_barrier((g_down, g_gu, g_out, g_qkv))
    g_out, g_qkv = lax.psum((g_out, g_qkv), "dp")

    first_rank = (z == 0).astype(f32)
    totals = jnp.stack(
        [
            jnp.sum(valid * out_full * out_full),
            jnp.sum(valid * attn_local * attn_local),
            jnp.sum(valid * ffn_local * ffn_local),
            first_rank * jnp.sum(valid) * width,
        ]
    )
    small = jnp.concatenate(
        [jnp.sum(gag, axis=0), jnp.sum(gfg, axis=0), jnp.sum(qgg, axis=0), jnp.sum(kgg, axis=0), totals]
    )
    small = lax.psum(small, ("dp", "tensor"))
    mine = z * shard
    grad_attn_gain = lax.dynamic_slice(small, (mine,), (shard,))
    grad_ffn_gain = lax.dynamic_slice(small, (width + mine,), (shard,))
    rest = small[2 * width :]
    totals = rest[2 * hd :]
    stat_rms = jnp.sqrt(totals[:3] / totals[3])
    return (
        out_full.astype(bf16),
        input_grad,
        g_qkv[:, :qw].astype(f32),
        g_qkv[:, qw : qw + kw].astype(f32),
        g_qkv[:, qw + kw :].astype(f32),
        g_out.astype(f32),
        grad_attn_gain,
        grad_ffn_gain,
        rest[:hd],
        rest[hd : 2 * hd],
        g_gu[:, :hidden].astype(f32),
        g_gu[:, hidden:].astype(f32),
        g_down.astype(f32),
        stat_rms,
    )


def solution(mesh):
    rows, cols, first = P("dp", "tensor"), P(None, "tensor"), P("tensor", None)
    gain = P("tensor")
    return jax.shard_map(
        per_device,
        mesh=mesh,
        in_specs=(rows, P("dp"), cols, cols, cols, first, gain, gain, P(), P(), cols, cols, first, rows),
        out_specs=(rows, rows, cols, cols, cols, first, gain, gain, P(), P(), cols, cols, first, P()),
        check_vma=False,
    )
```

time: 786 us -> 386 us (0.49)
  waiting for transfers between devices: 495 us -> 78.8 us
  starting transfers between devices: 0.76 us -> 102 us
  local copies, waits for them, and re-layouts: 75 us -> 8.89 us
  Pallas kernels: 0 us -> 66.1 us
  matrix products: 83.9 us -> 23.2 us
  other arithmetic: 47.1 us -> 25 us
    reduce_scatter x4 -> x0, waiting for transfers between devices: 195 us -> none  [narrow(): lax.psum_scatter(part_sums, 'tensor', scatter_dimension=1, tiled=True)]
    psum x1 -> x2, waiting for transfers between devices: 185 us -> 27.3 us  [the longest x1 17.4 us: per_device(): g_out, g_qkv = lax.psum((g_out, g_qkv), 'dp')]
    all_gather x4 -> x0, waiting for transfers between devices: 115 us -> none  [widen(): return lax.all_gather(local_rows, 'tensor', axis=1, tiled=True)]
    ppermute x0 -> x40, starting transfers between devices: none -> 102 us  [send(): return lax.ppermute(rows, 'tensor', pairs)]
    pallas_call x0 -> x3, Pallas kernels: none -> 66.1 us  [call(): pl.pallas_call(body, out_shape=[jax.ShapeDtypeStruct(s, d) for s, d in ou...]
    dot_general x27 -> x8, matrix products: 83.9 us -> 23.2 us  [the longest x4 13.1 us: t_dot(): lax.dot_general(a, b, (((0,), (0,)), ((), ())), preferred_element_type=f32)]
    ppermute x0 -> x40, waiting for transfers between devices: none -> 51.4 us  [send(): return lax.ppermute(rows, 'tensor', pairs)]
    all_gather x0 -> x1, blocking collectives: none -> 24.1 us  [per_device(): lax.all_gather(jnp.stack([attn_gain, ffn_gain]), 'tensor', axis=1, tiled=...]
  transfers between devices with their start and end apart: 9 -> 42, of which waited for: 9 -> 14; matrix products, arithmetic and copies ran while one was open for 7% -> 12% of each run, Pallas kernels for 0% -> 7%
where the time goes in v1:
time: 386 us; the launch traced here: 384 us
  starting transfers between devices  102 us (26%)
  waiting for transfers between devices  78.8 us (20%)
  Pallas kernels  66.1 us (17%)
  blocking collectives  64.2 us (17%)
  other arithmetic  25 us (6%)
  matrix products  23.2 us (6%)
  between operations  16 us (4%)
  local copies, waits for them, and re-layouts  8.89 us (2%)
    ppermute x40, starting transfers between devices, send(): return lax.ppermute(rows, 'tensor', pairs)  102 us
    pallas_call x3, Pallas kernels, call(): pl.pallas_call(body, out_shape=[jax.ShapeDtypeStruct(s, d) for s, d in ou...  66.1 us
    ppermute x40, waiting for transfers between devices, send(): return lax.ppermute(rows, 'tensor', pairs)  51.4 us
    psum x1, blocking collectives, per_device(): small = lax.psum(small, ('dp', 'tensor'))  40.1 us
    all_gather x1, blocking collectives, per_device(): lax.all_gather(jnp.stack([attn_gain, ffn_gain]), 'tensor', axis=1, tiled=...  24.1 us
    psum x1, waiting for transfers between devices, per_device(): g_out, g_qkv = lax.psum((g_out, g_qkv), 'dp')  17.4 us
    dot_general x4, matrix products, t_dot(): lax.dot_general(a, b, (((0,), (0,)), ((), ())), preferred_element_type=f32)  13.1 us
    dot_general x4, matrix products, dot(): return jnp.dot(a, b, preferred_element_type=f32)  10.1 us
  transfers between devices with their start and end apart: 42, of which 14 were waited for; matrix products, arithmetic and copies ran while one was open for 12% of the time, Pallas kernels for 7%

profile of v1, /device:TPU:0, one launch (start us, length us, event | category | flops | bytes accessed | tf_op | source)
XLA Modules:
  0.0 384.5 jit_solution(7379341559859041716)
XLA Ops:
  13.8 5.2 %collective-permute-done.x1 = bf16[704,256]{1,0:T(8,128)(2,1)S(1)} collective-permute-done((bf16[704,256]{1,0:T(8,128)(2,1)}, bf16[704,256]{1,0:T(8,128)(2,1)S(1)}, u32[]{:S(2)}, u32[]{:S(2)}) %collective-permute-start) | collective-permute-done | bytes 360480 | tf_op jit(solution)/shard_map/ppermute | solution.py:354
  22.3 24.1 %all_gather.3 = f32[2,1024]{1,0:T(2,128)S(1)} all-gather(f32[2,256]{1,0:T(2,128)S(1)} %pad_maximum_fusion.2), channel_id=1, replica_groups=mesh['dp'=8,'tensor'=4] {'tensor'}, dimensions={1}, use_global_device_ids=true | all-gather | bytes 10240 | tf_op jit(solution)/shard_map/all_gather | solution.py:392
  46.8 14.8 %shard_map.245 = (bf16[704,1024]{1,0:T(8,128)(2,1)}, f32[704,512]{1,0:T(8,128)}, f32[704,256]{1,0:T(8,128)}, bf16[704,512]{1,0:T(8,128)(2,1)}, bf16[768,256]{1,0...) custom-call(s32[2]{0:T(128)S(1)} %pad_add_fusion.info_ref, ...), custom_call_target="tpu_custom_call" | custom-call | flops 3229614080 | bytes 14000000 | tf_op jit(solution)/shard_map/pallas_call | solution.py:334
  62.5 6.0 %collective-permute-start.5 = (bf16[704,256]{1,0:T(8,128)(2,1)S(1)}, bf16[704,256]{1,0:T(8,128)(2,1)S(1)}, u32[]{:S(2)}, u32[]{:S(2)}) collective-permute-start(bf16[704,256]{1,0:T(8,128)(2,1)S(1)} %get-tuple-element.50), channel_id=1, source_target_pairs={{0,2},{3,1},{4,6},{7,5},{8,10},{11,9},{12,14},{15,13},{16,18},{19,... | collective-permute-start | bytes 1081352 | tf_op jit(solution)/shard_map/ppermute | solution.py:354
  69.9 7.5 %collective-permute-done.5 = bf16[704,256]{1,0:T(8,128)(2,1)S(1)} collective-permute-done((bf16[704,256]{1,0:T(8,128)(2,1)S(1)}, bf16[704,256]{1,0:T(8,128)(2,1)S(1)}, u32[]{:S(2)}, u32[]{:S(2)}) %collective-permute-start.5) | collective-permute-done | bytes 360480 | tf_op jit(solution)/shard_map/ppermute | solution.py:354
  77.5 4.0 %collective-permute-start.7 = (bf16[704,256]{1,0:T(8,128)(2,1)S(1)}, bf16[704,256]{1,0:T(8,128)(2,1)S(1)}, u32[]{:S(2)}, u32[]{:S(2)}) collective-permute-start(bf16[704,256]{1,0:T(8,128)(2,1)S(1)} %add_convert_fusion.7), channel_id=1, source_target_pairs={{0,1},{1,0},{2,3},{3,2},{4,5},{5,4},{6,7},{7,6},{8,9},{9,8},{10,11... | collective-permute-start | bytes 1081352 | tf_op jit(solution)/shard_map/ppermute | solution.py:354
  86.6 7.0 %collective-permute-start.15 = (bf16[704,256]{1,0:T(8,128)(2,1)S(1)}, bf16[704,256]{1,0:T(8,128)(2,1)S(1)}, u32[]{:S(2)}, u32[]{:S(2)}) collective-permute-start(bf16[704,256]{1,0:T(8,128)(2,1)S(1)} %copy-done.1), channel_id=1, source_target_pairs={{0,1},{1,0},{2,3},{3,2},{4,5},{5,4},{6,7},{7,6},{8,9},{9,8},{10,11... | collective-permute-start | bytes 1081352 | tf_op jit(solution)/shard_map/ppermute | solution.py:354
  95.3 7.9 %collective-permute-start.10 = (bf16[704,256]{1,0:T(8,128)(2,1)S(1)}, bf16[704,256]{1,0:T(8,128)(2,1)}, u32[]{:S(2)}, u32[]{:S(2)}) collective-permute-start(bf16[704,256]{1,0:T(8,128)(2,1)S(1)} %fusion.9.m0), channel_id=1, source_target_pairs={{0,1},{1,0},{2,3},{3,2},{4,5},{5,4},{6,7},{7,6},{8,9},{9,8},{10,11... | collective-permute-start | bytes 1081352 | tf_op jit(solution)/shard_map/ppermute | solution.py:354
  109.2 5.9 %collective-permute-done.10.m1 = bf16[704,256]{1,0:T(8,128)(2,1)} collective-permute-done((bf16[704,256]{1,0:T(8,128)(2,1)S(1)}, bf16[704,256]{1,0:T(8,128)(2,1)}, u32[]{:S(2)}, u32[]{:S(2)}) %collective-permute-start.10) | collective-permute-done | bytes 360480 | tf_op jit(solution)/shard_map/ppermute | solution.py:354
  116.4 11.8 %collective-permute-done.17.c3 = bf16[704,256]{1,0:T(8,128)(2,1)S(1)} collective-permute-done((bf16[704,256]{1,0:T(8,128)(2,1)S(1)}, bf16[704,256]{1,0:T(8,128)(2,1)S(1)}, u32[]{:S(2)}, u32[]{:S(2)}) %collective-permute-start.17) | collective-permute-done | bytes 360480 | tf_op jit(solution)/shard_map/ppermute | solution.py:354
  130.3 5.7 %collective-permute-done.12.m3 = bf16[704,256]{1,0:T(8,128)(2,1)} collective-permute-done((bf16[704,256]{1,0:T(8,128)(2,1)}, bf16[704,256]{1,0:T(8,128)(2,1)}, u32[]{:S(2)}, u32[]{:S(2)}) %collective-permute-start.12) | collective-permute-done | bytes 360480 | tf_op jit(solution)/shard_map/ppermute | solution.py:354
  137.9 25.4 %shard_map.246 = (bf16[704,1024]{1,0:T(8,128)(2,1)}, bf16[704,1024]{1,0:T(8,128)(2,1)}, bf16[704,768]{1,0:T(8,128)(2,1)}, bf16[704,1536]{1,0:T(8,128)(2,1)}, bf1...) custom-call(s32[2]{0:T(128)S(1)} %pad_add_fusion.info_ref, ...), custom_call_target="tpu_custom_call" | custom-call | flops 5536481280 | bytes 16000000 | tf_op jit(solution)/shard_map/pallas_call | solution.py:334
  164.0 9.0 %collective-permute-start.25 = (bf16[704,256]{1,0:T(8,128)(2,1)S(1)}, bf16[704,256]{1,0:T(8,128)(2,1)S(1)}, u32[]{:S(2)}, u32[]{:S(2)}) collective-permute-start(bf16[704,256]{1,0:T(8,128)(2,1)S(1)} %get-tuple-element.55), channel_id=1, source_target_pairs={{0,2},{3,1},{4,6},{7,5},{8,10},{11,9},{12,14},{15,13},{16,18},{19,... | collective-permute-start | bytes 1081352 | tf_op jit(solution)/shard_map/ppermute | solution.py:354
  181.9 6.8 %collective-permute-start.27 = (bf16[704,256]{1,0:T(8,128)(2,1)S(1)}, bf16[704,256]{1,0:T(8,128)(2,1)S(1)}, u32[]{:S(2)}, u32[]{:S(2)}) collective-permute-start(bf16[704,256]{1,0:T(8,128)(2,1)S(1)} %add_convert_fusion.4), channel_id=1, source_target_pairs={{0,1},{1,0},{2,3},{3,2},{4,5},{5,4},{6,7},{7,6},{8,9},{9,8},{10,11... | collective-permute-start | bytes 1081352 | tf_op jit(solution)/shard_map/ppermute | solution.py:354
  190.1 4.1 %convolution_convert_fusion = bf16[1024,1536]{1,0:T(8,128)(2,1)} fusion(bf16[704,1024]{1,0:T(8,128)(2,1)S(1)} %copy-done.32, bf16[704,1536]{1,0:T(8,128)(2,1)S(1)} %copy-done.31), kind=kOutput, calls=%fused_computation | convolution fusion | flops 2216165376 | bytes 6750208 | tf_op jit(solution)/shard_map/dot_general | solution.py:31
  198.5 8.4 %collective-permute-start.30 = (bf16[704,256]{1,0:T(8,128)(2,1)S(1)}, bf16[704,256]{1,0:T(8,128)(2,1)}, u32[]{:S(2)}, u32[]{:S(2)}) collective-permute-start(bf16[704,256]{1,0:T(8,128)(2,1)S(1)} %fusion.17.g0), channel_id=1, source_target_pairs={{0,1},{1,0},{2,3},{3,2},{4,5},{5,4},{6,7},{7,6},{8,9},{9,8},{10,11... | collective-permute-start | bytes 1081352 | tf_op jit(solution)/shard_map/ppermute | solution.py:354
  222.3 5.3 %collective-permute-start.22 = (bf16[704,256]{1,0:T(8,128)(2,1)}, bf16[704,256]{1,0:T(8,128)(2,1)}, u32[]{:S(2)}, u32[]{:S(2)}) collective-permute-start(bf16[704,256]{1,0:T(8,128)(2,1)} %fusion.2), channel_id=1, source_target_pairs={{0,1},{1,0},{2,3},{3,2},{4,5},{5,4},{6,7},{7,6},{8,9},{9,8},{10,11... | collective-permute-start | bytes 1081352 | tf_op jit(solution)/shard_map/ppermute | solution.py:354
  231.0 5.2 %collective-permute-done.32.g3 = bf16[704,256]{1,0:T(8,128)(2,1)S(1)} collective-permute-done((bf16[704,256]{1,0:T(8,128)(2,1)S(1)}, bf16[704,256]{1,0:T(8,128)(2,1)S(1)}, u32[]{:S(2)}, u32[]{:S(2)}) %collective-permute-start.32) | collective-permute-done | bytes 360480 | tf_op jit(solution)/shard_map/ppermute | solution.py:354
  237.2 25.9 %shard_map.247 = (bf16[704,1024]{1,0:T(8,128)(2,1)}, bf16[704,1024]{1,0:T(8,128)(2,1)}, bf16[704,256]{1,0:T(8,128)(2,1)S(1)}, bf16[704,256]{1,0:T(8,128)(2,1)S(1...) custom-call(s32[2]{0:T(128)S(1)} %pad_add_fusion.info_ref, ...), custom_call_target="tpu_custom_call" | custom-call | flops 4752146432 | bytes 16000000 | tf_op jit(solution)/shard_map/pallas_call | solution.py:334
  263.7 6.5 %collective-permute-start.35 = (bf16[704,256]{1,0:T(8,128)(2,1)S(1)}, bf16[704,256]{1,0:T(8,128)(2,1)S(1)}, u32[]{:S(2)}, u32[]{:S(2)}) collective-permute-start(bf16[704,256]{1,0:T(8,128)(2,1)S(1)} %get-tuple-element.67), channel_id=1, source_target_pairs={{0,2},{3,1},{4,6},{7,5},{8,10},{11,9},{12,14},{15,13},{16,18},{19,... | collective-permute-start | bytes 1081352 | tf_op jit(solution)/shard_map/ppermute | solution.py:354
  271.6 4.5 %convolution_convert_fusion.1 = bf16[1024,1024]{1,0:T(8,128)(2,1)} fusion(bf16[704,1024]{1,0:T(8,128)(2,1)S(1)} %copy-done.30, bf16[704,1024]{1,0:T(8,128)(2,1)} %get-tuple-element.73), kind=kOutput, calls=%fused_computation.1 | convolution fusion | flops 1477443584 | bytes 4980736 | tf_op jit(solution)/shard_map/dot_general | solution.py:31
  286.7 9.9 %all-reduce.7.cloned.1.call-done = (bf16[768,1024]{1,0:T(8,128)(2,1)}, bf16[1024,1536]{1,0:T(8,128)(2,1)}) async-done(((bf16[768,1024]{1,0:T(8,128)(2,1)}, bf16[1024,1536]{1,0:T(8,128)(2,1)}), (bf16[768,1024]{1,0:T(8,128)(2,1)}, bf16[1024,1536]{1,0:T(8,128)(2,1)})) %all-reduce.7.cloned.1.call-update) | async-done | bytes 4718608 | tf_op jit(solution)/shard_map/psum | solution.py:436
  304.4 40.1 %psum.39 = f32[2308]{0:T(1024)S(1)} all-reduce(f32[2308]{0:T(1024)S(1)} %concatenate.11), channel_id=1, replica_groups=mesh['dp'=8,'tensor'=4] {'dp','tensor'}, use_global_device_ids=true, to_apply=%region_12.13 | all-reduce | flops 2308 | bytes 18464 | tf_op jit(solution)/shard_map/psum | solution.py:471
  354.1 17.4 %all-reduce.5.cloned.1.call-done = (bf16[1024,1024]{1,0:T(8,128)(2,1)}, bf16[512,1024]{1,0:T(8,128)(2,1)}) async-done(((bf16[1024,1024]{1,0:T(8,128)(2,1)}, bf16[512,1024]{1,0:T(8,128)(2,1)}), (bf16[1024,1024]{1,0:T(8,128)(2,1)}, bf16[512,1024]{1,0:T(8,128)(2,1)})) %all-reduce.5.cloned.1.call-update) | async-done | bytes 3145744 | tf_op jit(solution)/shard_map/psum | solution.py:457
  (173 shorter events, 100.0 us)
Async XLA Ops:
  7.2 289.4 %all-reduce.7.cloned.1.call-start = ((), (), s32[]{:S(2)}) async-start(), calls=%async_computation.1 | async-start | bytes 9437184 | tf_op jit(solution)/shard_map/psum | solution.py:436
  19.0 27.8 %collective-permute-start.4 = (bf16[704,256]{1,0:T(8,128)(2,1)S(1)}, bf16[704,256]{1,0:T(8,128)(2,1)S(1)}, u32[]{:S(2)}, u32[]{:S(2)}) collective-permute-start(bf16[704,256]{1,0:T(8,128)(2,1)S(1)} %collective-permute-done.x1), channel_id=1, source_target_pairs={{2,0},{1,3},{6,4},{5,7},{10,8},{9,11},{14,12},{13,15},{18,16},{17,... | collective-permute-start | bytes 1081352 | tf_op jit(solution)/shard_map/ppermute | solution.py:354
  20.3 26.5 %collective-permute-start.3 = (bf16[704,256]{1,0:T(8,128)(2,1)S(1)}, bf16[704,256]{1,0:T(8,128)(2,1)S(1)}, u32[]{:S(2)}, u32[]{:S(2)}) collective-permute-start(bf16[704,256]{1,0:T(8,128)(2,1)S(1)} %collective-permute-done.x1), channel_id=1, source_target_pairs={{1,2},{2,1},{5,6},{6,5},{9,10},{10,9},{13,14},{14,13},{17,18},{18,... | collective-permute-start | bytes 1081352 | tf_op jit(solution)/shard_map/ppermute | solution.py:354
  21.0 25.8 %collective-permute-start.2 = (bf16[704,256]{1,0:T(8,128)(2,1)S(1)}, bf16[704,256]{1,0:T(8,128)(2,1)S(1)}, u32[]{:S(2)}, u32[]{:S(2)}) collective-permute-start(bf16[704,256]{1,0:T(8,128)(2,1)S(1)} %collective-permute-done.1.x2), channel_id=1, source_target_pairs={{1,0},{2,3},{5,4},{6,7},{9,8},{10,11},{13,12},{14,15},{17,16},{18,... | collective-permute-start | bytes 1081352 | tf_op jit(solution)/shard_map/ppermute | solution.py:354
  86.6 17.8 %collective-permute-start.15 = (bf16[704,256]{1,0:T(8,128)(2,1)S(1)}, bf16[704,256]{1,0:T(8,128)(2,1)S(1)}, u32[]{:S(2)}, u32[]{:S(2)}) collective-permute-start(bf16[704,256]{1,0:T(8,128)(2,1)S(1)} %copy-done.1), channel_id=1, source_target_pairs={{0,1},{1,0},{2,3},{3,2},{4,5},{5,4},{6,7},{7,6},{8,9},{9,8},{10,11... | collective-permute-start | bytes 1081352 | tf_op jit(solution)/shard_map/ppermute | solution.py:354
  95.3 19.8 %collective-permute-start.10 = (bf16[704,256]{1,0:T(8,128)(2,1)S(1)}, bf16[704,256]{1,0:T(8,128)(2,1)}, u32[]{:S(2)}, u32[]{:S(2)}) collective-permute-start(bf16[704,256]{1,0:T(8,128)(2,1)S(1)} %fusion.9.m0), channel_id=1, source_target_pairs={{0,1},{1,0},{2,3},{3,2},{4,5},{5,4},{6,7},{7,6},{8,9},{9,8},{10,11... | collective-permute-start | bytes 1081352 | tf_op jit(solution)/shard_map/ppermute | solution.py:354
  103.1 25.0 %collective-permute-start.17 = (bf16[704,256]{1,0:T(8,128)(2,1)S(1)}, bf16[704,256]{1,0:T(8,128)(2,1)S(1)}, u32[]{:S(2)}, u32[]{:S(2)}) collective-permute-start(bf16[704,256]{1,0:T(8,128)(2,1)S(1)} %collective-permute-done.16.c2), channel_id=1, source_target_pairs={{1,0},{2,3},{5,4},{6,7},{9,8},{10,11},{13,12},{14,15},{17,16},{18,... | collective-permute-start | bytes 1081352 | tf_op jit(solution)/shard_map/ppermute | solution.py:354
  104.4 25.8 %collective-permute-start.19 = (bf16[704,256]{1,0:T(8,128)(2,1)S(1)}, bf16[704,256]{1,0:T(8,128)(2,1)}, u32[]{:S(2)}, u32[]{:S(2)}) collective-permute-start(bf16[704,256]{1,0:T(8,128)(2,1)S(1)} %collective-permute-done.15.c1), channel_id=1, source_target_pairs={{2,0},{1,3},{6,4},{5,7},{10,8},{9,11},{14,12},{13,15},{18,16},{17,... | collective-permute-start | bytes 1081352 | tf_op jit(solution)/shard_map/ppermute | solution.py:354
  105.7 24.5 %collective-permute-start.18 = (bf16[704,256]{1,0:T(8,128)(2,1)S(1)}, bf16[704,256]{1,0:T(8,128)(2,1)}, u32[]{:S(2)}, u32[]{:S(2)}) collective-permute-start(bf16[704,256]{1,0:T(8,128)(2,1)S(1)} %collective-permute-done.15.c1), channel_id=1, source_target_pairs={{1,2},{2,1},{5,6},{6,5},{9,10},{10,9},{13,14},{14,13},{17,18},{18,... | collective-permute-start | bytes 1081352 | tf_op jit(solution)/shard_map/ppermute | solution.py:354
  107.9 28.1 %collective-permute-start.12 = (bf16[704,256]{1,0:T(8,128)(2,1)}, bf16[704,256]{1,0:T(8,128)(2,1)}, u32[]{:S(2)}, u32[]{:S(2)}) collective-permute-start(bf16[704,256]{1,0:T(8,128)(2,1)} %collective-permute-done.11.m2), channel_id=1, source_target_pairs={{1,0},{2,3},{5,4},{6,7},{9,8},{10,11},{13,12},{14,15},{17,16},{18,... | collective-permute-start | bytes 1081352 | tf_op jit(solution)/shard_map/ppermute | solution.py:354
  115.1 20.9 %collective-permute-start.14 = (bf16[704,256]{1,0:T(8,128)(2,1)}, bf16[704,256]{1,0:T(8,128)(2,1)}, u32[]{:S(2)}, u32[]{:S(2)}) collective-permute-start(bf16[704,256]{1,0:T(8,128)(2,1)} %collective-permute-done.10.m1), channel_id=1, source_target_pairs={{2,0},{1,3},{6,4},{5,7},{10,8},{9,11},{14,12},{13,15},{18,16},{17,... | collective-permute-start | bytes 1081352 | tf_op jit(solution)/shard_map/ppermute | solution.py:354
  163.4 18.2 %collective-permute-start.26 = (bf16[704,256]{1,0:T(8,128)(2,1)S(1)}, bf16[704,256]{1,0:T(8,128)(2,1)S(1)}, u32[]{:S(2)}, u32[]{:S(2)}) collective-permute-start(bf16[704,256]{1,0:T(8,128)(2,1)S(1)} %get-tuple-element.55), channel_id=1, source_target_pairs={{1,2},{2,1},{5,6},{6,5},{9,10},{10,9},{13,14},{14,13},{17,18},{18,... | collective-permute-start | bytes 1081352 | tf_op jit(solution)/shard_map/ppermute | solution.py:354
  164.0 17.8 %collective-permute-start.25 = (bf16[704,256]{1,0:T(8,128)(2,1)S(1)}, bf16[704,256]{1,0:T(8,128)(2,1)S(1)}, u32[]{:S(2)}, u32[]{:S(2)}) collective-permute-start(bf16[704,256]{1,0:T(8,128)(2,1)S(1)} %get-tuple-element.55), channel_id=1, source_target_pairs={{0,2},{3,1},{4,6},{7,5},{8,10},{11,9},{12,14},{15,13},{16,18},{19,... | collective-permute-start | bytes 1081352 | tf_op jit(solution)/shard_map/ppermute | solution.py:354
  177.0 40.4 %collective-permute-start.21 = (bf16[704,256]{1,0:T(8,128)(2,1)}, bf16[704,256]{1,0:T(8,128)(2,1)}, u32[]{:S(2)}, u32[]{:S(2)}) collective-permute-start(bf16[704,256]{1,0:T(8,128)(2,1)} %convolution_convert_fusion.5), channel_id=1, source_target_pairs={{1,2},{2,1},{5,6},{6,5},{9,10},{10,9},{13,14},{14,13},{17,18},{18,... | collective-permute-start | bytes 1081352 | tf_op jit(solution)/shard_map/ppermute | solution.py:354
  178.5 40.9 %collective-permute-start.20 = (bf16[704,256]{1,0:T(8,128)(2,1)}, bf16[704,256]{1,0:T(8,128)(2,1)}, u32[]{:S(2)}, u32[]{:S(2)}) collective-permute-start(bf16[704,256]{1,0:T(8,128)(2,1)} %convolution_convert_fusion.5), channel_id=1, source_target_pairs={{0,2},{3,1},{4,6},{7,5},{8,10},{11,9},{12,14},{15,13},{16,18},{19,... | collective-permute-start | bytes 1081352 | tf_op jit(solution)/shard_map/ppermute | solution.py:354
  197.8 20.3 %collective-permute-start.31 = (bf16[704,256]{1,0:T(8,128)(2,1)S(1)}, bf16[704,256]{1,0:T(8,128)(2,1)S(1)}, u32[]{:S(2)}, u32[]{:S(2)}) collective-permute-start(bf16[704,256]{1,0:T(8,128)(2,1)S(1)} %fusion.17.g0), channel_id=1, source_target_pairs={{1,2},{2,1},{5,6},{6,5},{9,10},{10,9},{13,14},{14,13},{17,18},{18,... | collective-permute-start | bytes 1081352 | tf_op jit(solution)/shard_map/ppermute | solution.py:354
  198.5 17.5 %collective-permute-start.30 = (bf16[704,256]{1,0:T(8,128)(2,1)S(1)}, bf16[704,256]{1,0:T(8,128)(2,1)}, u32[]{:S(2)}, u32[]{:S(2)}) collective-permute-start(bf16[704,256]{1,0:T(8,128)(2,1)S(1)} %fusion.17.g0), channel_id=1, source_target_pairs={{0,1},{1,0},{2,3},{3,2},{4,5},{5,4},{6,7},{7,6},{8,9},{9,8},{10,11... | collective-permute-start | bytes 1081352 | tf_op jit(solution)/shard_map/ppermute | solution.py:354
  209.4 162.1 %all-reduce.5.cloned.1.call-start = ((), (), s32[]{:S(2)}) async-start(), calls=%async_computation | async-start | bytes 6291456 | tf_op jit(solution)/shard_map/psum | solution.py:457
  216.0 20.2 %collective-permute-start.34 = (bf16[704,256]{1,0:T(8,128)(2,1)}, bf16[704,256]{1,0:T(8,128)(2,1)S(1)}, u32[]{:S(2)}, u32[]{:S(2)}) collective-permute-start(bf16[704,256]{1,0:T(8,128)(2,1)} %collective-permute-done.30.g1), channel_id=1, source_target_pairs={{2,0},{1,3},{6,4},{5,7},{10,8},{9,11},{14,12},{13,15},{18,16},{17,... | collective-permute-start | bytes 1081352 | tf_op jit(solution)/shard_map/ppermute | solution.py:354
  217.4 18.8 %collective-permute-start.33 = (bf16[704,256]{1,0:T(8,128)(2,1)}, bf16[704,256]{1,0:T(8,128)(2,1)S(1)}, u32[]{:S(2)}, u32[]{:S(2)}) collective-permute-start(bf16[704,256]{1,0:T(8,128)(2,1)} %collective-permute-done.30.g1), channel_id=1, source_target_pairs={{1,2},{2,1},{5,6},{6,5},{9,10},{10,9},{13,14},{14,13},{17,18},{18,... | collective-permute-start | bytes 1081352 | tf_op jit(solution)/shard_map/ppermute | solution.py:354
  218.1 18.0 %collective-permute-start.32 = (bf16[704,256]{1,0:T(8,128)(2,1)S(1)}, bf16[704,256]{1,0:T(8,128)(2,1)S(1)}, u32[]{:S(2)}, u32[]{:S(2)}) collective-permute-start(bf16[704,256]{1,0:T(8,128)(2,1)S(1)} %collective-permute-done.31.g2), channel_id=1, source_target_pairs={{1,0},{2,3},{5,4},{6,7},{9,8},{10,11},{13,12},{14,15},{17,16},{18,... | collective-permute-start | bytes 1081352 | tf_op jit(solution)/shard_map/ppermute | solution.py:354
  222.3 74.4 %collective-permute-start.22 = (bf16[704,256]{1,0:T(8,128)(2,1)}, bf16[704,256]{1,0:T(8,128)(2,1)}, u32[]{:S(2)}, u32[]{:S(2)}) collective-permute-start(bf16[704,256]{1,0:T(8,128)(2,1)} %fusion.2), channel_id=1, source_target_pairs={{0,1},{1,0},{2,3},{3,2},{4,5},{5,4},{6,7},{7,6},{8,9},{9,8},{10,11... | collective-permute-start | bytes 1081352 | tf_op jit(solution)/shard_map/ppermute | solution.py:354
  229.6 67.1 %collective-permute-start.24 = (bf16[704,256]{1,0:T(8,128)(2,1)}, bf16[704,256]{1,0:T(8,128)(2,1)}, u32[]{:S(2)}, u32[]{:S(2)}) collective-permute-start(bf16[704,256]{1,0:T(8,128)(2,1)} %add_convert_fusion.5), channel_id=1, source_target_pairs={{1,2},{2,1},{5,6},{6,5},{9,10},{10,9},{13,14},{14,13},{17,18},{18,... | collective-permute-start | bytes 1081352 | tf_op jit(solution)/shard_map/ppermute | solution.py:354
  279.6 19.2 %collective-permute-start.37 = (bf16[704,256]{1,0:T(8,128)(2,1)}, bf16[704,256]{1,0:T(8,128)(2,1)}, u32[]{:S(2)}, u32[]{:S(2)}) collective-permute-start(bf16[704,256]{1,0:T(8,128)(2,1)} %add_convert_fusion.2), channel_id=1, source_target_pairs={{0,1},{1,0},{2,3},{3,2},{4,5},{5,4},{6,7},{7,6},{8,9},{9,8},{10,11... | collective-permute-start | bytes 1081352 | tf_op jit(solution)/shard_map/ppermute | solution.py:354
  (51 other events, 784.7 us)
Sparse Core Ops, SparseCore 0:
  209.6 87.0 all-reduce.6
  300.9 70.5 all-reduce.4

commit v2 on v1

v2 whole, which is shorter than its diff:
```python
import functools

import jax
import jax.numpy as jnp
from jax import lax
from jax.experimental import pallas as pl
from jax.experimental.pallas import tpu as pltpu
from jax.sharding import PartitionSpec as P

BLOCK = 256
NORM_EPSILON = 1e-06
ROPE_THETA = 1000000.0
LOG2E = 1.4426950408889634
NEG = -1e30
ROWS = 64
TAIL = 16
VMEM_BYTES = 60 * 1024 * 1024
SMALL_BYTES = 24 * 1024 * 1024

bf16 = jnp.bfloat16
f32 = jnp.float32


def dot(a, b):
    return jnp.dot(a, b, preferred_element_type=f32)


def dot_t(a, b):
    return lax.dot_general(a, b, (((1,), (1,)), ((), ())), preferred_element_type=f32)


def t_dot(a, b):
    return lax.dot_general(a, b, (((0,), (0,)), ((), ())), preferred_element_type=f32)


def row_loop(count, step, body):
    for start in range(0, count, step):
        body(pl.ds(start, step))


def rope_tables(length, width):
    half_width = width // 2
    frequency = ROPE_THETA ** (-(jnp.arange(half_width, dtype=f32) * (2.0 / width)))
    angles = jnp.arange(length, dtype=f32)[:, None] * frequency[None, :]
    cos, sin = jnp.cos(angles), jnp.sin(angles)
    return jnp.concatenate([cos, cos], axis=1), jnp.concatenate([-sin, sin], axis=1)


def query_units(seq_len):
    units = []
    start = 0
    while start < seq_len:
        rows = min(128, seq_len - start)
        keys = (start // BLOCK + 1) * BLOCK
        units.append((start, rows, keys))
        start += rows
    return units


def roles(z):
    low = z < 2
    return jnp.where(low, 2, 1), jnp.where(low, 3, 0), z + 1 - 2 * lax.rem(z, 2), z


def shard_slices(z, width):
    return [pl.ds(pl.multiple_of(shard * width, width), width) for shard in roles(z)]


def assemble(z, pieces, body):
    own, pair_mid, pair_end, across_mid, across_end, far_mid, far_end = pieces
    end = (z == 0) | (z == 3)

    @pl.when(end)
    def _():
        body((across_end, far_end, pair_end, own))

    @pl.when(jnp.logical_not(end))
    def _():
        body((across_mid, far_mid, pair_mid, own))


def key_bias(length, keys):
    slot = lax.broadcasted_iota(jnp.int32, (1, keys), 1)
    return jnp.where(slot < length, 0.0, NEG).astype(f32)


def row_scale(squares, width):
    return lax.rsqrt(jnp.sum(squares, axis=1, keepdims=True) * (1.0 / width) + NORM_EPSILON)


def copies(sources, targets, sems):
    pending = [pltpu.make_async_copy(a, b, sems.at[i]) for i, (a, b) in enumerate(zip(sources, targets))]
    for copy in pending:
        copy.start()
    return pending


def attn_forward_kernel(
    info_ref, x0, x1, x2, x3, x4, x5, qg_ref, kg_ref, wk_hbm, cos_hbm, sin_hbm, wv_hbm, wq_hbm, wo_hbm,
    p_across, p_far, p_pair, p_own, n1_hbm, qpre_hbm, kpre_hbm, qrot_hbm, krot_hbm, val_hbm, mixed_hbm, lse_hbm,
    r1_hbm, gain_hbm,
    wk_ref, cos_ref, sin_ref, wv_ref, wq_ref, wo_ref, n1_ref, qpre_ref, kpre_ref, qrot_ref, krot_ref, val_ref,
    mixed_ref, lse_ref, r1_ref, gain_ref, in_sems, out_sems,
):
    seq_len, width = n1_ref.shape
    hd = qg_ref.shape[1]
    heads = wq_ref.shape[1] // hd
    kvs = wk_ref.shape[1] // hd
    group = heads // kvs
    padded = krot_ref.shape[0]
    length, z = info_ref[0], info_ref[1]
    scale = hd ** (-0.5) * LOG2E
    slices = shard_slices(z, width // 4)
    pending = copies(
        (wk_hbm, cos_hbm, sin_hbm, wv_hbm, wq_hbm, wo_hbm), (wk_ref, cos_ref, sin_ref, wv_ref, wq_ref, wo_ref), in_sems
    )
    sent = []

    def put(source, target):
        copy = pltpu.make_async_copy(source, target, out_sems.at[len(sent)])
        copy.start()
        sent.append(copy)

    def normalise(refs):
        for ref, cols in zip(refs, slices):
            tail = ref[seq_len : seq_len + TAIL, :].astype(f32)
            gain_ref[:, cols] = tail[0:8] + tail[8:16]

        def norm(rows):
            xs = [ref[rows, :].astype(f32) for ref in refs]
            r1 = row_scale(sum(x * x for x in xs), width)
            r1_ref[rows, :] = jnp.broadcast_to(r1, (ROWS, 128))
            for x, cols in zip(xs, slices):
                n1_ref[rows, cols] = (x * r1 * gain_ref[0:1, cols]).astype(bf16)

        row_loop(seq_len, ROWS, norm)

    assemble(z, (x0, x1, x1, x2, x3, x4, x5), normalise)
    put(n1_ref, n1_hbm)
    put(r1_ref, r1_hbm)
    put(gain_ref, gain_hbm)

    def project(w_ref, pre_ref, rot_ref, g_ref):
        count = w_ref.shape[1]
        for c in range(0, count, 2 * hd):
            pre_ref[:, c : c + 2 * hd] = dot(n1_ref[...], w_ref[:, c : c + 2 * hd])

        def rotate(rows):
            cos, sin = cos_ref[rows, :], sin_ref[rows, :]
            for c in range(0, count, hd):
                v = pre_ref[rows, c : c + hd]
                v = v * row_scale(v * v, hd) * g_ref[...]
                rot_ref[rows, c : c + hd] = (v * cos + pltpu.roll(v, hd // 2, 1) * sin).astype(bf16)

        row_loop(seq_len, ROWS, rotate)

    for copy in pending:
        copy.wait()
    project(wk_ref, kpre_ref, krot_ref, kg_ref)
    val_ref[0:seq_len, :] = dot(n1_ref[...], wv_ref[...]).astype(bf16)
    if padded > seq_len:
        krot_ref[seq_len:padded, :] = jnp.zeros((padded - seq_len, kvs * hd), bf16)
        val_ref[seq_len:padded, :] = jnp.zeros((padded - seq_len, kvs * hd), bf16)
    put(kpre_ref, kpre_hbm)
    put(krot_ref, krot_hbm)
    put(val_ref, val_hbm)
    project(wq_ref, qpre_ref, qrot_ref, qg_ref)
    put(qpre_ref, qpre_hbm)
    put(qrot_ref, qrot_hbm)

    for start, rows, keys in query_units(seq_len):
        bias = key_bias(length, keys)
        for g in range(kvs):
            key = krot_ref[0:keys, g * hd : (g + 1) * hd]
            val = val_ref[0:keys, g * hd : (g + 1) * hd]
            first = g * group
            q = jnp.concatenate(
                [qrot_ref[start : start + rows, h * hd : (h + 1) * hd] for h in range(first, first + group)], axis=0
            )
            e = jnp.exp2(dot_t(q, key) * scale + bias)
            total = jnp.sum(e, axis=1, keepdims=True)
            mixed = dot(e.astype(bf16), val) * (1.0 / total)
            lse = jnp.log2(total)
            for r in range(group):
                h = first + r
                mixed_ref[start : start + rows, h * hd : (h + 1) * hd] = mixed[r * rows : (r + 1) * rows].astype(bf16)
                lse_ref[start : start + rows, h : h + 1] = lse[r * rows : (r + 1) * rows]

    put(mixed_ref, mixed_hbm)
    put(lse_ref, lse_hbm)
    for part_ref, cols in zip((p_across, p_far, p_pair, p_own), slices):
        part_ref[...] = dot(mixed_ref[...], wo_ref[:, cols]).astype(part_ref.dtype)
    for copy in sent:
        copy.wait()


def wide(column, width):
    return jnp.concatenate([column] * (width // column.shape[1]), axis=1)


def norm_back(grad_s, normed_ref, scale_ref, inner_s, gain, part_ref, cols, width, gain_grad_ref=None):
    seq_len, step = grad_s.shape
    inverse = 1.0 / gain
    total = jnp.zeros((8, step), f32)
    for start in range(0, seq_len, ROWS):
        rows = pl.ds(start, ROWS)
        grad = grad_s[rows, :]
        unit = normed_ref[rows, cols].astype(f32) * inverse
        coef = wide(inner_s[rows, :] * (1.0 / width), step)
        part_ref[rows, :] = (wide(scale_ref[rows, :], step) * (grad * gain - unit * coef)).astype(part_ref.dtype)
        if gain_grad_ref is not None:
            total = total + jnp.sum((grad * unit).reshape(ROWS // 8, 8, step), axis=0)
    if gain_grad_ref is not None:
        gain_grad_ref[:, cols] = total


def ffn_kernel(
    info_ref, m0, m1, m2, m3, m4, m5, gain_hbm, wg_hbm, wu_hbm, wd_hbm, c0, c1, c2, c3, c4, c5, c6,
    p_across, p_far, p_pair, p_own, gfg_ref, n2_hbm, cotm_hbm, hid_hbm, dgu_hbm,
    gain_ref, wg_ref, wu_ref, wd_ref, cot_s, n2_ref, cotm_ref, hid_ref, dgu_ref,
    gate_s, up_s, gh_s, inner_s, r2_s, in_sems, out_sems,
):
    seq_len, width = n2_ref.shape
    hidden = wg_ref.shape[1]
    length, z = info_ref[0], info_ref[1]
    step = gate_s.shape[1]
    shard = width // 4
    slices = shard_slices(z, shard)
    got_gain, got_wg, got_wu, got_wd = copies(
        (gain_hbm, wg_hbm, wu_hbm, wd_hbm), (gain_ref, wg_ref, wu_ref, wd_ref), in_sems
    )

    def fetch(refs):
        return [
            pltpu.make_async_copy(
                ref.at[pl.ds(0, seq_len), :], cot_s.at[:, pl.ds(k * shard, shard)], in_sems.at[4 + k]
            )
            for k, ref in enumerate(refs)
        ]

    def start_cot(refs):
        for copy in fetch(refs):
            copy.start()

    assemble(z, (c0, c1, c2, c3, c4, c5, c6), start_cot)
    got_gain.wait()

    def normalise(refs):
        def norm(rows):
            ms = [ref[rows, :].astype(f32) for ref in refs]
            r2 = row_scale(sum(m * m for m in ms), width)
            r2_s[rows, :] = jnp.broadcast_to(r2, (ROWS, 128))
            inner_s[rows, :] = jnp.zeros((ROWS, 128), f32)
            for m, cols in zip(ms, slices):
                n2_ref[rows, cols] = (m * r2 * gain_ref[1:2, cols]).astype(bf16)

        row_loop(seq_len, ROWS, norm)

    assemble(z, (m0, m1, m1, m2, m3, m4, m5), normalise)
    for copy in fetch((c0, c1, c2, c3)) + [got_wg, got_wu, got_wd]:
        copy.wait()

    def mask(rows):
        slot = rows.start + lax.broadcasted_iota(jnp.int32, (ROWS, 1), 0)
        for k, cols in enumerate(slices):
            cot = cot_s[rows, k * shard : (k + 1) * shard].astype(f32)
            cotm_ref[rows, cols] = jnp.where(slot < length, cot, 0.0).astype(bf16)

    row_loop(seq_len, ROWS, mask)

    for j in range(0, hidden, step):
        gate_s[...] = dot(n2_ref[...], wg_ref[:, j : j + step])
        up_s[...] = dot(n2_ref[...], wu_ref[:, j : j + step])
        gh_s[...] = dot_t(cotm_ref[...], wd_ref[j : j + step, :])

        def elementwise(rows):
            gate, up, gh = gate_s[rows, :], up_s[rows, :], gh_s[rows, :]
            sig = jax.nn.sigmoid(gate)
            silu = gate * sig
            hid_ref[rows, j : j + step] = (silu * up).astype(bf16)
            dg = (gh * up * (sig * (1.0 + gate * (1.0 - sig)))).astype(bf16)
            du = (gh * silu).astype(bf16)
            dgu_ref[rows, j : j + step] = dg
            dgu_ref[rows, hidden + j : hidden + j + step] = du
            inner = jnp.sum(dg.astype(f32) * gate + du.astype(f32) * up, axis=1, keepdims=True)
            inner_s[rows, :] += jnp.broadcast_to(inner, (ROWS, 128))

        row_loop(seq_len, ROWS, elementwise)

    sent = copies(
        (n2_ref, cotm_ref, hid_ref, dgu_ref), (n2_hbm, cotm_hbm, hid_hbm, dgu_hbm), out_sems
    )
    for part_ref, cols in zip((p_across, p_far, p_pair, p_own), slices):
        gate_s[...] = dot_t(dgu_ref[:, 0:hidden], wg_ref[cols, :]) + dot_t(
            dgu_ref[:, hidden : 2 * hidden], wu_ref[cols, :]
        )
        norm_back(gate_s, n2_ref, r2_s, inner_s, gain_ref[1:2, cols], part_ref, cols, width, gfg_ref)
    for copy in sent:
        copy.wait()


def share(grads_s, core, keep_hbm, give_hbm, sems):
    return copies(
        (grads_s.at[pl.ds(core * 4, 4)], grads_s.at[pl.ds((1 - core) * 4, 4)]), (keep_hbm, give_hbm), sems
    )


def ffn_grad_kernel(
    info_ref, n2_hbm, dgu_hbm, hid_hbm, cotm_hbm, wd_hbm,
    p_across, p_far, p_pair, p_own, keep_hbm, give_hbm,
    n2_ref, dgu_ref, hid_ref, cotm_ref, wd_ref, grads_ref, in_sems, out_sems,
):
    pending = copies(
        (n2_hbm, dgu_hbm, hid_hbm, cotm_hbm, wd_hbm), (n2_ref, dgu_ref, hid_ref, cotm_ref, wd_ref), in_sems
    )
    width, hidden = n2_ref.shape[1], hid_ref.shape[1]
    upper, lower = width // 8, hidden // 8
    rest = upper - lower
    pending[0].wait()
    pending[1].wait()
    for c in range(0, 2 * hidden, 256):
        grad = t_dot(n2_ref[...], dgu_ref[:, c : c + 256])
        for d in range(8):
            grads_ref[d, :, c : c + 256] = grad[d * upper : (d + 1) * upper].astype(bf16)
    for copy in pending[2:]:
        copy.wait()
    for c in range(0, width, 256):
        grad = t_dot(hid_ref[...], cotm_ref[:, c : c + 256])
        for d in range(8):
            block = grad[d * lower : (d + 1) * lower].astype(bf16)
            if c < hidden:
                grads_ref[d, 0:lower, 2 * hidden + c : 2 * hidden + c + 256] = block
            else:
                for k in range(lower // rest):
                    col = 2 * hidden + k * 256
                    grads_ref[d, lower:upper, col : col + 256] = block[k * rest : (k + 1) * rest]
    sent = share(grads_ref, info_ref[3], keep_hbm, give_hbm, out_sems)
    for part_ref, cols in zip((p_across, p_far, p_pair, p_own), shard_slices(info_ref[1], p_own.shape[1])):
        part_ref[...] = dot(hid_ref[...], wd_ref[:, cols]).astype(bf16)
    for copy in sent:
        copy.wait()


def chip_blocks_kernel(info_ref, keep_hbm, other_ref, b0, b1, b2, b3, keep_ref, sems):
    (got,) = copies((keep_hbm,), (keep_ref,), sems)
    got.wait()
    for k, out_ref in enumerate((b0, b1, b2, b3)):
        block = jnp.bitwise_xor(info_ref[2], k)
        out_ref[...] = (keep_ref[block].astype(f32) + other_ref[block].astype(f32)).astype(bf16)


def halves_kernel(info_ref, keep_hbm, other_hbm, to_x, to_y, keep_x, keep_y, keep_ref, other_ref, sems):
    for copy in copies((keep_hbm, other_hbm), (keep_ref, other_ref), sems):
        copy.wait()
    cols = to_x.shape[2]
    for out_ref, first, flips in ((to_x, 0, (1, 3)), (keep_x, 0, (0, 2)), (to_y, cols, (2, 3)), (keep_y, cols, (0, 1))):
        for i, flip in enumerate(flips):
            block = jnp.bitwise_xor(info_ref[2], flip)
            out_ref[i] = (
                keep_ref[block, :, first : first + cols].astype(f32) + other_ref[block, :, first : first + cols].astype(f32)
            ).astype(bf16)


def halve_kernel(info_ref, keep_x, keep_y, got_x, got_y, to_y, to_x, own_x, own_y):
    own_x[...] = (keep_x[0].astype(f32) + got_x[0].astype(f32)).astype(bf16)
    own_y[...] = (keep_y[0].astype(f32) + got_y[0].astype(f32)).astype(bf16)
    to_y[...] = (keep_x[1].astype(f32) + got_x[1].astype(f32)).astype(bf16)
    to_x[...] = (keep_y[1].astype(f32) + got_y[1].astype(f32)).astype(bf16)


def join_kernel(info_ref, own_x, own_y, from_y, from_x, left_ref, right_ref):
    left_ref[...] = (own_x[...].astype(f32) + from_y[...].astype(f32)).astype(bf16)
    right_ref[...] = (own_y[...].astype(f32) + from_x[...].astype(f32)).astype(bf16)


def unpack_ffn_kernel(info_ref, *refs):
    q, core = info_ref[2], info_ref[3]
    gate_ref, up_ref, down_ref = refs[8:]
    width, hidden = gate_ref.shape
    upper, lower = width // 8, hidden // 8
    rest = upper - lower
    cols = 3 * hidden // 2
    first = 2 * hidden - cols
    for half, (lefts, lefts_x, rights, rights_y) in ((core, refs[0:4]), (1 - core, refs[4:8])):
        for k in range(4):
            block = half * 4 + jnp.bitwise_xor(q, k)
            left, i = (lefts if k in (0, 2) else lefts_x), (0 if k in (0, 1) else 1)
            right, j = (rights if k in (0, 1) else rights_y), (0 if k in (0, 2) else 1)
            rows = pl.ds(pl.multiple_of(block * upper, upper), upper)
            gate_ref[rows, :] = left[i, :, 0:hidden].astype(f32)
            up_ref[rows, 0 : cols - hidden] = left[i, :, hidden:cols].astype(f32)
            up_ref[rows, cols - hidden : hidden] = right[j, :, 0:first].astype(f32)
            rows = pl.ds(pl.multiple_of(block * lower, lower), lower)
            down_ref[rows, 0:hidden] = right[j, 0:lower, first : first + hidden].astype(f32)
            for n in range(lower // rest):
                rows = pl.ds(pl.multiple_of(block * lower + n * rest, rest), rest)
                col = first + n * 256
                down_ref[rows, hidden:width] = right[j, lower:upper, col : col + 256].astype(f32)


def attn_backward_kernel(
    info_ref, g0, g1, g2, g3, g4, g5, qg_ref, kg_ref, wo_hbm, qrot_hbm, krot_hbm, val_hbm, mixed_hbm, lse_hbm,
    cos_hbm, sin_hbm, qpre_hbm, kpre_hbm, n1_hbm, wq_hbm, wk_hbm, wv_hbm, r1_hbm, gain_hbm,
    p_across, p_far, p_pair, p_own, gag_ref, qgg_ref, kgg_ref, keep_hbm, give_hbm,
    wo_ref, qrot_ref, krot_ref, val_ref, mixed_ref, lse_ref, cos_ref, sin_ref, qpre_ref, kpre_ref, n1_ref,
    wq_ref, wk_ref, wv_ref, r1_ref, gain_ref,
    ga_ref, gm_s, dq_s, dk_s, dv_s, dqkv_ref, inner_ref, acc_s, grads_ref, sems, out_sems,
):
    seq_len, width = ga_ref.shape
    hd = qg_ref.shape[1]
    qw, kw = qpre_ref.shape[1], kpre_ref.shape[1]
    heads, kvs = qw // hd, kw // hd
    group = heads // kvs
    length, z = info_ref[0], info_ref[1]
    scale = hd ** (-0.5)
    slices = shard_slices(z, width // 4)
    pending = copies(
        (
            wo_hbm, qrot_hbm, krot_hbm, val_hbm, mixed_hbm, lse_hbm, cos_hbm, sin_hbm, qpre_hbm, kpre_hbm, n1_hbm,
            wq_hbm, wk_hbm, wv_hbm, r1_hbm, gain_hbm,
        ),
        (
            wo_ref, qrot_ref, krot_ref, val_ref, mixed_ref, lse_ref, cos_ref, sin_ref, qpre_ref, kpre_ref, n1_ref,
            wq_ref, wk_ref, wv_ref, r1_ref, gain_ref,
        ),
        sems,
    )

    def collect(refs):
        for ref, cols in zip(refs, slices):
            ga_ref[:, cols] = ref[...]

    assemble(z, (g0, g1, g1, g2, g3, g4, g5), collect)

    pending[0].wait()
    for c in range(0, qw, 256):
        gm_s[:, c : c + 256] = dot_t(ga_ref[...], wo_ref[c : c + 256, :]).astype(bf16)
    dk_s[...] = jnp.zeros_like(dk_s)
    dv_s[...] = jnp.zeros_like(dv_s)
    for copy in pending[1:6]:
        copy.wait()

    for start, rows, keys in query_units(seq_len):
        bias = key_bias(length, keys)
        for g in range(kvs):
            first = g * group
            cols = slice(g * hd, (g + 1) * hd)
            key, val = krot_ref[0:keys, cols], val_ref[0:keys, cols]

            def stacked(ref):
                return jnp.concatenate(
                    [ref[start : start + rows, h * hd : (h + 1) * hd] for h in range(first, first + group)], axis=0
                )

            q, gm, mixed = stacked(qrot_ref), stacked(gm_s), stacked(mixed_ref)
            lse = jnp.concatenate(
                [lse_ref[start : start + rows, h : h + 1] for h in range(first, first + group)], axis=0
            )
            p = jnp.exp2(dot_t(q, key) * (scale * LOG2E) + bias - lse)
            delta = jnp.sum(gm.astype(f32) * mixed.astype(f32), axis=1, keepdims=True)
            ds = (p * (dot_t(gm, val) - delta)).astype(bf16)
            dv_s[0:keys, cols] += t_dot(p.astype(bf16), gm)
            dk_s[0:keys, cols] += t_dot(ds, q)
            dq = dot(ds, key)
            for r in range(group):
                h = first + r
                dq_s[start : start + rows, h * hd : (h + 1) * hd] = dq[r * rows : (r + 1) * rows]

    for copy in pending[6:]:
        copy.wait()
    ones = jnp.full((hd, hd), 1.0 / hd, bf16)

    def unrotate(rows, rot_s, pre_ref, g_ref, count, base, gain_sum):
        cos, sin = cos_ref[rows, :], sin_ref[rows, :]
        inner = jnp.zeros((ROWS, hd), f32)
        for c in range(0, count, hd):
            g = rot_s[rows, c : c + hd] * scale
            u = g * cos + pltpu.roll(g * sin, hd // 2, 1)
            v = pre_ref[rows, c : c + hd]
            r = lax.rsqrt(dot((v * v).astype(bf16), ones) + NORM_EPSILON)
            unit = v * r
            t = u * unit
            gain_sum = gain_sum + jnp.sum(t.reshape(ROWS // 8, 8, hd), axis=0)
            mean = dot((t * g_ref[...]).astype(bf16), ones)
            dqkv_ref[rows, base + c : base + c + hd] = (r * (u * g_ref[...] - unit * mean)).astype(bf16)
            inner = inner + (hd * NORM_EPSILON) * (r * r * mean)
        return inner, gain_sum

    qgs = kgs = jnp.zeros((8, hd), f32)
    for start in range(0, seq_len, ROWS):
        rows = pl.ds(start, ROWS)
        qi, qgs = unrotate(rows, dq_s, qpre_ref, qg_ref, qw, 0, qgs)
        ki, kgs = unrotate(rows, dk_s, kpre_ref, kg_ref, kw, qw, kgs)
        dv = dv_s[rows, :].astype(bf16)
        dqkv_ref[rows, qw + kw : qw + 2 * kw] = dv
        vi = jnp.sum(dv.astype(f32) * val_ref[rows, :].astype(f32), axis=1, keepdims=True)
        inner_ref[rows, :] = qi + ki + vi
    qgg_ref[...] = qgs
    kgg_ref[...] = kgs

    upper, lower = width // 8, qw // 8
    for c in range(0, width, 256):
        grad = t_dot(n1_ref[...], dqkv_ref[:, c : c + 256])
        out = t_dot(mixed_ref[...], ga_ref[:, c : c + 256])
        for d in range(8):
            grads_ref[d, 0:upper, c : c + 256] = grad[d * upper : (d + 1) * upper].astype(bf16)
            grads_ref[d, upper : upper + lower, c : c + 256] = out[d * lower : (d + 1) * lower].astype(bf16)
    sent = share(grads_ref, info_ref[3], keep_hbm, give_hbm, out_sems)
    for part_ref, cols in zip((p_across, p_far, p_pair, p_own), slices):
        acc_s[...] = (
            dot_t(dqkv_ref[:, 0:qw], wq_ref[cols, :])
            + dot_t(dqkv_ref[:, qw : qw + kw], wk_ref[cols, :])
            + dot_t(dqkv_ref[:, qw + kw : qw + 2 * kw], wv_ref[cols, :])
        )
        norm_back(acc_s, n1_ref, r1_ref, inner_ref, gain_ref[0:1, cols], part_ref, cols, width, gag_ref)
    for copy in sent:
        copy.wait()


def output_kernel(info_ref, middle_ref, attn_ref, own_ref, pair_ref, across_ref, out_ref, sums_ref):
    seq_len, shard = middle_ref.shape
    length = info_ref[0]
    sums = [jnp.zeros((8, shard), f32)] * 3
    for start in range(0, seq_len, ROWS):
        rows = pl.ds(start, ROWS)
        ffn = own_ref[rows, :].astype(f32) + (pair_ref[rows, :].astype(f32) + across_ref[rows, :].astype(f32))
        out = middle_ref[rows, :] + ffn
        out_ref[rows, :] = out.astype(bf16)
        slot = start + lax.broadcasted_iota(jnp.int32, (ROWS, 1), 0)
        for i, v in enumerate((out, attn_ref[rows, :], ffn)):
            v = jnp.where(slot < length, v, 0.0)
            sums[i] = sums[i] + jnp.sum((v * v).reshape(ROWS // 8, 8, shard), axis=0)
    for i in range(3):
        sums_ref[i : i + 1, :] = jnp.sum(sums[i], axis=0, keepdims=True)


def small_kernel(info_ref, gag_ref, gfg_ref, qgg_ref, kgg_ref, sums_ref, small_ref):
    hd, shard = qgg_ref.shape[1], sums_ref.shape[1]
    small_ref[...] = jnp.zeros(small_ref.shape, f32)
    small_ref[0:1, :] = jnp.sum(gag_ref[...], axis=0, keepdims=True)
    small_ref[1:2, :] = jnp.sum(gfg_ref[...], axis=0, keepdims=True)
    small_ref[2:3, 0:hd] = jnp.sum(qgg_ref[...], axis=0, keepdims=True)
    small_ref[2:3, hd : 2 * hd] = jnp.sum(kgg_ref[...], axis=0, keepdims=True)
    lane = lax.broadcasted_iota(jnp.int32, (1, 128), 1)
    totals = (info_ref[0] * shard).astype(f32) * (lane == 3).astype(f32)
    for i in range(3):
        totals = totals + jnp.sum(sums_ref[i : i + 1, :], axis=1, keepdims=True) * (lane == i).astype(f32)
    small_ref[2:3, 2 * hd : 2 * hd + 128] = totals


def block_kernel(info_ref, b0, b1, b2, b3, small_ref, out_ref):
    rows = b0.shape[0]
    out_ref[0:rows, :] = (
        (b0[...].astype(f32) + b1[...].astype(f32)) + (b2[...].astype(f32) + b3[...].astype(f32))
    ).astype(bf16)
    small = small_ref[...]
    high = small.astype(bf16)
    out_ref[rows : rows + TAIL, :] = jnp.concatenate([high, (small - high.astype(f32)).astype(bf16)], axis=0)


def unpack_kernel(info_ref, h0, h1, h2, h3, t0, t1, t2, t3, gq_ref, gk_ref, gv_ref, go_ref, small_ref):
    q, core = info_ref[2], info_ref[3]
    qw, kw = gq_ref.shape[1], gk_ref.shape[1]
    upper, lower = gq_ref.shape[0] // 8, go_ref.shape[0] // 8
    small = jnp.zeros(small_ref.shape, f32)
    for refs, half in (((h0, h1, h2, h3), core), ((t0, t1, t2, t3), 1 - core)):
        for k, ref in enumerate(refs):
            block = half * 4 + jnp.bitwise_xor(q, k)
            rows = pl.ds(pl.multiple_of(block * upper, upper), upper)
            gq_ref[rows, :] = ref[0:upper, 0:qw].astype(f32)
            gk_ref[rows, :] = ref[0:upper, qw : qw + kw].astype(f32)
            gv_ref[rows, :] = ref[0:upper, qw + kw : qw + 2 * kw].astype(f32)
            rows = pl.ds(pl.multiple_of(block * lower, lower), lower)
            go_ref[rows, :] = ref[upper : upper + lower, :].astype(f32)
            tail = ref[upper + lower : upper + lower + TAIL, :].astype(f32)
            small = small + (tail[0:8] + tail[8:16])
    small_ref[...] = small


SPECS = {
    "s": pl.BlockSpec(memory_space=pltpu.SMEM),
    "v": pl.BlockSpec(memory_space=pltpu.VMEM),
    "a": pl.BlockSpec(memory_space=pl.ANY),
}


def call(body, outs, args, scratch=(), sems=(), flops=0, bytes_accessed=0, limit=SMALL_BYTES):
    places, arrays = [], []
    for place, *group in args:
        places += [place] * len(group)
        arrays += group
    return pl.pallas_call(
        body,
        out_shape=[jax.ShapeDtypeStruct(s, d) for s, d, _ in outs],
        in_specs=[SPECS[p] for p in places],
        out_specs=[SPECS[p] for _, _, p in outs],
        scratch_shapes=[pltpu.VMEM(s, d) for s, d in scratch] + [pltpu.SemaphoreType.DMA((n,)) for n in sems],
        compiler_params=pltpu.CompilerParams(vmem_limit_bytes=limit),
        cost_estimate=pl.CostEstimate(flops=flops, bytes_accessed=bytes_accessed, transcendentals=0),
    )(*arrays)


PAIRS = ((0, 1), (1, 0), (2, 3), (3, 2))
MIDDLE = ((1, 2), (2, 1))
OUTWARD = ((1, 0), (2, 3))
INWARD = ((0, 1), (3, 2))
OUTWARD_TWO = ((2, 0), (1, 3))
INWARD_TWO = ((0, 2), (3, 1))


def send(rows, pairs):
    return lax.ppermute(rows, "tensor", pairs)


def hold(*values):
    return lax.optimization_barrier(values)


def gather_line(own):
    pair = send(own, PAIRS)
    across_mid = send(own, MIDDLE)
    far_end = send(pair, OUTWARD_TWO)
    far_mid = send(pair, MIDDLE)
    across_end = send(across_mid, OUTWARD)
    return own, pair, across_mid, across_end, far_mid, far_end


def pick(end, from_end, from_middle):
    return jnp.where(end, from_end, from_middle)


def scatter_first(parts):
    across, far, _, _ = parts
    return send(far, INWARD_TWO), send(far, MIDDLE), send(across, INWARD)


def scatter_last(parts, first):
    across, _, pair, own = parts
    two, three, one = first
    to_pair = (pair.astype(f32) + (two.astype(f32) + three.astype(f32))).astype(bf16)
    to_across = (across.astype(f32) + one.astype(f32)).astype(bf16)
    return own, send(to_pair, PAIRS), send(to_across, MIDDLE)


def add(a, b):
    return (a.astype(f32) + b.astype(f32)).astype(bf16)


def total(terms):
    own, pair, across = terms
    return own.astype(f32) + (pair.astype(f32) + across.astype(f32))


def split_rows(values):
    high = lax.optimization_barrier(values.astype(bf16))
    low = (values - high.astype(f32)).astype(bf16)
    return jnp.concatenate([high, low], axis=0)


def swap(values, bit):
    return lax.ppermute(values, "dp", [(i, i ^ bit) for i in range(8)])


def to_chips(keep, other, info):
    rows, width = keep.shape[1:]
    blocks = call(
        chip_blocks_kernel,
        [((rows, width), bf16, "v")] * 4,
        (("s", info), ("a", keep), ("v", other)),
        scratch=[((4, rows, width), bf16)],
        sems=(1,),
        bytes_accessed=12 * rows * width,
    )
    return [blocks[0]] + [swap(blocks[k], 2 * k) for k in (1, 2, 3)]


def from_chips(own):
    return [own] + [swap(own, 2 * k) for k in (1, 2, 3)]


def per_device(
    hidden_in, lengths, w_query, w_key, w_value, w_out, attn_gain, ffn_gain,
    query_gain, key_gain, w_gate, w_up, w_down, cotangent,
):
    seq_len, shard = hidden_in.shape
    width = w_query.shape[0]
    hd = query_gain.shape[0]
    qw, kw = w_query.shape[1], w_key.shape[1]
    hidden = w_gate.shape[1]
    padded = -(-seq_len // BLOCK) * BLOCK
    z = lax.axis_index("tensor").astype(jnp.int32)
    dp = lax.axis_index("dp").astype(jnp.int32)
    chips = lax.axis_size("dp") == 8
    q, core = (dp // 2, dp % 2) if chips else (0 * dp, 0 * dp)
    info = jnp.stack([lengths[0], z, q, core])
    parts = [((seq_len, shard), bf16, "v")] * 4

    end = (z == 0) | (z == 3)
    gains = jnp.concatenate([attn_gain[None], ffn_gain[None], jnp.zeros((6, shard), f32)], axis=0)
    x = jnp.concatenate([hidden_in, split_rows(gains)], axis=0)
    cot = jnp.concatenate([cotangent, jnp.zeros((TAIL, shard), bf16)], axis=0)
    x_pair, x_mid = send(x, PAIRS), send(x, MIDDLE)
    x_pair, x_mid, cot = hold(x_pair, x_mid, cot)
    x_end, x_far = send(pick(end, cot, x_mid), PAIRS), send(x_pair, MIDDLE)
    x_end, x_far, cot = hold(x_end, x_far, cot)
    x_last, cot_far = send(x_far, OUTWARD), send(x_end, MIDDLE)
    x_last, cot_far, x_end, cot = hold(x_last, cot_far, x_end, cot)
    cot_mid, cot_pair, cot_last = send(cot, MIDDLE), send(cot, OUTWARD), send(cot_far, OUTWARD)
    cos, sin = rope_tables(seq_len, hd)
    qg, kg = query_gain[None], key_gain[None]
    resid = hidden_in.astype(f32)
    valid = (jnp.arange(seq_len, dtype=jnp.int32) < lengths[0]).astype(f32)[:, None]

    saved = [
        ((seq_len, width), bf16), ((seq_len, qw), f32), ((seq_len, kw), f32), ((seq_len, qw), bf16),
        ((padded, kw), bf16), ((padded, kw), bf16), ((seq_len, qw), bf16), ((seq_len, 128), f32),
        ((seq_len, 128), f32), ((8, width), f32),
    ]
    weights = [((width, kw), bf16), ((width, kw), bf16), ((width, qw), bf16), ((qw, width), bf16)]
    tables = [((seq_len, hd), f32)] * 2
    *attn_parts, n1, qpre, kpre, qrot, krot, val, mixed, lse, r1, gain = call(
        attn_forward_kernel,
        parts + [(s, d, "a") for s, d in saved],
        (
            ("s", info), ("v", x, x_pair, x_mid, x_end, x_far, x_last, qg, kg),
            ("a", w_key, cos, sin, w_value, w_query, w_out),
        ),
        scratch=weights[:1] + tables + weights[1:] + saved,
        sems=(6, 10),
        limit=VMEM_BYTES,
        flops=2 * seq_len * width * (2 * qw + 2 * kw) + 4 * seq_len * seq_len * qw,
        bytes_accessed=14_000_000,
    )
    attn_parts, cot_mid, cot_pair, cot_last = hold(attn_parts, cot_mid, cot_pair, cot_last)
    across, far, pair, own = attn_parts
    two, three = send(far, INWARD_TWO), send(far, MIDDLE)
    one = send(pick(end, across, cot_mid[:seq_len]), PAIRS)
    zero_end = pick(end, jnp.zeros_like(one), one)
    attn_local = total(scatter_last(attn_parts, (two, three, zero_end)))
    middle = resid + attn_local
    shard_two, one = hold(middle.astype(bf16), one)
    m_parts = gather_line(shard_two)

    kept = [((seq_len, width), bf16), ((seq_len, width), bf16), ((seq_len, hidden), bf16), ((seq_len, 2 * hidden), bf16)]
    *ffn_parts, gfg, n2, cotm, hid, dgu = call(
        ffn_kernel,
        parts + [((8, width), f32, "v")] + [(s, d, "a") for s, d in kept],
        (
            ("s", info), ("v", *m_parts), ("a", gain, w_gate, w_up, w_down),
            ("a", cot, x_end, cot_pair, cot_mid, one, cot_far, cot_last),
        ),
        scratch=[((8, width), f32)] + [((width, hidden), bf16)] * 2 + [((hidden, width), bf16), ((seq_len, width), bf16)]
        + kept + [((seq_len, 256), f32)] * 3 + [((seq_len, 128), f32)] * 2,
        sems=(8, 4),
        limit=VMEM_BYTES,
        flops=2 * seq_len * width * hidden * 5,
        bytes_accessed=16_000_000,
    )
    grad_top = cotangent.astype(f32) * valid
    first = scatter_first(ffn_parts)
    blocks = ((4, width // 8, 3 * hidden), bf16, "a")
    *down_parts, ffn_keep, ffn_give = call(
        ffn_grad_kernel,
        parts + [blocks] * 2,
        (("s", info), ("a", n2, dgu, hid, cotm, w_down)),
        scratch=[kept[0], kept[3], kept[2], kept[1], ((hidden, width), bf16), ((8, width // 8, 3 * hidden), bf16)],
        sems=(5, 2),
        flops=2 * seq_len * width * hidden * 4,
        bytes_accessed=14_000_000,
    )
    first, ffn_keep, ffn_give = hold(first, ffn_keep, ffn_give)
    back = scatter_last(ffn_parts, first)
    if chips:
        ffn_other = swap(ffn_give, 1)
        cols = (width // 8, 3 * hidden // 2)
        to_x, to_y, keep_x, keep_y = call(
            halves_kernel,
            [((2, *cols), bf16, "v")] * 4,
            (("s", info), ("a", ffn_keep, ffn_other)),
            scratch=[((4, width // 8, 3 * hidden), bf16)] * 2,
            sems=(2,),
        )
        back, to_x, to_y, keep_x, keep_y = hold(back, to_x, to_y, keep_x, keep_y)
    grad_middle = grad_top + total(back)
    across, far, pair, own = down_parts
    ga = grad_middle.astype(bf16)
    ga_pair, ga_mid = send(ga, PAIRS), send(ga, MIDDLE)
    if chips:
        got_x, got_y = swap(to_x, 2), swap(to_y, 4)
    if chips:
        ga_pair, ga_mid, far, got_x, got_y = hold(ga_pair, ga_mid, far, got_x, got_y)
        to_y, to_x, own_x, own_y = call(
            halve_kernel, [(cols, bf16, "v")] * 4, (("s", info), ("v", keep_x, keep_y, got_x, got_y))
        )
        from_y, from_x = swap(to_y, 4), swap(to_x, 2)
    ga_end, ga_far = send(pick(end, far, ga_mid), PAIRS), send(ga_pair, MIDDLE)
    if chips:
        ga_end, ga_far, across, from_y, from_x = hold(ga_end, ga_far, across, from_y, from_x)
        left, right = call(
            join_kernel, [(cols, bf16, "v")] * 2, (("s", info), ("v", own_x, own_y, from_y, from_x))
        )
        left_y, right_x = swap(left, 4), swap(right, 2)
    ga_last = send(pick(end, across, ga_far), PAIRS)
    got_far = send(add(far, ga_end), MIDDLE)
    if chips:
        ga_last, got_far, left_y, right_x = hold(ga_last, got_far, left_y, right_x)
        lefts, rights = jnp.stack([left, left_y]), jnp.stack([right, right_x])
        lefts_x, rights_y = swap(lefts, 2), swap(rights, 4)
    ga_parts = (ga, ga_pair, ga_mid, ga_end, ga_far, ga_last)
    ffn_terms = (own, send(add(pair, got_far), PAIRS), send(add(across, ga_last), MIDDLE))

    blocks = (4, (width + qw) // 8, width)
    *back_parts, gag, qgg, kgg, keep, give = call(
        attn_backward_kernel,
        parts + [((8, width), f32, "v"), ((8, hd), f32, "v"), ((8, hd), f32, "v"), (blocks, bf16, "a"), (blocks, bf16, "a")],
        (
            ("s", info), ("v", *ga_parts, qg, kg),
            ("a", w_out, qrot, krot, val, mixed, lse, cos, sin, qpre, kpre, n1, w_query, w_key, w_value, r1, gain),
        ),
        scratch=[weights[3], saved[3], saved[4], saved[5], saved[6], saved[7], *tables, saved[1], saved[2], saved[0]]
        + [weights[2], weights[0], weights[1], saved[8], saved[9]]
        + [((seq_len, width), bf16), ((seq_len, qw), bf16), ((seq_len, qw), f32), ((padded, kw), f32), ((padded, kw), f32)]
        + [((seq_len, qw + 2 * kw), bf16), ((seq_len, 128), f32), ((seq_len, shard), f32), ((8, *blocks[1:]), bf16)],
        sems=(16, 2),
        limit=VMEM_BYTES,
        flops=2 * seq_len * width * (4 * qw + 4 * kw) + 10 * seq_len * seq_len * qw,
        bytes_accessed=20_000_000,
    )
    if chips:
        back_parts, ffn_terms, keep, give, lefts_x, rights_y = hold(back_parts, ffn_terms, keep, give, lefts_x, rights_y)
        blocks = to_chips(keep, swap(give, 1), info)
    out_rows, sums = call(
        output_kernel,
        [((seq_len, shard), bf16, "v"), ((8, shard), f32, "v")],
        (("s", info), ("v", middle, attn_local, *ffn_terms)),
        bytes_accessed=2_000_000,
    )
    small = call(small_kernel, [((8, width), f32, "v")], (("s", info), ("v", gag, gfg, qgg, kgg, sums)))[0]
    shapes = [(width, qw), (width, kw), (width, kw), (qw, width)]
    if chips:
        ffn_halves = (lefts, lefts_x, rights, rights_y)
        g_gate, g_up, g_down = call(
            unpack_ffn_kernel,
            [(s, f32, "v") for s in ((width, hidden), (width, hidden), (hidden, width))],
            (("s", info), ("v", *ffn_halves, *[swap(b, 1) for b in ffn_halves])),
            bytes_accessed=14_000_000,
        )
        small = small + send(small, PAIRS)
        small = small + send(small, ((0, 2), (2, 0), (1, 3), (3, 1)))
        small, back_parts = hold(small, back_parts)
        blocks, small, g_gate, g_up, g_down = hold(blocks, small, g_gate, g_up, g_down)
        own = call(
            block_kernel,
            [((blocks[0].shape[0] + TAIL, width), bf16, "v")],
            (("s", info), ("v", *blocks, small)),
            bytes_accessed=2_000_000,
        )[0]
        everyone = from_chips(own)
        back_terms = scatter_last(back_parts, scatter_first(back_parts))
        gq, gk, gv, go, small = call(
            unpack_kernel,
            [(s, f32, "v") for s in shapes] + [((8, width), f32, "v")],
            (("s", info), ("v", *everyone, *[swap(b, 1) for b in everyone])),
            bytes_accessed=9_000_000,
        )
    else:
        back_terms = scatter_last(back_parts, scatter_first(back_parts))
        grads, ffn_grads = lax.psum((jnp.concatenate([keep, give]), jnp.concatenate([ffn_keep, ffn_give])), "dp")
        small = lax.psum(small, ("dp", "tensor"))
        g_qkv = grads[:, : width // 8].reshape(width, width).astype(f32)
        gq, gk, gv = g_qkv[:, :qw], g_qkv[:, qw : qw + kw], g_qkv[:, qw + kw :]
        go = grads[:, width // 8 :].reshape(qw, width).astype(f32)
        g_gate = ffn_grads[:, :, :hidden].reshape(width, hidden).astype(f32)
        g_up = ffn_grads[:, :, hidden : 2 * hidden].reshape(width, hidden).astype(f32)
        folded = ffn_grads[:, :, 2 * hidden :]
        lower = hidden // 8
        tail = folded[:, lower:].reshape(8, width // 8 - lower, -1, 256).transpose(0, 2, 1, 3).reshape(8, lower, 256)
        g_down = jnp.concatenate([folded[:, :lower], tail], axis=2).reshape(hidden, width).astype(f32)
    input_grad = (grad_middle + total(back_terms)).astype(bf16)
    grad_attn_gain = lax.dynamic_slice(small[0], (z * shard,), (shard,))
    grad_ffn_gain = lax.dynamic_slice(small[1], (z * shard,), (shard,))
    totals = small[2, 2 * hd : 2 * hd + 4]
    return (
        out_rows,
        input_grad,
        gq,
        gk,
        gv,
        go,
        grad_attn_gain,
        grad_ffn_gain,
        small[2, :hd],
        small[2, hd : 2 * hd],
        g_gate,
        g_up,
        g_down,
        jnp.sqrt(totals[:3] / totals[3]),
    )


def solution(mesh):
    rows, cols, first = P("dp", "tensor"), P(None, "tensor"), P("tensor", None)
    gain = P("tensor")
    return jax.shard_map(
        per_device,
        mesh=mesh,
        in_specs=(rows, P("dp"), cols, cols, cols, first, gain, gain, P(), P(), cols, cols, first, rows),
        out_specs=(rows, rows, cols, cols, cols, first, gain, gain, P(), P(), cols, cols, first, P()),
        check_vma=False,
    )
```

time: 386 us -> 325 us (0.84)
  the two profiles are of different devices: /device:TPU:0 before, /device:TPU:9 now
where the time goes in v2:
time: 325 us; the launch traced here: 319 us
  starting transfers between devices  120 us (37%)
  waiting for transfers between devices  98.3 us (30%)
  Pallas kernels  73.4 us (23%)
  other arithmetic  14.4 us (4%)
  local copies, waits for them, and re-layouts  10.8 us (3%)
    ppermute x39, waiting for transfers between devices, send(): return lax.ppermute(rows, 'tensor', pairs)  82.6 us
    pallas_call x13, Pallas kernels, call(): pl.pallas_call(body, out_shape=[jax.ShapeDtypeStruct(s, d) for s, d, _ in...  73.4 us
    ppermute x39, starting transfers between devices, send(): return lax.ppermute(rows, 'tensor', pairs)  71.4 us
    ppermute x24, starting transfers between devices, swap(): return lax.ppermute(values, 'dp', [(i, i ^ bit) for i in range(8)])  48.3 us
    ppermute x24, waiting for transfers between devices, swap(): return lax.ppermute(values, 'dp', [(i, i ^ bit) for i in range(8)])  15.7 us
    unnamed x102, local copies, waits for them, and re-layouts  7.47 us
  transfers between devices with their start and end apart: 63, of which 32 were waited for; matrix products, arithmetic and copies ran while one was open for 4% of the time, Pallas kernels for 18%

profile of v2, /device:TPU:9, one launch (start us, length us, event | category | flops | bytes accessed | tf_op | source)
XLA Modules:
  0.0 319.1 jit_solution(1135887547201432264)
XLA Ops:
  3.4 4.5 %collective-permute-start.1 = (bf16[720,256]{1,0:T(8,128)(2,1)S(1)}, bf16[720,256]{1,0:T(8,128)(2,1)S(1)}, u32[]{:S(2)}, u32[]{:S(2)}) collective-permute-start(bf16[720,256]{1,0:T(8,128)(2,1)S(1)} %pad_maximum_fusion.2.x0), channel_id=1, source_target_pairs={{1,2},{2,1},{5,6},{6,5},{9,10},{10,9},{13,14},{14,13},{17,18},{18,... | collective-permute-start | bytes 1105928 | tf_op jit(solution)/shard_map/ppermute | solution.py:612
  8.9 3.9 %collective-permute-done.x1 = bf16[720,256]{1,0:T(8,128)(2,1)S(1)} collective-permute-done((bf16[720,256]{1,0:T(8,128)(2,1)S(1)}, bf16[720,256]{1,0:T(8,128)(2,1)S(1)}, u32[]{:S(2)}, u32[]{:S(2)}) %collective-permute-start) | collective-permute-done | bytes 368672 | tf_op jit(solution)/shard_map/ppermute | solution.py:612
  19.7 4.8 %collective-permute-done.2.x3.c1 = bf16[720,256]{1,0:T(8,128)(2,1)S(1)} collective-permute-done((bf16[720,256]{1,0:T(8,128)(2,1)S(1)}, bf16[720,256]{1,0:T(8,128)(2,1)S(1)}, u32[]{:S(2)}, u32[]{:S(2)}) %collective-permute-start.2) | collective-permute-done | bytes 368672 | tf_op jit(solution)/shard_map/ppermute | solution.py:612
  33.3 3.9 %collective-permute-done.5.c5 = bf16[720,256]{1,0:T(8,128)(2,1)S(1)} collective-permute-done((bf16[720,256]{1,0:T(8,128)(2,1)S(1)}, bf16[720,256]{1,0:T(8,128)(2,1)S(1)}, u32[]{:S(2)}, u32[]{:S(2)}) %collective-permute-start.5) | collective-permute-done | bytes 368672 | tf_op jit(solution)/shard_map/ppermute | solution.py:612
  42.9 12.3 %shard_map.245 = (bf16[704,256]{1,0:T(8,128)(2,1)}, bf16[704,256]{1,0:T(8,128)(2,1)}, bf16[704,256]{1,0:T(8,128)(2,1)}, bf16[704,256]{1,0:T(8,128)(2,1)}, bf16[7...) custom-call(s32[4]{0:T(128)} %pad_add_fusion.info_ref, ...), custom_call_target="tpu_custom_call" | custom-call | flops 3229614080 | bytes 14000000 | tf_op jit(solution)/shard_map/pallas_call | solution.py:592
  63.0 4.2 %collective-permute-done.10 = bf16[704,256]{1,0:T(8,128)(2,1)S(1)} collective-permute-done((bf16[704,256]{1,0:T(8,128)(2,1)}, bf16[704,256]{1,0:T(8,128)(2,1)S(1)}, u32[]{:S(2)}, u32[]{:S(2)}) %collective-permute-start.10) | collective-permute-done | bytes 360480 | tf_op jit(solution)/shard_map/ppermute | solution.py:612
  68.9 5.2 %collective-permute-done.12.c4 = bf16[704,256]{1,0:T(8,128)(2,1)S(1)} collective-permute-done((bf16[704,256]{1,0:T(8,128)(2,1)S(1)}, bf16[704,256]{1,0:T(8,128)(2,1)S(1)}, u32[]{:S(2)}, u32[]{:S(2)}) %collective-permute-start.12) | collective-permute-done | bytes 360480 | tf_op jit(solution)/shard_map/ppermute | solution.py:612
  77.4 4.4 %collective-permute-done.11 = bf16[704,256]{1,0:T(8,128)(2,1)S(1)} collective-permute-done((bf16[704,256]{1,0:T(8,128)(2,1)S(1)}, bf16[704,256]{1,0:T(8,128)(2,1)S(1)}, u32[]{:S(2)}, u32[]{:S(2)}) %collective-permute-start.11) | collective-permute-done | bytes 360480 | tf_op jit(solution)/shard_map/ppermute | solution.py:612
  86.2 8.3 %collective-permute-done.15.m2 = bf16[704,256]{1,0:T(8,128)(2,1)S(1)} collective-permute-done((bf16[704,256]{1,0:T(8,128)(2,1)S(1)}, bf16[704,256]{1,0:T(8,128)(2,1)S(1)}, u32[]{:S(2)}, u32[]{:S(2)}) %collective-permute-start.15) | collective-permute-done | bytes 360480 | tf_op jit(solution)/shard_map/ppermute | solution.py:612
  100.8 7.3 %collective-permute-done.17.m4 = bf16[704,256]{1,0:T(8,128)(2,1)S(1)} collective-permute-done((bf16[704,256]{1,0:T(8,128)(2,1)S(1)}, bf16[704,256]{1,0:T(8,128)(2,1)S(1)}, u32[]{:S(2)}, u32[]{:S(2)}) %collective-permute-start.17) | collective-permute-done | bytes 360480 | tf_op jit(solution)/shard_map/ppermute | solution.py:612
  112.2 12.7 %shard_map.246 = (bf16[704,256]{1,0:T(8,128)(2,1)}, bf16[704,256]{1,0:T(8,128)(2,1)}, bf16[704,256]{1,0:T(8,128)(2,1)}, bf16[704,256]{1,0:T(8,128)(2,1)}, f32[8,...) custom-call(s32[4]{0:T(128)} %pad_add_fusion.info_ref, ...), custom_call_target="tpu_custom_call" | custom-call | flops 5536481280 | bytes 16000000 | tf_op jit(solution)/shard_map/pallas_call | solution.py:592
  135.1 7.4 %shard_map.247 = (bf16[704,256]{1,0:T(8,128)(2,1)S(1)}, bf16[704,256]{1,0:T(8,128)(2,1)S(1)}, bf16[704,256]{1,0:T(8,128)(2,1)S(1)}, bf16[704,256]{1,0:T(8,128)(2...) custom-call(s32[4]{0:T(128)S(1)} %copy-done.3, bf16[704,1024]{1,0:T(8,128)(2,1)S(1)} %copy-done.11, ...), custom_call_target="tpu_custom_call" | custom-call | flops 4429185024 | bytes 14000000 | tf_op jit(solution)/shard_map/pallas_call | solution.py:592
  142.5 11.7 %collective-permute-start.24 = (bf16[4,128,2304]{2,1,0:T(8,128)(2,1)S(1)}, bf16[4,128,2304]{2,1,0:T(8,128)(2,1)S(1)}, u32[]{:S(2)}, u32[]{:S(2)}) collective-permute-start(bf16[4,128,2304]{2,1,0:T(8,128)(2,1)S(1)} %get-tuple-element.183), channel_id=1, source_target_pairs={{0,4},{4,0},{8,12},{12,8},{16,20},{20,16},{24,28},{28,24},{1,5},{5... | collective-permute-start | bytes 7077896 | tf_op jit(solution)/shard_map/ppermute | solution.py:661
  159.7 6.4 %collective-permute-done.23 = bf16[704,256]{1,0:T(8,128)(2,1)S(1)} collective-permute-done((bf16[704,256]{1,0:T(8,128)(2,1)S(1)}, bf16[704,256]{1,0:T(8,128)(2,1)S(1)}, u32[]{:S(2)}, u32[]{:S(2)}) %collective-permute-start.23) | collective-permute-done | bytes 360480 | tf_op jit(solution)/shard_map/ppermute | solution.py:612
  173.5 4.8 %collective-permute-done.25.g1 = bf16[704,256]{1,0:T(8,128)(2,1)S(1)} collective-permute-done((bf16[704,256]{1,0:T(8,128)(2,1)S(1)}, bf16[704,256]{1,0:T(8,128)(2,1)S(1)}, u32[]{:S(2)}, u32[]{:S(2)}) %collective-permute-start.25) | collective-permute-done | bytes 360480 | tf_op jit(solution)/shard_map/ppermute | solution.py:612
  188.3 4.4 %collective-permute-done.31.from_y = bf16[128,1152]{1,0:T(8,128)(2,1)S(1)} collective-permute-done((bf16[128,1152]{1,0:T(8,128)(2,1)S(1)}, bf16[128,1152]{1,0:T(8,128)(2,1)S(1)}, u32[]{:S(2)}, u32[]{:S(2)}) %collective-permute-start.31) | collective-permute-done | bytes 294944 | tf_op jit(solution)/shard_map/ppermute | solution.py:661
  197.9 5.0 %collective-permute-done.35 = bf16[128,1152]{1,0:T(8,128)(2,1)S(1)} collective-permute-done((bf16[128,1152]{1,0:T(8,128)(2,1)S(1)}, bf16[128,1152]{1,0:T(8,128)(2,1)S(1)}, u32[]{:S(2)}, u32[]{:S(2)}) %collective-permute-start.35) | collective-permute-done | bytes 294944 | tf_op jit(solution)/shard_map/ppermute | solution.py:661
  209.7 25.3 %shard_map.251 = (bf16[704,256]{1,0:T(8,128)(2,1)}, bf16[704,256]{1,0:T(8,128)(2,1)}, bf16[704,256]{1,0:T(8,128)(2,1)}, bf16[704,256]{1,0:T(8,128)(2,1)}, f32[8,...) custom-call(s32[4]{0:T(128)} %pad_add_fusion.info_ref, ...), custom_call_target="tpu_custom_call" | custom-call | flops 6966738944 | bytes 20000000 | tf_op jit(solution)/shard_map/pallas_call | solution.py:592
  235.1 7.4 %collective-permute-start.48 = (bf16[4,192,1024]{2,1,0:T(8,128)(2,1)}, bf16[4,192,1024]{2,1,0:T(8,128)(2,1)S(1)}, u32[]{:S(2)}, u32[]{:S(2)}) collective-permute-start(bf16[4,192,1024]{2,1,0:T(8,128)(2,1)} %get-tuple-element.252), channel_id=1, source_target_pairs={{0,4},{4,0},{8,12},{12,8},{16,20},{20,16},{24,28},{28,24},{1,5},{5... | collective-permute-start | bytes 4718600 | tf_op jit(solution)/shard_map/ppermute | solution.py:661
  263.9 10.6 %collective-permute-done.44 = bf16[704,256]{1,0:T(8,128)(2,1)S(1)} collective-permute-done((bf16[704,256]{1,0:T(8,128)(2,1)S(1)}, bf16[704,256]{1,0:T(8,128)(2,1)S(1)}, u32[]{:S(2)}, u32[]{:S(2)}) %collective-permute-start.44) | collective-permute-done | bytes 360480 | tf_op jit(solution)/shard_map/ppermute | solution.py:612
  278.8 4.9 %shard_map.255 = (f32[1024,768]{1,0:T(8,128)}, f32[1024,768]{1,0:T(8,128)}, f32[768,1024]{1,0:T(8,128)}) custom-call(s32[4]{0:T(128)S(1)} %copy-done.4, bf16[2,128,1152]{2,1,0:T(8,128)(2,1)S(1)} %pad_maximum_fusion.refs_0_, bf16[2,128,1152]{2,1,0:T(8,128)(2,1)S(1)} %collective-permute-done.39.refs_1_, bf16[2,128,1152]{2,1,0:T(8,128)(2,1)S(1)} %pad_maximum_fusion.1.refs_2_, ...), custom_call_target="tpu_custom_call" | custom-call | bytes 14000000 | tf_op jit(solution)/shard_map/pallas_call | solution.py:592
  296.3 4.1 %collective-permute-start.60 = (bf16[208,1024]{1,0:T(8,128)(2,1)S(1)}, bf16[208,1024]{1,0:T(8,128)(2,1)S(1)}, u32[]{:S(2)}, u32[]{:S(2)}) collective-permute-start(bf16[208,1024]{1,0:T(8,128)(2,1)S(1)} %collective-permute-done.56.h1), channel_id=1, source_target_pairs={{0,4},{4,0},{8,12},{12,8},{16,20},{20,16},{24,28},{28,24},{1,5},{5... | collective-permute-start | bytes 1277960 | tf_op jit(solution)/shard_map/ppermute | solution.py:661
  300.5 8.5 %collective-permute-start.61 = (bf16[208,1024]{1,0:T(8,128)(2,1)S(1)}, bf16[208,1024]{1,0:T(8,128)(2,1)S(1)}, u32[]{:S(2)}, u32[]{:S(2)}) collective-permute-start(bf16[208,1024]{1,0:T(8,128)(2,1)S(1)} %collective-permute-done.57.h2), channel_id=1, source_target_pairs={{0,4},{4,0},{8,12},{12,8},{16,20},{20,16},{24,28},{28,24},{1,5},{5... | collective-permute-start | bytes 1277960 | tf_op jit(solution)/shard_map/ppermute | solution.py:661
  311.8 3.6 %shard_map.257 = (f32[1024,512]{1,0:T(8,128)}, f32[1024,256]{1,0:T(8,128)}, f32[1024,256]{1,0:T(8,128)}, f32[512,1024]{1,0:T(8,128)}, f32[8,1024]{1,0:T(8,128)S(1)}) custom-call(s32[4]{0:T(128)S(1)} %copy-done.4, bf16[208,1024]{1,0:T(8,128)(2,1)S(1)} %shard_map.256.h0, bf16[208,1024]{1,0:T(8,128)(2,1)S(1)} %collective-permute-done.56.h1, ...), custom_call_target="tpu_custom_call" | custom-call | bytes 9000000 | tf_op jit(solution)/shard_map/pallas_call | solution.py:592
  (254 shorter events, 141.1 us)
Async XLA Ops:
  37.2 18.0 %collective-permute-start.6 = (bf16[720,256]{1,0:T(8,128)(2,1)S(1)}, bf16[720,256]{1,0:T(8,128)(2,1)S(1)}, u32[]{:S(2)}, u32[]{:S(2)}) collective-permute-start(bf16[720,256]{1,0:T(8,128)(2,1)S(1)} %concatenate.17.c0), channel_id=1, source_target_pairs={{1,2},{2,1},{5,6},{6,5},{9,10},{10,9},{13,14},{14,13},{17,18},{18,... | collective-permute-start | bytes 1105928 | tf_op jit(solution)/shard_map/ppermute | solution.py:612
  39.6 15.6 %collective-permute-start.7 = (bf16[720,256]{1,0:T(8,128)(2,1)S(1)}, bf16[720,256]{1,0:T(8,128)(2,1)S(1)}, u32[]{:S(2)}, u32[]{:S(2)}) collective-permute-start(bf16[720,256]{1,0:T(8,128)(2,1)S(1)} %concatenate.17.c0), channel_id=1, source_target_pairs={{1,0},{2,3},{5,4},{6,7},{9,8},{10,11},{13,12},{14,15},{17,16},{18,... | collective-permute-start | bytes 1105928 | tf_op jit(solution)/shard_map/ppermute | solution.py:612
  40.9 14.3 %collective-permute-start.8 = (bf16[720,256]{1,0:T(8,128)(2,1)S(1)}, bf16[720,256]{1,0:T(8,128)(2,1)S(1)}, u32[]{:S(2)}, u32[]{:S(2)}) collective-permute-start(bf16[720,256]{1,0:T(8,128)(2,1)S(1)} %collective-permute-done.5.c5), channel_id=1, source_target_pairs={{1,0},{2,3},{5,4},{6,7},{9,8},{10,11},{13,12},{14,15},{17,16},{18,... | collective-permute-start | bytes 1105928 | tf_op jit(solution)/shard_map/ppermute | solution.py:612
  59.6 14.4 %collective-permute-start.12 = (bf16[704,256]{1,0:T(8,128)(2,1)S(1)}, bf16[704,256]{1,0:T(8,128)(2,1)S(1)}, u32[]{:S(2)}, u32[]{:S(2)}) collective-permute-start(bf16[704,256]{1,0:T(8,128)(2,1)S(1)} %slice_select_fusion), channel_id=1, source_target_pairs={{0,1},{1,0},{2,3},{3,2},{4,5},{5,4},{6,7},{7,6},{8,9},{9,8},{10,11... | collective-permute-start | bytes 1081352 | tf_op jit(solution)/shard_map/ppermute | solution.py:612
  124.9 17.5 %collective-permute-start.19 = (bf16[704,256]{1,0:T(8,128)(2,1)}, bf16[704,256]{1,0:T(8,128)(2,1)S(1)}, u32[]{:S(2)}, u32[]{:S(2)}) collective-permute-start(bf16[704,256]{1,0:T(8,128)(2,1)} %get-tuple-element.171), channel_id=1, source_target_pairs={{0,2},{3,1},{4,6},{7,5},{8,10},{11,9},{12,14},{15,13},{16,18},{19,... | collective-permute-start | bytes 1081352 | tf_op jit(solution)/shard_map/ppermute | solution.py:612
  126.2 16.2 %collective-permute-start.20 = (bf16[704,256]{1,0:T(8,128)(2,1)}, bf16[704,256]{1,0:T(8,128)(2,1)S(1)}, u32[]{:S(2)}, u32[]{:S(2)}) collective-permute-start(bf16[704,256]{1,0:T(8,128)(2,1)} %get-tuple-element.171), channel_id=1, source_target_pairs={{1,2},{2,1},{5,6},{6,5},{9,10},{10,9},{13,14},{14,13},{17,18},{18,... | collective-permute-start | bytes 1081352 | tf_op jit(solution)/shard_map/ppermute | solution.py:612
  128.2 14.3 %collective-permute-start.21 = (bf16[704,256]{1,0:T(8,128)(2,1)}, bf16[704,256]{1,0:T(8,128)(2,1)S(1)}, u32[]{:S(2)}, u32[]{:S(2)}) collective-permute-start(bf16[704,256]{1,0:T(8,128)(2,1)} %get-tuple-element.172), channel_id=1, source_target_pairs={{0,1},{3,2},{4,5},{7,6},{8,9},{11,10},{12,13},{15,14},{16,17},{19,... | collective-permute-start | bytes 1081352 | tf_op jit(solution)/shard_map/ppermute | solution.py:612
  142.5 15.8 %collective-permute-start.24 = (bf16[4,128,2304]{2,1,0:T(8,128)(2,1)S(1)}, bf16[4,128,2304]{2,1,0:T(8,128)(2,1)S(1)}, u32[]{:S(2)}, u32[]{:S(2)}) collective-permute-start(bf16[4,128,2304]{2,1,0:T(8,128)(2,1)S(1)} %get-tuple-element.183), channel_id=1, source_target_pairs={{0,4},{4,0},{8,12},{12,8},{16,20},{20,16},{24,28},{28,24},{1,5},{5... | collective-permute-start | bytes 7077896 | tf_op jit(solution)/shard_map/ppermute | solution.py:661
  203.5 31.6 %collective-permute-start.40 = (bf16[2,128,1152]{2,1,0:T(8,128)(2,1)S(1)}, bf16[2,128,1152]{2,1,0:T(8,128)(2,1)S(1)}, u32[]{:S(2)}, u32[]{:S(2)}) collective-permute-start(bf16[2,128,1152]{2,1,0:T(8,128)(2,1)S(1)} %pad_maximum_fusion.1.refs_2_), channel_id=1, source_target_pairs={{0,16},{4,20},{8,24},{12,28},{16,0},{20,4},{24,8},{28,12},{1,17},{... | collective-permute-start | bytes 1769480 | tf_op jit(solution)/shard_map/ppermute | solution.py:661
  204.6 30.5 %collective-permute-start.39 = (bf16[2,128,1152]{2,1,0:T(8,128)(2,1)S(1)}, bf16[2,128,1152]{2,1,0:T(8,128)(2,1)S(1)}, u32[]{:S(2)}, u32[]{:S(2)}) collective-permute-start(bf16[2,128,1152]{2,1,0:T(8,128)(2,1)S(1)} %pad_maximum_fusion.refs_0_), channel_id=1, source_target_pairs={{0,8},{4,12},{8,0},{12,4},{16,24},{20,28},{24,16},{28,20},{1,9},{5... | collective-permute-start | bytes 1769480 | tf_op jit(solution)/shard_map/ppermute | solution.py:661
  205.8 29.2 %collective-permute-start.38 = (bf16[704,256]{1,0:T(8,128)(2,1)}, bf16[704,256]{1,0:T(8,128)(2,1)}, u32[]{:S(2)}, u32[]{:S(2)}) collective-permute-start(bf16[704,256]{1,0:T(8,128)(2,1)} %add_convert_fusion.3), channel_id=1, source_target_pairs={{1,2},{2,1},{5,6},{6,5},{9,10},{10,9},{13,14},{14,13},{17,18},{18,... | collective-permute-start | bytes 1081352 | tf_op jit(solution)/shard_map/ppermute | solution.py:612
  209.7 25.3 %collective-permute-start.37 = (bf16[704,256]{1,0:T(8,128)(2,1)}, bf16[704,256]{1,0:T(8,128)(2,1)}, u32[]{:S(2)}, u32[]{:S(2)}) collective-permute-start(bf16[704,256]{1,0:T(8,128)(2,1)} %add_convert_fusion.4), channel_id=1, source_target_pairs={{0,1},{1,0},{2,3},{3,2},{4,5},{5,4},{6,7},{7,6},{8,9},{9,8},{10,11... | collective-permute-start | bytes 1081352 | tf_op jit(solution)/shard_map/ppermute | solution.py:612
  235.1 23.0 %collective-permute-start.48 = (bf16[4,192,1024]{2,1,0:T(8,128)(2,1)}, bf16[4,192,1024]{2,1,0:T(8,128)(2,1)S(1)}, u32[]{:S(2)}, u32[]{:S(2)}) collective-permute-start(bf16[4,192,1024]{2,1,0:T(8,128)(2,1)} %get-tuple-element.252), channel_id=1, source_target_pairs={{0,4},{4,0},{8,12},{12,8},{16,20},{20,16},{24,28},{28,24},{1,5},{5... | collective-permute-start | bytes 4718600 | tf_op jit(solution)/shard_map/ppermute | solution.py:661
  242.6 19.6 %collective-permute-start.52 = (bf16[2,128,1152]{2,1,0:T(8,128)(2,1)S(1)}, bf16[2,128,1152]{2,1,0:T(8,128)(2,1)S(1)}, u32[]{:S(2)}, u32[]{:S(2)}) collective-permute-start(bf16[2,128,1152]{2,1,0:T(8,128)(2,1)S(1)} %pad_maximum_fusion.refs_0_), channel_id=1, source_target_pairs={{0,4},{4,0},{8,12},{12,8},{16,20},{20,16},{24,28},{28,24},{1,5},{5... | collective-permute-start | bytes 1769480 | tf_op jit(solution)/shard_map/ppermute | solution.py:661
  243.0 32.2 %collective-permute-start.53 = (bf16[2,128,1152]{2,1,0:T(8,128)(2,1)S(1)}, bf16[2,128,1152]{2,1,0:T(8,128)(2,1)S(1)}, u32[]{:S(2)}, u32[]{:S(2)}) collective-permute-start(bf16[2,128,1152]{2,1,0:T(8,128)(2,1)S(1)} %collective-permute-done.39.refs_1_), channel_id=1, source_target_pairs={{0,4},{4,0},{8,12},{12,8},{16,20},{20,16},{24,28},{28,24},{1,5},{5... | collective-permute-start | bytes 1769480 | tf_op jit(solution)/shard_map/ppermute | solution.py:661
  254.9 19.5 %collective-permute-start.44 = (bf16[704,256]{1,0:T(8,128)(2,1)S(1)}, bf16[704,256]{1,0:T(8,128)(2,1)S(1)}, u32[]{:S(2)}, u32[]{:S(2)}) collective-permute-start(bf16[704,256]{1,0:T(8,128)(2,1)S(1)} %copy-done.45), channel_id=1, source_target_pairs={{1,2},{2,1},{5,6},{6,5},{9,10},{10,9},{13,14},{14,13},{17,18},{18,... | collective-permute-start | bytes 1081352 | tf_op jit(solution)/shard_map/ppermute | solution.py:612
  258.1 18.6 %collective-permute-start.55 = (bf16[2,128,1152]{2,1,0:T(8,128)(2,1)S(1)}, bf16[2,128,1152]{2,1,0:T(8,128)(2,1)S(1)}, u32[]{:S(2)}, u32[]{:S(2)}) collective-permute-start(bf16[2,128,1152]{2,1,0:T(8,128)(2,1)S(1)} %collective-permute-done.40.refs_3_), channel_id=1, source_target_pairs={{0,4},{4,0},{8,12},{12,8},{16,20},{20,16},{24,28},{28,24},{1,5},{5... | collective-permute-start | bytes 1769480 | tf_op jit(solution)/shard_map/ppermute | solution.py:661
  262.2 21.5 %collective-permute-start.49 = (bf16[192,1024]{1,0:T(8,128)(2,1)S(1)}, bf16[192,1024]{1,0:T(8,128)(2,1)S(1)}, u32[]{:S(2)}, u32[]{:S(2)}) collective-permute-start(bf16[192,1024]{1,0:T(8,128)(2,1)S(1)} %get-tuple-element.254), channel_id=1, source_target_pairs={{0,8},{4,12},{8,0},{12,4},{16,24},{20,28},{24,16},{28,20},{1,9},{5... | collective-permute-start | bytes 1179656 | tf_op jit(solution)/shard_map/ppermute | solution.py:661
  263.9 19.8 %collective-permute-start.50 = (bf16[192,1024]{1,0:T(8,128)(2,1)S(1)}, bf16[192,1024]{1,0:T(8,128)(2,1)S(1)}, u32[]{:S(2)}, u32[]{:S(2)}) collective-permute-start(bf16[192,1024]{1,0:T(8,128)(2,1)S(1)} %get-tuple-element.255), channel_id=1, source_target_pairs={{0,16},{4,20},{8,24},{12,28},{16,0},{20,4},{24,8},{28,12},{1,17},{... | collective-permute-start | bytes 1179656 | tf_op jit(solution)/shard_map/ppermute | solution.py:661
  276.6 17.3 %collective-permute-start.45 = (bf16[704,256]{1,0:T(8,128)(2,1)S(1)}, bf16[704,256]{1,0:T(8,128)(2,1)S(1)}, u32[]{:S(2)}, u32[]{:S(2)}) collective-permute-start(bf16[704,256]{1,0:T(8,128)(2,1)S(1)} %add_convert_fusion.2), channel_id=1, source_target_pairs={{0,1},{1,0},{2,3},{3,2},{4,5},{5,4},{6,7},{7,6},{8,9},{9,8},{10,11... | collective-permute-start | bytes 1081352 | tf_op jit(solution)/shard_map/ppermute | solution.py:612
  287.6 21.4 %collective-permute-start.58 = (bf16[208,1024]{1,0:T(8,128)(2,1)S(1)}, bf16[208,1024]{1,0:T(8,128)(2,1)S(1)}, u32[]{:S(2)}, u32[]{:S(2)}) collective-permute-start(bf16[208,1024]{1,0:T(8,128)(2,1)S(1)} %shard_map.256.h0), channel_id=1, source_target_pairs={{0,24},{4,28},{8,16},{12,20},{16,8},{20,12},{24,0},{28,4},{1,25},{... | collective-permute-start | bytes 1277960 | tf_op jit(solution)/shard_map/ppermute | solution.py:661
  289.8 19.2 %collective-permute-start.47 = (bf16[704,256]{1,0:T(8,128)(2,1)}, bf16[704,256]{1,0:T(8,128)(2,1)}, u32[]{:S(2)}, u32[]{:S(2)}) collective-permute-start(bf16[704,256]{1,0:T(8,128)(2,1)} %add_convert_fusion.1), channel_id=1, source_target_pairs={{1,2},{2,1},{5,6},{6,5},{9,10},{10,9},{13,14},{14,13},{17,18},{18,... | collective-permute-start | bytes 1081352 | tf_op jit(solution)/shard_map/ppermute | solution.py:612
  294.0 17.8 %collective-permute-start.59 = (bf16[208,1024]{1,0:T(8,128)(2,1)S(1)}, bf16[208,1024]{1,0:T(8,128)(2,1)S(1)}, u32[]{:S(2)}, u32[]{:S(2)}) collective-permute-start(bf16[208,1024]{1,0:T(8,128)(2,1)S(1)} %shard_map.256.h0), channel_id=1, source_target_pairs={{0,4},{4,0},{8,12},{12,8},{16,20},{20,16},{24,28},{28,24},{1,5},{5... | collective-permute-start | bytes 1277960 | tf_op jit(solution)/shard_map/ppermute | solution.py:661
  296.3 15.5 %collective-permute-start.60 = (bf16[208,1024]{1,0:T(8,128)(2,1)S(1)}, bf16[208,1024]{1,0:T(8,128)(2,1)S(1)}, u32[]{:S(2)}, u32[]{:S(2)}) collective-permute-start(bf16[208,1024]{1,0:T(8,128)(2,1)S(1)} %collective-permute-done.56.h1), channel_id=1, source_target_pairs={{0,4},{4,0},{8,12},{12,8},{16,20},{20,16},{24,28},{28,24},{1,5},{5... | collective-permute-start | bytes 1277960 | tf_op jit(solution)/shard_map/ppermute | solution.py:661
  (90 other events, 1132.6 us)

commit v3 on v2

--- a/solution.py
+++ b/solution.py
@@ -14,7 +14,8 @@
 NEG = -1e30
 ROWS = 64
 TAIL = 16
-VMEM_BYTES = 60 * 1024 * 1024
+FULL_BYTES = 60 * 1024 * 1024
+VMEM_BYTES = 40 * 1024 * 1024
 SMALL_BYTES = 24 * 1024 * 1024
 
 bf16 = jnp.bfloat16
@@ -341,14 +342,6 @@
         copy.wait()
 
 
-def chip_blocks_kernel(info_ref, keep_hbm, other_ref, b0, b1, b2, b3, keep_ref, sems):
-    (got,) = copies((keep_hbm,), (keep_ref,), sems)
-    got.wait()
-    for k, out_ref in enumerate((b0, b1, b2, b3)):
-        block = jnp.bitwise_xor(info_ref[2], k)
-        out_ref[...] = (keep_ref[block].astype(f32) + other_ref[block].astype(f32)).astype(bf16)
-
-
 def halves_kernel(info_ref, keep_hbm, other_hbm, to_x, to_y, keep_x, keep_y, keep_ref, other_ref, sems):
     for copy in copies((keep_hbm, other_hbm), (keep_ref, other_ref), sems):
         copy.wait()
@@ -548,33 +541,50 @@
     small_ref[2:3, 2 * hd : 2 * hd + 128] = totals
 
 
-def block_kernel(info_ref, b0, b1, b2, b3, small_ref, out_ref):
-    rows = b0.shape[0]
-    out_ref[0:rows, :] = (
-        (b0[...].astype(f32) + b1[...].astype(f32)) + (b2[...].astype(f32) + b3[...].astype(f32))
-    ).astype(bf16)
+def block_kernel(info_ref, own_x, own_y, from_y, from_x, small_ref, left_ref, right_ref):
+    rows, cols = own_x.shape
     small = small_ref[...]
     high = small.astype(bf16)
-    out_ref[rows : rows + TAIL, :] = jnp.concatenate([high, (small - high.astype(f32)).astype(bf16)], axis=0)
-
-
-def unpack_kernel(info_ref, h0, h1, h2, h3, t0, t1, t2, t3, gq_ref, gk_ref, gv_ref, go_ref, small_ref):
+    tail = jnp.concatenate([high, (small - high.astype(f32)).astype(bf16)], axis=0)
+    for a, b, out_ref, first in ((own_x, from_y, left_ref, 0), (own_y, from_x, right_ref, cols)):
+        out_ref[0:rows, :] = (a[...].astype(f32) + b[...].astype(f32)).astype(bf16)
+        out_ref[rows : rows + TAIL, :] = tail[:, first : first + cols]
+
+
+def unpack_kernel(info_ref, *refs):
     q, core = info_ref[2], info_ref[3]
-    qw, kw = gq_ref.shape[1], gk_ref.shape[1]
+    gq_ref, gk_ref, gv_ref, go_ref, ag_ref, fg_ref, qg_ref, kg_ref, rms_ref, small_ref = refs[8:]
+    cols, kw = gq_ref.shape[1], gk_ref.shape[1]
     upper, lower = gq_ref.shape[0] // 8, go_ref.shape[0] // 8
-    small = jnp.zeros(small_ref.shape, f32)
-    for refs, half in (((h0, h1, h2, h3), core), ((t0, t1, t2, t3), 1 - core)):
-        for k, ref in enumerate(refs):
+    for half, (lefts, lefts_x, rights, rights_y) in ((core, refs[0:4]), (1 - core, refs[4:8])):
+        for k in range(4):
             block = half * 4 + jnp.bitwise_xor(q, k)
+            left, i = (lefts if k in (0, 2) else lefts_x), (0 if k in (0, 1) else 1)
+            right, j = (rights if k in (0, 1) else rights_y), (0 if k in (0, 2) else 1)
             rows = pl.ds(pl.multiple_of(block * upper, upper), upper)
-            gq_ref[rows, :] = ref[0:upper, 0:qw].astype(f32)
-            gk_ref[rows, :] = ref[0:upper, qw : qw + kw].astype(f32)
-            gv_ref[rows, :] = ref[0:upper, qw + kw : qw + 2 * kw].astype(f32)
+            gq_ref[rows, :] = left[i, 0:upper, :].astype(f32)
+            gk_ref[rows, :] = right[j, 0:upper, 0:kw].astype(f32)
+            gv_ref[rows, :] = right[j, 0:upper, kw : 2 * kw].astype(f32)
             rows = pl.ds(pl.multiple_of(block * lower, lower), lower)
-            go_ref[rows, :] = ref[upper : upper + lower, :].astype(f32)
-            tail = ref[upper + lower : upper + lower + TAIL, :].astype(f32)
-            small = small + (tail[0:8] + tail[8:16])
-    small_ref[...] = small
+            go_ref[rows, 0:cols] = left[i, upper : upper + lower, :].astype(f32)
+            go_ref[rows, cols : 2 * cols] = right[j, upper : upper + lower, :].astype(f32)
+    for first, group in ((0, (0, 1, 4, 5)), (cols, (2, 3, 6, 7))):
+        total = jnp.zeros((8, cols), f32)
+        for n in group:
+            for i in range(2):
+                tail = refs[n][i, upper + lower : upper + lower + TAIL, :].astype(f32)
+                total = total + (tail[0:8] + tail[8:16])
+        small_ref[:, first : first + cols] = total
+    shard, hd = ag_ref.shape[1], qg_ref.shape[1]
+    mine = pl.ds(pl.multiple_of(info_ref[1] * shard, shard), shard)
+    ag_ref[...] = small_ref[0:1, mine]
+    fg_ref[...] = small_ref[1:2, mine]
+    qg_ref[...] = small_ref[2:3, 0:hd]
+    kg_ref[...] = small_ref[2:3, hd : 2 * hd]
+    totals = small_ref[2:3, 2 * hd : 2 * hd + 128]
+    lane = lax.broadcasted_iota(jnp.int32, (1, 128), 1)
+    count = jnp.sum(jnp.where(lane == 3, totals, 0.0), axis=1, keepdims=True)
+    rms_ref[...] = jnp.sqrt(totals / count)
 
 
 SPECS = {
@@ -661,21 +671,21 @@
     return lax.ppermute(values, "dp", [(i, i ^ bit) for i in range(8)])
 
 
-def to_chips(keep, other, info):
-    rows, width = keep.shape[1:]
-    blocks = call(
-        chip_blocks_kernel,
-        [((rows, width), bf16, "v")] * 4,
-        (("s", info), ("a", keep), ("v", other)),
-        scratch=[((4, rows, width), bf16)],
-        sems=(1,),
-        bytes_accessed=12 * rows * width,
-    )
-    return [blocks[0]] + [swap(blocks[k], 2 * k) for k in (1, 2, 3)]
-
-
-def from_chips(own):
-    return [own] + [swap(own, 2 * k) for k in (1, 2, 3)]
+def halve(keep, other, info):
+    _, rows, width = keep.shape
+    return call(
+        halves_kernel,
+        [((2, rows, width // 2), bf16, "v")] * 4,
+        (("s", info), ("a", keep, other)),
+        scratch=[((4, rows, width), bf16)] * 2,
+        sems=(2,),
+    )
+
+
+def halve_again(keep_x, keep_y, got_x, got_y, info):
+    return call(
+        halve_kernel, [(keep_x.shape[1:], bf16, "v")] * 4, (("s", info), ("v", keep_x, keep_y, got_x, got_y))
+    )
 
 
 def per_device(
@@ -727,16 +737,18 @@
         ),
         scratch=weights[:1] + tables + weights[1:] + saved,
         sems=(6, 10),
-        limit=VMEM_BYTES,
+        limit=FULL_BYTES,
         flops=2 * seq_len * width * (2 * qw + 2 * kw) + 4 * seq_len * seq_len * qw,
         bytes_accessed=14_000_000,
     )
     attn_parts, cot_mid, cot_pair, cot_last = hold(attn_parts, cot_mid, cot_pair, cot_last)
     across, far, pair, own = attn_parts
-    two, three = send(far, INWARD_TWO), send(far, MIDDLE)
-    one = send(pick(end, across, cot_mid[:seq_len]), PAIRS)
+    two = send(far, INWARD_TWO)
+    one, three = hold(pick(end, across, cot_mid[:seq_len]), far)
+    three, one = send(three, MIDDLE), send(one, PAIRS)
     zero_end = pick(end, jnp.zeros_like(one), one)
-    attn_local = total(scatter_last(attn_parts, (two, three, zero_end)))
+    pair = lax.optimization_barrier(pair.astype(f32) + two.astype(f32))
+    attn_local = total(scatter_last((across, far, pair, own), (jnp.zeros_like(two), three, zero_end)))
     middle = resid + attn_local
     shard_two, one = hold(middle.astype(bf16), one)
     m_parts = gather_line(shard_two)
@@ -765,6 +777,7 @@
         (("s", info), ("a", n2, dgu, hid, cotm, w_down)),
         scratch=[kept[0], kept[3], kept[2], kept[1], ((hidden, width), bf16), ((8, width // 8, 3 * hidden), bf16)],
         sems=(5, 2),
+        limit=VMEM_BYTES,
         flops=2 * seq_len * width * hidden * 4,
         bytes_accessed=14_000_000,
     )
@@ -773,25 +786,16 @@
     if chips:
         ffn_other = swap(ffn_give, 1)
         cols = (width // 8, 3 * hidden // 2)
-        to_x, to_y, keep_x, keep_y = call(
-            halves_kernel,
-            [((2, *cols), bf16, "v")] * 4,
-            (("s", info), ("a", ffn_keep, ffn_other)),
-            scratch=[((4, width // 8, 3 * hidden), bf16)] * 2,
-            sems=(2,),
-        )
+        to_x, to_y, keep_x, keep_y = halve(ffn_keep, ffn_other, info)
         back, to_x, to_y, keep_x, keep_y = hold(back, to_x, to_y, keep_x, keep_y)
     grad_middle = grad_top + total(back)
+    ga = grad_middle.astype(bf16)
     across, far, pair, own = down_parts
-    ga = grad_middle.astype(bf16)
     ga_pair, ga_mid = send(ga, PAIRS), send(ga, MIDDLE)
     if chips:
         got_x, got_y = swap(to_x, 2), swap(to_y, 4)
-    if chips:
         ga_pair, ga_mid, far, got_x, got_y = hold(ga_pair, ga_mid, far, got_x, got_y)
-        to_y, to_x, own_x, own_y = call(
-            halve_kernel, [(cols, bf16, "v")] * 4, (("s", info), ("v", keep_x, keep_y, got_x, got_y))
-        )
+        to_y, to_x, own_x, own_y = halve_again(keep_x, keep_y, got_x, got_y, info)
         from_y, from_x = swap(to_y, 4), swap(to_x, 2)
     ga_end, ga_far = send(pick(end, far, ga_mid), PAIRS), send(ga_pair, MIDDLE)
     if chips:
@@ -826,9 +830,10 @@
         flops=2 * seq_len * width * (4 * qw + 4 * kw) + 10 * seq_len * seq_len * qw,
         bytes_accessed=20_000_000,
     )
+    across, far, pair, own = back_parts
     if chips:
-        back_parts, ffn_terms, keep, give, lefts_x, rights_y = hold(back_parts, ffn_terms, keep, give, lefts_x, rights_y)
-        blocks = to_chips(keep, swap(give, 1), info)
+        far, ffn_terms, keep, give, lefts_x, rights_y = hold(far, ffn_terms, keep, give, lefts_x, rights_y)
+        other = swap(give, 1)
     out_rows, sums = call(
         output_kernel,
         [((seq_len, shard), bf16, "v"), ((8, shard), f32, "v")],
@@ -838,6 +843,24 @@
     small = call(small_kernel, [((8, width), f32, "v")], (("s", info), ("v", gag, gfg, qgg, kgg, sums)))[0]
     shapes = [(width, qw), (width, kw), (width, kw), (qw, width)]
     if chips:
+        other, small = hold(other, small)
+        to_x, to_y, keep_x, keep_y = halve(keep, other, info)
+        got_x, got_y = swap(to_x, 2), swap(to_y, 4)
+        small = small + send(small, PAIRS)
+        small = small + send(small, ((0, 2), (2, 0), (1, 3), (3, 1)))
+        got_x, got_y, small, far, across = hold(got_x, got_y, small, far, across)
+        to_y, to_x, own_x, own_y = halve_again(keep_x, keep_y, got_x, got_y, info)
+        from_y, from_x, two = hold(swap(to_y, 4), swap(to_x, 2), send(far, INWARD_TWO))
+        late_left, late_right = call(
+            block_kernel,
+            [((own_x.shape[0] + TAIL, own_x.shape[1]), bf16, "v")] * 2,
+            (("s", info), ("v", own_x, own_y, from_y, from_x, small)),
+        )
+        late_left, late_right, far, across = hold(late_left, late_right, far, across)
+        three, one = send(far, MIDDLE), send(across, INWARD)
+        left_y, right_x, three, one = hold(swap(late_left, 4), swap(late_right, 2), three, one)
+        late_lefts, late_rights = jnp.stack([late_left, left_y]), jnp.stack([late_right, right_x])
+        back_terms = scatter_last((across, far, pair, own), (two, three, one))
         ffn_halves = (lefts, lefts_x, rights, rights_y)
         g_gate, g_up, g_down = call(
             unpack_ffn_kernel,
@@ -845,28 +868,24 @@
             (("s", info), ("v", *ffn_halves, *[swap(b, 1) for b in ffn_halves])),
             bytes_accessed=14_000_000,
         )
-        small = small + send(small, PAIRS)
-        small = small + send(small, ((0, 2), (2, 0), (1, 3), (3, 1)))
-        small, back_parts = hold(small, back_parts)
-        blocks, small, g_gate, g_up, g_down = hold(blocks, small, g_gate, g_up, g_down)
-        own = call(
-            block_kernel,
-            [((blocks[0].shape[0] + TAIL, width), bf16, "v")],
-            (("s", info), ("v", *blocks, small)),
-            bytes_accessed=2_000_000,
-        )[0]
-        everyone = from_chips(own)
-        back_terms = scatter_last(back_parts, scatter_first(back_parts))
-        gq, gk, gv, go, small = call(
+        late = (late_lefts, swap(late_lefts, 2), late_rights, swap(late_rights, 4))
+        late, back_terms, g_gate, g_up, g_down = hold(late, back_terms, g_gate, g_up, g_down)
+        everyone = [*late, *[swap(b, 1) for b in late]]
+        gq, gk, gv, go, ag, fg, qgg, kgg, rms = call(
             unpack_kernel,
-            [(s, f32, "v") for s in shapes] + [((8, width), f32, "v")],
-            (("s", info), ("v", *everyone, *[swap(b, 1) for b in everyone])),
+            [(s, f32, "v") for s in shapes + [(1, shard), (1, shard), (1, hd), (1, hd), (1, 128)]],
+            (("s", info), ("v", *everyone)),
+            scratch=[((8, width), f32)],
             bytes_accessed=9_000_000,
         )
     else:
         back_terms = scatter_last(back_parts, scatter_first(back_parts))
         grads, ffn_grads = lax.psum((jnp.concatenate([keep, give]), jnp.concatenate([ffn_keep, ffn_give])), "dp")
         small = lax.psum(small, ("dp", "tensor"))
+        ag, fg = [lax.dynamic_slice(small, (i, z * shard), (1, shard)) for i in (0, 1)]
+        qgg, kgg = small[2:3, :hd], small[2:3, hd : 2 * hd]
+        totals = small[2:3, 2 * hd : 2 * hd + 4]
+        rms = jnp.sqrt(totals / totals[:, 3:])
         g_qkv = grads[:, : width // 8].reshape(width, width).astype(f32)
         gq, gk, gv = g_qkv[:, :qw], g_qkv[:, qw : qw + kw], g_qkv[:, qw + kw :]
         go = grads[:, width // 8 :].reshape(qw, width).astype(f32)
@@ -877,9 +896,6 @@
         tail = folded[:, lower:].reshape(8, width // 8 - lower, -1, 256).transpose(0, 2, 1, 3).reshape(8, lower, 256)
         g_down = jnp.concatenate([folded[:, :lower], tail], axis=2).reshape(hidden, width).astype(f32)
     input_grad = (grad_middle + total(back_terms)).astype(bf16)
-    grad_attn_gain = lax.dynamic_slice(small[0], (z * shard,), (shard,))
-    grad_ffn_gain = lax.dynamic_slice(small[1], (z * shard,), (shard,))
-    totals = small[2, 2 * hd : 2 * hd + 4]
     return (
         out_rows,
         input_grad,
@@ -887,14 +903,14 @@
         gk,
         gv,
         go,
-        grad_attn_gain,
-        grad_ffn_gain,
-        small[2, :hd],
-        small[2, hd : 2 * hd],
+        ag[0],
+        fg[0],
+        qgg[0],
+        kgg[0],
         g_gate,
         g_up,
         g_down,
-        jnp.sqrt(totals[:3] / totals[3]),
+        rms[0, :3],
     )
 
 

time: 325 us -> 304 us (0.935)
  the two profiles are of different devices: /device:TPU:9 before, /device:TPU:0 now
where the time goes in v3:
time: 304 us; the launch traced here: 299 us
  waiting for transfers between devices  117 us (38%)
  starting transfers between devices  90.3 us (30%)
  Pallas kernels  72 us (24%)
  other arithmetic  10.6 us (3%)
  local copies, waits for them, and re-layouts  6.33 us (2%)
    ppermute x39, waiting for transfers between devices, send(): return lax.ppermute(rows, 'tensor', pairs)  85.2 us
    ppermute x39, starting transfers between devices, send(): return lax.ppermute(rows, 'tensor', pairs)  73.8 us
    pallas_call x14, Pallas kernels, call(): pl.pallas_call(body, out_shape=[jax.ShapeDtypeStruct(s, d) for s, d, _ in...  72 us
    ppermute x26, waiting for transfers between devices, swap(): return lax.ppermute(values, 'dp', [(i, i ^ bit) for i in range(8)])  32.1 us
    ppermute x26, starting transfers between devices, swap(): return lax.ppermute(values, 'dp', [(i, i ^ bit) for i in range(8)])  16.5 us
  transfers between devices with their start and end apart: 65, of which 31 were waited for; matrix products, arithmetic and copies ran while one was open for 3% of the time, Pallas kernels for 19%

profile of v3, /device:TPU:0, one launch (start us, length us, event | category | flops | bytes accessed | tf_op | source)
XLA Modules:
  0.0 299.0 jit_solution(16772815074530879857)
XLA Ops:
  8.1 6.9 %collective-permute-done.x1 = bf16[720,256]{1,0:T(8,128)(2,1)S(1)} collective-permute-done((bf16[720,256]{1,0:T(8,128)(2,1)S(1)}, bf16[720,256]{1,0:T(8,128)(2,1)S(1)}, u32[]{:S(2)}, u32[]{:S(2)}) %collective-permute-start) | collective-permute-done | bytes 368672 | tf_op jit(solution)/shard_map/ppermute | solution.py:622
  15.0 4.8 %collective-permute-start.2 = (bf16[720,256]{1,0:T(8,128)(2,1)S(1)}, bf16[720,256]{1,0:T(8,128)(2,1)S(1)}, u32[]{:S(2)}, u32[]{:S(2)}) collective-permute-start(bf16[720,256]{1,0:T(8,128)(2,1)S(1)} %broadcast_select_fusion), channel_id=1, source_target_pairs={{0,1},{1,0},{2,3},{3,2},{4,5},{5,4},{6,7},{7,6},{8,9},{9,8},{10,11... | collective-permute-start | bytes 1105928 | tf_op jit(solution)/shard_map/ppermute | solution.py:622
  21.2 6.4 %collective-permute-done.2.x3.c1 = bf16[720,256]{1,0:T(8,128)(2,1)S(1)} collective-permute-done((bf16[720,256]{1,0:T(8,128)(2,1)S(1)}, bf16[720,256]{1,0:T(8,128)(2,1)S(1)}, u32[]{:S(2)}, u32[]{:S(2)}) %collective-permute-start.2) | collective-permute-done | bytes 368672 | tf_op jit(solution)/shard_map/ppermute | solution.py:622
  32.0 7.2 %collective-permute-done.4.x5 = bf16[720,256]{1,0:T(8,128)(2,1)S(1)} collective-permute-done((bf16[720,256]{1,0:T(8,128)(2,1)S(1)}, bf16[720,256]{1,0:T(8,128)(2,1)S(1)}, u32[]{:S(2)}, u32[]{:S(2)}) %collective-permute-start.4) | collective-permute-done | bytes 368672 | tf_op jit(solution)/shard_map/ppermute | solution.py:622
  43.9 12.2 %shard_map.245 = (bf16[704,256]{1,0:T(8,128)(2,1)}, bf16[704,256]{1,0:T(8,128)(2,1)}, bf16[704,256]{1,0:T(8,128)(2,1)}, bf16[704,256]{1,0:T(8,128)(2,1)}, bf16[7...) custom-call(s32[4]{0:T(128)} %pad_add_fusion.info_ref, ...), custom_call_target="tpu_custom_call" | custom-call | flops 3229614080 | bytes 14000000 | tf_op jit(solution)/shard_map/pallas_call | solution.py:602
  65.8 6.8 %collective-permute-done.9 = bf16[704,256]{1,0:T(8,128)(2,1)S(1)} collective-permute-done((bf16[704,256]{1,0:T(8,128)(2,1)}, bf16[704,256]{1,0:T(8,128)(2,1)S(1)}, u32[]{:S(2)}, u32[]{:S(2)}) %collective-permute-start.9) | collective-permute-done | bytes 360480 | tf_op jit(solution)/shard_map/ppermute | solution.py:622
  73.8 5.4 %collective-permute-start.11 = (bf16[704,256]{1,0:T(8,128)(2,1)S(1)}, bf16[704,256]{1,0:T(8,128)(2,1)S(1)}, u32[]{:S(2)}, u32[]{:S(2)}) collective-permute-start(bf16[704,256]{1,0:T(8,128)(2,1)S(1)} %add_convert_fusion.9), channel_id=1, source_target_pairs={{0,1},{1,0},{2,3},{3,2},{4,5},{5,4},{6,7},{7,6},{8,9},{9,8},{10,11... | collective-permute-start | bytes 1081352 | tf_op jit(solution)/shard_map/ppermute | solution.py:622
  80.1 6.7 %collective-permute-done.11 = bf16[704,256]{1,0:T(8,128)(2,1)S(1)} collective-permute-done((bf16[704,256]{1,0:T(8,128)(2,1)S(1)}, bf16[704,256]{1,0:T(8,128)(2,1)S(1)}, u32[]{:S(2)}, u32[]{:S(2)}) %collective-permute-start.11) | collective-permute-done | bytes 360480 | tf_op jit(solution)/shard_map/ppermute | solution.py:622
  87.8 6.9 %collective-permute-start.14 = (bf16[704,256]{1,0:T(8,128)(2,1)S(1)}, bf16[704,256]{1,0:T(8,128)(2,1)S(1)}, u32[]{:S(2)}, u32[]{:S(2)}) collective-permute-start(bf16[704,256]{1,0:T(8,128)(2,1)S(1)} %get-tuple-element.190.m0), channel_id=1, source_target_pairs={{0,1},{1,0},{2,3},{3,2},{4,5},{5,4},{6,7},{7,6},{8,9},{9,8},{10,11... | collective-permute-start | bytes 1081352 | tf_op jit(solution)/shard_map/ppermute | solution.py:622
  96.0 5.7 %collective-permute-done.14.m1 = bf16[704,256]{1,0:T(8,128)(2,1)S(1)} collective-permute-done((bf16[704,256]{1,0:T(8,128)(2,1)S(1)}, bf16[704,256]{1,0:T(8,128)(2,1)S(1)}, u32[]{:S(2)}, u32[]{:S(2)}) %collective-permute-start.14) | collective-permute-done | bytes 360480 | tf_op jit(solution)/shard_map/ppermute | solution.py:622
  103.7 6.1 %collective-permute-done.16.m3 = bf16[704,256]{1,0:T(8,128)(2,1)S(1)} collective-permute-done((bf16[704,256]{1,0:T(8,128)(2,1)S(1)}, bf16[704,256]{1,0:T(8,128)(2,1)S(1)}, u32[]{:S(2)}, u32[]{:S(2)}) %collective-permute-start.16) | collective-permute-done | bytes 360480 | tf_op jit(solution)/shard_map/ppermute | solution.py:622
  109.9 10.2 %collective-permute-done.18.m5 = bf16[704,256]{1,0:T(8,128)(2,1)S(1)} collective-permute-done((bf16[704,256]{1,0:T(8,128)(2,1)S(1)}, bf16[704,256]{1,0:T(8,128)(2,1)S(1)}, u32[]{:S(2)}, u32[]{:S(2)}) %collective-permute-start.18) | collective-permute-done | bytes 360480 | tf_op jit(solution)/shard_map/ppermute | solution.py:622
  120.1 10.3 %shard_map.246 = (bf16[704,256]{1,0:T(8,128)(2,1)S(1)}, bf16[704,256]{1,0:T(8,128)(2,1)S(1)}, bf16[704,256]{1,0:T(8,128)(2,1)S(1)}, bf16[704,256]{1,0:T(8,128)(2...) custom-call(s32[4]{0:T(128)S(1)} %copy-done.3, ...), custom_call_target="tpu_custom_call" | custom-call | flops 5536481280 | bytes 16000000 | tf_op jit(solution)/shard_map/pallas_call | solution.py:602
  139.5 7.4 %shard_map.247 = (bf16[704,256]{1,0:T(8,128)(2,1)S(1)}, bf16[704,256]{1,0:T(8,128)(2,1)S(1)}, bf16[704,256]{1,0:T(8,128)(2,1)S(1)}, bf16[704,256]{1,0:T(8,128)(2...) custom-call(s32[4]{0:T(128)S(1)} %copy-done.3, ...), custom_call_target="tpu_custom_call" | custom-call | flops 4429185024 | bytes 14000000 | tf_op jit(solution)/shard_map/pallas_call | solution.py:602
  153.2 7.3 %collective-permute-done.22 = bf16[704,256]{1,0:T(8,128)(2,1)S(1)} collective-permute-done((bf16[704,256]{1,0:T(8,128)(2,1)S(1)}, bf16[704,256]{1,0:T(8,128)(2,1)S(1)}, u32[]{:S(2)}, u32[]{:S(2)}) %collective-permute-start.22) | collective-permute-done | bytes 360480 | tf_op jit(solution)/shard_map/ppermute | solution.py:622
  166.2 7.1 %collective-permute-done.25.g1 = bf16[704,256]{1,0:T(8,128)(2,1)S(1)} collective-permute-done((bf16[704,256]{1,0:T(8,128)(2,1)S(1)}, bf16[704,256]{1,0:T(8,128)(2,1)S(1)}, u32[]{:S(2)}, u32[]{:S(2)}) %collective-permute-start.25) | collective-permute-done | bytes 360480 | tf_op jit(solution)/shard_map/ppermute | solution.py:622
  181.9 4.8 %collective-permute-done.31.from_y = bf16[128,1152]{1,0:T(8,128)(2,1)S(1)} collective-permute-done((bf16[128,1152]{1,0:T(8,128)(2,1)S(1)}, bf16[128,1152]{1,0:T(8,128)(2,1)S(1)}, u32[]{:S(2)}, u32[]{:S(2)}) %collective-permute-start.31) | collective-permute-done | bytes 294944 | tf_op jit(solution)/shard_map/ppermute | solution.py:671
  189.1 5.1 %collective-permute-start.33 = (bf16[704,256]{1,0:T(8,128)(2,1)S(1)}, bf16[704,256]{1,0:T(8,128)(2,1)S(1)}, u32[]{:S(2)}, u32[]{:S(2)}) collective-permute-start(bf16[704,256]{1,0:T(8,128)(2,1)S(1)} %broadcast_select_fusion.1), channel_id=1, source_target_pairs={{0,1},{1,0},{2,3},{3,2},{4,5},{5,4},{6,7},{7,6},{8,9},{9,8},{10,11... | collective-permute-start | bytes 1081352 | tf_op jit(solution)/shard_map/ppermute | solution.py:622
  196.0 7.0 %collective-permute-done.35 = bf16[128,1152]{1,0:T(8,128)(2,1)S(1)} collective-permute-done((bf16[128,1152]{1,0:T(8,128)(2,1)S(1)}, bf16[128,1152]{1,0:T(8,128)(2,1)S(1)}, u32[]{:S(2)}, u32[]{:S(2)}) %collective-permute-start.35) | collective-permute-done | bytes 294944 | tf_op jit(solution)/shard_map/ppermute | solution.py:671
  209.8 26.1 %shard_map.251 = (bf16[704,256]{1,0:T(8,128)(2,1)S(1)}, bf16[704,256]{1,0:T(8,128)(2,1)S(1)}, bf16[704,256]{1,0:T(8,128)(2,1)S(1)}, bf16[704,256]{1,0:T(8,128)(2...) custom-call(s32[4]{0:T(128)S(1)} %copy-done.3, ...), custom_call_target="tpu_custom_call" | custom-call | flops 6966738944 | bytes 20000000 | tf_op jit(solution)/shard_map/pallas_call | solution.py:602
  257.2 4.8 %collective-permute-done.46.from_y = bf16[192,512]{1,0:T(8,128)(2,1)S(1)} collective-permute-done((bf16[192,512]{1,0:T(8,128)(2,1)S(1)}, bf16[192,512]{1,0:T(8,128)(2,1)S(1)}, u32[]{:S(2)}, u32[]{:S(2)}) %collective-permute-start.46) | collective-permute-done | bytes 196640 | tf_op jit(solution)/shard_map/ppermute | solution.py:671
  263.6 7.1 %collective-permute-start.52 = (bf16[704,256]{1,0:T(8,128)(2,1)S(1)}, bf16[704,256]{1,0:T(8,128)(2,1)S(1)}, u32[]{:S(2)}, u32[]{:S(2)}) collective-permute-start(bf16[704,256]{1,0:T(8,128)(2,1)S(1)} %get-tuple-element.292), channel_id=1, source_target_pairs={{0,1},{3,2},{4,5},{7,6},{8,9},{11,10},{12,13},{15,14},{16,17},{19,... | collective-permute-start | bytes 1081352 | tf_op jit(solution)/shard_map/ppermute | solution.py:622
  272.0 4.7 %collective-permute-done.49 = bf16[208,512]{1,0:T(8,128)(2,1)S(1)} collective-permute-done((bf16[208,512]{1,0:T(8,128)(2,1)S(1)}, bf16[208,512]{1,0:T(8,128)(2,1)S(1)}, u32[]{:S(2)}, u32[]{:S(2)}) %collective-permute-start.49) | collective-permute-done | bytes 213024 | tf_op jit(solution)/shard_map/ppermute | solution.py:671
  283.7 4.9 %shard_map.257 = (f32[1024,768]{1,0:T(8,128)}, f32[1024,768]{1,0:T(8,128)}, f32[768,1024]{1,0:T(8,128)}) custom-call(s32[4]{0:T(128)S(1)} %copy-done.3, bf16[2,128,1152]{2,1,0:T(8,128)(2,1)S(1)} %pad_maximum_fusion.refs_0_, bf16[2,128,1152]{2,1,0:T(8,128)(2,1)S(1)} %collective-permute-done.39.refs_1_, bf16[2,128,1152]{2,1,0:T(8,128)(2,1)S(1)} %pad_maximum_fusion.1.refs_2_, ...), custom_call_target="tpu_custom_call" | custom-call | bytes 14000000 | tf_op jit(solution)/shard_map/pallas_call | solution.py:602
  (229 shorter events, 114.8 us)
Async XLA Ops:
  15.0 12.5 %collective-permute-start.2 = (bf16[720,256]{1,0:T(8,128)(2,1)S(1)}, bf16[720,256]{1,0:T(8,128)(2,1)S(1)}, u32[]{:S(2)}, u32[]{:S(2)}) collective-permute-start(bf16[720,256]{1,0:T(8,128)(2,1)S(1)} %broadcast_select_fusion), channel_id=1, source_target_pairs={{0,1},{1,0},{2,3},{3,2},{4,5},{5,4},{6,7},{7,6},{8,9},{9,8},{10,11... | collective-permute-start | bytes 1105928 | tf_op jit(solution)/shard_map/ppermute | solution.py:622
  40.0 16.1 %collective-permute-start.6 = (bf16[720,256]{1,0:T(8,128)(2,1)S(1)}, bf16[720,256]{1,0:T(8,128)(2,1)S(1)}, u32[]{:S(2)}, u32[]{:S(2)}) collective-permute-start(bf16[720,256]{1,0:T(8,128)(2,1)S(1)} %concatenate.17.c0), channel_id=1, source_target_pairs={{1,2},{2,1},{5,6},{6,5},{9,10},{10,9},{13,14},{14,13},{17,18},{18,... | collective-permute-start | bytes 1105928 | tf_op jit(solution)/shard_map/ppermute | solution.py:622
  40.7 15.8 %collective-permute-start.7 = (bf16[720,256]{1,0:T(8,128)(2,1)S(1)}, bf16[720,256]{1,0:T(8,128)(2,1)S(1)}, u32[]{:S(2)}, u32[]{:S(2)}) collective-permute-start(bf16[720,256]{1,0:T(8,128)(2,1)S(1)} %concatenate.17.c0), channel_id=1, source_target_pairs={{1,0},{2,3},{5,4},{6,7},{9,8},{10,11},{13,12},{14,15},{17,16},{18,... | collective-permute-start | bytes 1105928 | tf_op jit(solution)/shard_map/ppermute | solution.py:622
  42.0 18.4 %collective-permute-start.8 = (bf16[720,256]{1,0:T(8,128)(2,1)S(1)}, bf16[720,256]{1,0:T(8,128)(2,1)S(1)}, u32[]{:S(2)}, u32[]{:S(2)}) collective-permute-start(bf16[720,256]{1,0:T(8,128)(2,1)S(1)} %collective-permute-done.5.c5), channel_id=1, source_target_pairs={{1,0},{2,3},{5,4},{6,7},{9,8},{10,11},{13,12},{14,15},{17,16},{18,... | collective-permute-start | bytes 1105928 | tf_op jit(solution)/shard_map/ppermute | solution.py:622
  65.6 13.6 %collective-permute-start.12 = (bf16[704,256]{1,0:T(8,128)(2,1)S(1)}, bf16[704,256]{1,0:T(8,128)(2,1)S(1)}, u32[]{:S(2)}, u32[]{:S(2)}) collective-permute-start(bf16[704,256]{1,0:T(8,128)(2,1)S(1)} %slice_select_fusion), channel_id=1, source_target_pairs={{0,1},{1,0},{2,3},{3,2},{4,5},{5,4},{6,7},{7,6},{8,9},{9,8},{10,11... | collective-permute-start | bytes 1081352 | tf_op jit(solution)/shard_map/ppermute | solution.py:622
  73.8 13.1 %collective-permute-start.11 = (bf16[704,256]{1,0:T(8,128)(2,1)S(1)}, bf16[704,256]{1,0:T(8,128)(2,1)S(1)}, u32[]{:S(2)}, u32[]{:S(2)}) collective-permute-start(bf16[704,256]{1,0:T(8,128)(2,1)S(1)} %add_convert_fusion.9), channel_id=1, source_target_pairs={{0,1},{1,0},{2,3},{3,2},{4,5},{5,4},{6,7},{7,6},{8,9},{9,8},{10,11... | collective-permute-start | bytes 1081352 | tf_op jit(solution)/shard_map/ppermute | solution.py:622
  87.8 14.0 %collective-permute-start.14 = (bf16[704,256]{1,0:T(8,128)(2,1)S(1)}, bf16[704,256]{1,0:T(8,128)(2,1)S(1)}, u32[]{:S(2)}, u32[]{:S(2)}) collective-permute-start(bf16[704,256]{1,0:T(8,128)(2,1)S(1)} %get-tuple-element.190.m0), channel_id=1, source_target_pairs={{0,1},{1,0},{2,3},{3,2},{4,5},{5,4},{6,7},{7,6},{8,9},{9,8},{10,11... | collective-permute-start | bytes 1081352 | tf_op jit(solution)/shard_map/ppermute | solution.py:622
  94.7 15.1 %collective-permute-start.16 = (bf16[704,256]{1,0:T(8,128)(2,1)S(1)}, bf16[704,256]{1,0:T(8,128)(2,1)S(1)}, u32[]{:S(2)}, u32[]{:S(2)}) collective-permute-start(bf16[704,256]{1,0:T(8,128)(2,1)S(1)} %collective-permute-done.15.m2), channel_id=1, source_target_pairs={{1,0},{2,3},{5,4},{6,7},{9,8},{10,11},{13,12},{14,15},{17,16},{18,... | collective-permute-start | bytes 1081352 | tf_op jit(solution)/shard_map/ppermute | solution.py:622
  102.4 17.6 %collective-permute-start.18 = (bf16[704,256]{1,0:T(8,128)(2,1)S(1)}, bf16[704,256]{1,0:T(8,128)(2,1)S(1)}, u32[]{:S(2)}, u32[]{:S(2)}) collective-permute-start(bf16[704,256]{1,0:T(8,128)(2,1)S(1)} %collective-permute-done.14.m1), channel_id=1, source_target_pairs={{2,0},{1,3},{6,4},{5,7},{10,8},{9,11},{14,12},{13,15},{18,16},{17,... | collective-permute-start | bytes 1081352 | tf_op jit(solution)/shard_map/ppermute | solution.py:622
  131.4 15.5 %collective-permute-start.19 = (bf16[704,256]{1,0:T(8,128)(2,1)S(1)}, bf16[704,256]{1,0:T(8,128)(2,1)S(1)}, u32[]{:S(2)}, u32[]{:S(2)}) collective-permute-start(bf16[704,256]{1,0:T(8,128)(2,1)S(1)} %get-tuple-element.197), channel_id=1, source_target_pairs={{0,2},{3,1},{4,6},{7,5},{8,10},{11,9},{12,14},{15,13},{16,18},{19,... | collective-permute-start | bytes 1081352 | tf_op jit(solution)/shard_map/ppermute | solution.py:622
  132.9 14.0 %collective-permute-start.20 = (bf16[704,256]{1,0:T(8,128)(2,1)S(1)}, bf16[704,256]{1,0:T(8,128)(2,1)S(1)}, u32[]{:S(2)}, u32[]{:S(2)}) collective-permute-start(bf16[704,256]{1,0:T(8,128)(2,1)S(1)} %get-tuple-element.197), channel_id=1, source_target_pairs={{1,2},{2,1},{5,6},{6,5},{9,10},{10,9},{13,14},{14,13},{17,18},{18,... | collective-permute-start | bytes 1081352 | tf_op jit(solution)/shard_map/ppermute | solution.py:622
  133.6 13.3 %collective-permute-start.21 = (bf16[704,256]{1,0:T(8,128)(2,1)S(1)}, bf16[704,256]{1,0:T(8,128)(2,1)S(1)}, u32[]{:S(2)}, u32[]{:S(2)}) collective-permute-start(bf16[704,256]{1,0:T(8,128)(2,1)S(1)} %get-tuple-element.198), channel_id=1, source_target_pairs={{0,1},{3,2},{4,5},{7,6},{8,9},{11,10},{12,13},{15,14},{16,17},{19,... | collective-permute-start | bytes 1081352 | tf_op jit(solution)/shard_map/ppermute | solution.py:622
  148.0 12.6 %collective-permute-start.22 = (bf16[704,256]{1,0:T(8,128)(2,1)S(1)}, bf16[704,256]{1,0:T(8,128)(2,1)S(1)}, u32[]{:S(2)}, u32[]{:S(2)}) collective-permute-start(bf16[704,256]{1,0:T(8,128)(2,1)S(1)} %add_convert_fusion.7), channel_id=1, source_target_pairs={{0,1},{1,0},{2,3},{3,2},{4,5},{5,4},{6,7},{7,6},{8,9},{9,8},{10,11... | collective-permute-start | bytes 1081352 | tf_op jit(solution)/shard_map/ppermute | solution.py:622
  160.5 15.0 %collective-permute-start.27 = (bf16[2,128,1152]{2,1,0:T(8,128)(2,1)S(1)}, bf16[2,128,1152]{2,1,0:T(8,128)(2,1)S(1)}, u32[]{:S(2)}, u32[]{:S(2)}) collective-permute-start(bf16[2,128,1152]{2,1,0:T(8,128)(2,1)S(1)} %get-tuple-element.218), channel_id=1, source_target_pairs={{0,8},{4,12},{8,0},{12,4},{16,24},{20,28},{24,16},{28,20},{1,9},{5... | collective-permute-start | bytes 1769480 | tf_op jit(solution)/shard_map/ppermute | solution.py:671
  162.0 14.7 %collective-permute-start.28 = (bf16[2,128,1152]{2,1,0:T(8,128)(2,1)S(1)}, bf16[2,128,1152]{2,1,0:T(8,128)(2,1)S(1)}, u32[]{:S(2)}, u32[]{:S(2)}) collective-permute-start(bf16[2,128,1152]{2,1,0:T(8,128)(2,1)S(1)} %get-tuple-element.219), channel_id=1, source_target_pairs={{0,16},{4,20},{8,24},{12,28},{16,0},{20,4},{24,8},{28,12},{1,17},{... | collective-permute-start | bytes 1769480 | tf_op jit(solution)/shard_map/ppermute | solution.py:671
  188.2 14.8 %collective-permute-start.34 = (bf16[704,256]{1,0:T(8,128)(2,1)S(1)}, bf16[704,256]{1,0:T(8,128)(2,1)S(1)}, u32[]{:S(2)}, u32[]{:S(2)}) collective-permute-start(bf16[704,256]{1,0:T(8,128)(2,1)S(1)} %add_convert_fusion.5), channel_id=1, source_target_pairs={{1,2},{2,1},{5,6},{6,5},{9,10},{10,9},{13,14},{14,13},{17,18},{18,... | collective-permute-start | bytes 1081352 | tf_op jit(solution)/shard_map/ppermute | solution.py:622
  189.1 13.9 %collective-permute-start.33 = (bf16[704,256]{1,0:T(8,128)(2,1)S(1)}, bf16[704,256]{1,0:T(8,128)(2,1)S(1)}, u32[]{:S(2)}, u32[]{:S(2)}) collective-permute-start(bf16[704,256]{1,0:T(8,128)(2,1)S(1)} %broadcast_select_fusion.1), channel_id=1, source_target_pairs={{0,1},{1,0},{2,3},{3,2},{4,5},{5,4},{6,7},{7,6},{8,9},{9,8},{10,11... | collective-permute-start | bytes 1081352 | tf_op jit(solution)/shard_map/ppermute | solution.py:622
  203.1 32.8 %collective-permute-start.40 = (bf16[2,128,1152]{2,1,0:T(8,128)(2,1)S(1)}, bf16[2,128,1152]{2,1,0:T(8,128)(2,1)S(1)}, u32[]{:S(2)}, u32[]{:S(2)}) collective-permute-start(bf16[2,128,1152]{2,1,0:T(8,128)(2,1)S(1)} %pad_maximum_fusion.1.refs_2_), channel_id=1, source_target_pairs={{0,16},{4,20},{8,24},{12,28},{16,0},{20,4},{24,8},{28,12},{1,17},{... | collective-permute-start | bytes 1769480 | tf_op jit(solution)/shard_map/ppermute | solution.py:671
  205.4 30.5 %collective-permute-start.39 = (bf16[2,128,1152]{2,1,0:T(8,128)(2,1)S(1)}, bf16[2,128,1152]{2,1,0:T(8,128)(2,1)S(1)}, u32[]{:S(2)}, u32[]{:S(2)}) collective-permute-start(bf16[2,128,1152]{2,1,0:T(8,128)(2,1)S(1)} %pad_maximum_fusion.refs_0_), channel_id=1, source_target_pairs={{0,8},{4,12},{8,0},{12,4},{16,24},{20,28},{24,16},{28,20},{1,9},{5... | collective-permute-start | bytes 1769480 | tf_op jit(solution)/shard_map/ppermute | solution.py:671
  206.0 29.9 %collective-permute-start.38 = (bf16[704,256]{1,0:T(8,128)(2,1)S(1)}, bf16[704,256]{1,0:T(8,128)(2,1)S(1)}, u32[]{:S(2)}, u32[]{:S(2)}) collective-permute-start(bf16[704,256]{1,0:T(8,128)(2,1)S(1)} %add_convert_fusion.3), channel_id=1, source_target_pairs={{1,2},{2,1},{5,6},{6,5},{9,10},{10,9},{13,14},{14,13},{17,18},{18,... | collective-permute-start | bytes 1081352 | tf_op jit(solution)/shard_map/ppermute | solution.py:622
  206.9 29.0 %collective-permute-start.37 = (bf16[704,256]{1,0:T(8,128)(2,1)S(1)}, bf16[704,256]{1,0:T(8,128)(2,1)S(1)}, u32[]{:S(2)}, u32[]{:S(2)}) collective-permute-start(bf16[704,256]{1,0:T(8,128)(2,1)S(1)} %add_convert_fusion.4), channel_id=1, source_target_pairs={{0,1},{1,0},{2,3},{3,2},{4,5},{5,4},{6,7},{7,6},{8,9},{9,8},{10,11... | collective-permute-start | bytes 1081352 | tf_op jit(solution)/shard_map/ppermute | solution.py:622
  262.9 14.2 %collective-permute-start.51 = (bf16[704,256]{1,0:T(8,128)(2,1)S(1)}, bf16[704,256]{1,0:T(8,128)(2,1)S(1)}, u32[]{:S(2)}, u32[]{:S(2)}) collective-permute-start(bf16[704,256]{1,0:T(8,128)(2,1)S(1)} %get-tuple-element.291), channel_id=1, source_target_pairs={{1,2},{2,1},{5,6},{6,5},{9,10},{10,9},{13,14},{14,13},{17,18},{18,... | collective-permute-start | bytes 1081352 | tf_op jit(solution)/shard_map/ppermute | solution.py:622
  263.6 14.1 %collective-permute-start.52 = (bf16[704,256]{1,0:T(8,128)(2,1)S(1)}, bf16[704,256]{1,0:T(8,128)(2,1)S(1)}, u32[]{:S(2)}, u32[]{:S(2)}) collective-permute-start(bf16[704,256]{1,0:T(8,128)(2,1)S(1)} %get-tuple-element.292), channel_id=1, source_target_pairs={{0,1},{3,2},{4,5},{7,6},{8,9},{11,10},{12,13},{15,14},{16,17},{19,... | collective-permute-start | bytes 1081352 | tf_op jit(solution)/shard_map/ppermute | solution.py:622
  277.7 13.1 %collective-permute-start.54 = (bf16[2,208,512]{2,1,0:T(8,128)(2,1)S(1)}, bf16[2,208,512]{2,1,0:T(8,128)(2,1)S(1)}, u32[]{:S(2)}, u32[]{:S(2)}) collective-permute-start(bf16[2,208,512]{2,1,0:T(8,128)(2,1)S(1)} %pad_maximum_fusion.3.refs_2_), channel_id=1, source_target_pairs={{0,16},{4,20},{8,24},{12,28},{16,0},{20,4},{24,8},{28,12},{1,17},{... | collective-permute-start | bytes 1277960 | tf_op jit(solution)/shard_map/ppermute | solution.py:671
  (78 other events, 951.8 us)

commit v4 on v3

--- a/solution.py
+++ b/solution.py
@@ -87,6 +87,14 @@
 
 def row_scale(squares, width):
     return lax.rsqrt(jnp.sum(squares, axis=1, keepdims=True) * (1.0 / width) + NORM_EPSILON)
+
+
+def pack_kernel(info_ref, x_ref, ag_ref, fg_ref, out_ref):
+    seq_len, shard = x_ref.shape
+    out_ref[0:seq_len, :] = x_ref[...]
+    gains = jnp.concatenate([ag_ref[...], fg_ref[...], jnp.zeros((6, shard), f32)], axis=0)
+    high = gains.astype(bf16)
+    out_ref[seq_len : seq_len + TAIL, :] = jnp.concatenate([high, (gains - high.astype(f32)).astype(bf16)], axis=0)
 
 
 def copies(sources, targets, sems):
@@ -342,28 +350,30 @@
         copy.wait()
 
 
-def halves_kernel(info_ref, keep_hbm, other_hbm, to_x, to_y, keep_x, keep_y, keep_ref, other_ref, sems):
+def halves_kernel(
+    info_ref, keep_hbm, other_hbm, on_x, to_x, on_y, to_y, keep_on_x, keep_x, keep_on_y, keep_y, keep_ref, other_ref, sems
+):
     for copy in copies((keep_hbm, other_hbm), (keep_ref, other_ref), sems):
         copy.wait()
-    cols = to_x.shape[2]
-    for out_ref, first, flips in ((to_x, 0, (1, 3)), (keep_x, 0, (0, 2)), (to_y, cols, (2, 3)), (keep_y, cols, (0, 1))):
-        for i, flip in enumerate(flips):
-            block = jnp.bitwise_xor(info_ref[2], flip)
-            out_ref[i] = (
-                keep_ref[block, :, first : first + cols].astype(f32) + other_ref[block, :, first : first + cols].astype(f32)
-            ).astype(bf16)
-
-
-def halve_kernel(info_ref, keep_x, keep_y, got_x, got_y, to_y, to_x, own_x, own_y):
-    own_x[...] = (keep_x[0].astype(f32) + got_x[0].astype(f32)).astype(bf16)
-    own_y[...] = (keep_y[0].astype(f32) + got_y[0].astype(f32)).astype(bf16)
-    to_y[...] = (keep_x[1].astype(f32) + got_x[1].astype(f32)).astype(bf16)
-    to_x[...] = (keep_y[1].astype(f32) + got_y[1].astype(f32)).astype(bf16)
-
-
-def join_kernel(info_ref, own_x, own_y, from_y, from_x, left_ref, right_ref):
-    left_ref[...] = (own_x[...].astype(f32) + from_y[...].astype(f32)).astype(bf16)
-    right_ref[...] = (own_y[...].astype(f32) + from_x[...].astype(f32)).astype(bf16)
+    cols = to_x.shape[1]
+    for out_ref, first, flip in (
+        (on_x, 0, 3), (to_x, 0, 1), (keep_on_x, 0, 2), (keep_x, 0, 0),
+        (on_y, cols, 3), (to_y, cols, 2), (keep_on_y, cols, 1), (keep_y, cols, 0),
+    ):
+        block = jnp.bitwise_xor(info_ref[2], flip)
+        out_ref[...] = (
+            keep_ref[block, :, first : first + cols].astype(f32) + other_ref[block, :, first : first + cols].astype(f32)
+        ).astype(bf16)
+
+
+def pass_kernel(info_ref, keep_on_x, got_on_x, keep_on_y, got_on_y, to_y, to_x):
+    to_y[...] = (keep_on_x[...].astype(f32) + got_on_x[...].astype(f32)).astype(bf16)
+    to_x[...] = (keep_on_y[...].astype(f32) + got_on_y[...].astype(f32)).astype(bf16)
+
+
+def join_kernel(info_ref, keep_x, got_x, from_y, keep_y, got_y, from_x, left_ref, right_ref):
+    left_ref[...] = (keep_x[...].astype(f32) + (got_x[...].astype(f32) + from_y[...].astype(f32))).astype(bf16)
+    right_ref[...] = (keep_y[...].astype(f32) + (got_y[...].astype(f32) + from_x[...].astype(f32))).astype(bf16)
 
 
 def unpack_ffn_kernel(info_ref, *refs):
@@ -541,13 +551,13 @@
     small_ref[2:3, 2 * hd : 2 * hd + 128] = totals
 
 
-def block_kernel(info_ref, own_x, own_y, from_y, from_x, small_ref, left_ref, right_ref):
-    rows, cols = own_x.shape
+def block_kernel(info_ref, keep_x, got_x, from_y, keep_y, got_y, from_x, small_ref, left_ref, right_ref):
+    rows, cols = keep_x.shape
     small = small_ref[...]
     high = small.astype(bf16)
     tail = jnp.concatenate([high, (small - high.astype(f32)).astype(bf16)], axis=0)
-    for a, b, out_ref, first in ((own_x, from_y, left_ref, 0), (own_y, from_x, right_ref, cols)):
-        out_ref[0:rows, :] = (a[...].astype(f32) + b[...].astype(f32)).astype(bf16)
+    for a, b, c, out_ref, first in ((keep_x, got_x, from_y, left_ref, 0), (keep_y, got_y, from_x, right_ref, cols)):
+        out_ref[0:rows, :] = (a[...].astype(f32) + (b[...].astype(f32) + c[...].astype(f32))).astype(bf16)
         out_ref[rows : rows + TAIL, :] = tail[:, first : first + cols]
 
 
@@ -661,12 +671,6 @@
     return own.astype(f32) + (pair.astype(f32) + across.astype(f32))
 
 
-def split_rows(values):
-    high = lax.optimization_barrier(values.astype(bf16))
-    low = (values - high.astype(f32)).astype(bf16)
-    return jnp.concatenate([high, low], axis=0)
-
-
 def swap(values, bit):
     return lax.ppermute(values, "dp", [(i, i ^ bit) for i in range(8)])
 
@@ -675,16 +679,16 @@
     _, rows, width = keep.shape
     return call(
         halves_kernel,
-        [((2, rows, width // 2), bf16, "v")] * 4,
+        [((rows, width // 2), bf16, "v")] * 8,
         (("s", info), ("a", keep, other)),
         scratch=[((4, rows, width), bf16)] * 2,
         sems=(2,),
     )
 
 
-def halve_again(keep_x, keep_y, got_x, got_y, info):
+def pass_on(keep_on_x, got_on_x, keep_on_y, got_on_y, info):
     return call(
-        halve_kernel, [(keep_x.shape[1:], bf16, "v")] * 4, (("s", info), ("v", keep_x, keep_y, got_x, got_y))
+        pass_kernel, [(keep_on_x.shape, bf16, "v")] * 2, (("s", info), ("v", keep_on_x, got_on_x, keep_on_y, got_on_y))
     )
 
 
@@ -706,8 +710,11 @@
     parts = [((seq_len, shard), bf16, "v")] * 4
 
     end = (z == 0) | (z == 3)
-    gains = jnp.concatenate([attn_gain[None], ffn_gain[None], jnp.zeros((6, shard), f32)], axis=0)
-    x = jnp.concatenate([hidden_in, split_rows(gains)], axis=0)
+    x = call(
+        pack_kernel,
+        [((seq_len + TAIL, shard), bf16, "v")],
+        (("s", lengths), ("v", hidden_in, attn_gain[None], ffn_gain[None])),
+    )[0]
     cot = jnp.concatenate([cotangent, jnp.zeros((TAIL, shard), bf16)], axis=0)
     x_pair, x_mid = send(x, PAIRS), send(x, MIDDLE)
     x_pair, x_mid, cot = hold(x_pair, x_mid, cot)
@@ -785,24 +792,27 @@
     back = scatter_last(ffn_parts, first)
     if chips:
         ffn_other = swap(ffn_give, 1)
-        cols = (width // 8, 3 * hidden // 2)
-        to_x, to_y, keep_x, keep_y = halve(ffn_keep, ffn_other, info)
-        back, to_x, to_y, keep_x, keep_y = hold(back, to_x, to_y, keep_x, keep_y)
+        halves = halve(ffn_keep, ffn_other, info)
+        back, halves = hold(back, halves)
+        on_x, to_x, on_y, to_y, keep_on_x, keep_x, keep_on_y, keep_y = halves
     grad_middle = grad_top + total(back)
     ga = grad_middle.astype(bf16)
     across, far, pair, own = down_parts
     ga_pair, ga_mid = send(ga, PAIRS), send(ga, MIDDLE)
     if chips:
+        got_on_x, got_on_y = swap(on_x, 2), swap(on_y, 4)
         got_x, got_y = swap(to_x, 2), swap(to_y, 4)
-        ga_pair, ga_mid, far, got_x, got_y = hold(ga_pair, ga_mid, far, got_x, got_y)
-        to_y, to_x, own_x, own_y = halve_again(keep_x, keep_y, got_x, got_y, info)
+        to_y, to_x = pass_on(keep_on_x, got_on_x, keep_on_y, got_on_y, info)
+        ga_pair, ga_mid, far, to_y, to_x = hold(ga_pair, ga_mid, far, to_y, to_x)
         from_y, from_x = swap(to_y, 4), swap(to_x, 2)
     ga_end, ga_far = send(pick(end, far, ga_mid), PAIRS), send(ga_pair, MIDDLE)
     if chips:
-        ga_end, ga_far, across, from_y, from_x = hold(ga_end, ga_far, across, from_y, from_x)
         left, right = call(
-            join_kernel, [(cols, bf16, "v")] * 2, (("s", info), ("v", own_x, own_y, from_y, from_x))
+            join_kernel,
+            [((width // 8, 3 * hidden // 2), bf16, "v")] * 2,
+            (("s", info), ("v", keep_x, got_x, from_y, keep_y, got_y, from_x)),
         )
+        ga_end, ga_far, across, left, right = hold(ga_end, ga_far, across, left, right)
         left_y, right_x = swap(left, 4), swap(right, 2)
     ga_last = send(pick(end, across, ga_far), PAIRS)
     got_far = send(add(far, ga_end), MIDDLE)
@@ -844,21 +854,22 @@
     shapes = [(width, qw), (width, kw), (width, kw), (qw, width)]
     if chips:
         other, small = hold(other, small)
-        to_x, to_y, keep_x, keep_y = halve(keep, other, info)
+        on_x, to_x, on_y, to_y, keep_on_x, keep_x, keep_on_y, keep_y = halve(keep, other, info)
+        got_on_x, got_on_y = swap(on_x, 2), swap(on_y, 4)
         got_x, got_y = swap(to_x, 2), swap(to_y, 4)
         small = small + send(small, PAIRS)
         small = small + send(small, ((0, 2), (2, 0), (1, 3), (3, 1)))
-        got_x, got_y, small, far, across = hold(got_x, got_y, small, far, across)
-        to_y, to_x, own_x, own_y = halve_again(keep_x, keep_y, got_x, got_y, info)
-        from_y, from_x, two = hold(swap(to_y, 4), swap(to_x, 2), send(far, INWARD_TWO))
+        to_y, to_x = pass_on(keep_on_x, got_on_x, keep_on_y, got_on_y, info)
+        to_y, to_x, small, far, across = hold(to_y, to_x, small, far, across)
+        from_y, from_x, two = swap(to_y, 4), swap(to_x, 2), send(far, INWARD_TWO)
         late_left, late_right = call(
             block_kernel,
-            [((own_x.shape[0] + TAIL, own_x.shape[1]), bf16, "v")] * 2,
-            (("s", info), ("v", own_x, own_y, from_y, from_x, small)),
+            [((keep_x.shape[0] + TAIL, keep_x.shape[1]), bf16, "v")] * 2,
+            (("s", info), ("v", keep_x, got_x, from_y, keep_y, got_y, from_x, small)),
         )
         late_left, late_right, far, across = hold(late_left, late_right, far, across)
         three, one = send(far, MIDDLE), send(across, INWARD)
-        left_y, right_x, three, one = hold(swap(late_left, 4), swap(late_right, 2), three, one)
+        left_y, right_x, two, three, one = hold(swap(late_left, 4), swap(late_right, 2), two, three, one)
         late_lefts, late_rights = jnp.stack([late_left, left_y]), jnp.stack([late_right, right_x])
         back_terms = scatter_last((across, far, pair, own), (two, three, one))
         ffn_halves = (lefts, lefts_x, rights, rights_y)

time: 304 us -> 302 us (level)
  waiting for transfers between devices: 117 us -> 112 us
  starting transfers between devices: 90.3 us -> 94.6 us
    ppermute x39, waiting for transfers between devices: 85.2 us -> 78.8 us  [send(): return lax.ppermute(rows, 'tensor', pairs)]
    ppermute x26 -> x30, starting transfers between devices: 16.5 us -> 21.5 us  [swap(): return lax.ppermute(values, 'dp', [(i, i ^ bit) for i in range(8)])]
    unnamed x74 -> x80, local copies, waits for them, and re-layouts: 4.72 us -> 6.32 us
    ppermute x26 -> x30, waiting for transfers between devices: 32.1 us -> 33.6 us  [swap(): return lax.ppermute(values, 'dp', [(i, i ^ bit) for i in range(8)])]
    pallas_call x14 -> x15, Pallas kernels: 72 us -> 71.9 us  [call(): pl.pallas_call(body, out_shape=[jax.ShapeDtypeStruct(s, d) for s, d, _ in...]
  transfers between devices with their start and end apart: 65 -> 69, of which waited for: 31 -> 26; matrix products, arithmetic and copies ran while one was open for 3% -> 3% of each run, Pallas kernels for 19% -> 19%
where the time goes in v4:
time: 302 us; the launch traced here: 297 us
  waiting for transfers between devices  112 us (37%)
  starting transfers between devices  94.6 us (31%)
  Pallas kernels  71.9 us (24%)
  other arithmetic  8.1 us (3%)
  local copies, waits for them, and re-layouts  7.85 us (3%)
    ppermute x39, waiting for transfers between devices, send(): return lax.ppermute(rows, 'tensor', pairs)  78.8 us
    ppermute x39, starting transfers between devices, send(): return lax.ppermute(rows, 'tensor', pairs)  73.1 us
    pallas_call x15, Pallas kernels, call(): pl.pallas_call(body, out_shape=[jax.ShapeDtypeStruct(s, d) for s, d, _ in...  71.9 us
    ppermute x30, waiting for transfers between devices, swap(): return lax.ppermute(values, 'dp', [(i, i ^ bit) for i in range(8)])  33.6 us
    ppermute x30, starting transfers between devices, swap(): return lax.ppermute(values, 'dp', [(i, i ^ bit) for i in range(8)])  21.5 us
    unnamed x80, local copies, waits for them, and re-layouts  6.32 us
  transfers between devices with their start and end apart: 69, of which 26 were waited for; matrix products, arithmetic and copies ran while one was open for 3% of the time, Pallas kernels for 19%

profile of v4, /device:TPU:0, one launch (start us, length us, event | category | flops | bytes accessed | tf_op | source)
XLA Modules:
  0.0 297.3 jit_solution(18294003895933233640)
XLA Ops:
  8.5 6.9 %collective-permute-done.x1 = bf16[720,256]{1,0:T(8,128)(2,1)S(1)} collective-permute-done((bf16[720,256]{1,0:T(8,128)(2,1)S(1)}, bf16[720,256]{1,0:T(8,128)(2,1)S(1)}, u32[]{:S(2)}, u32[]{:S(2)}) %collective-permute-start) | collective-permute-done | bytes 368672 | tf_op jit(solution)/shard_map/ppermute | solution.py:632
  15.4 4.8 %collective-permute-start.2 = (bf16[720,256]{1,0:T(8,128)(2,1)S(1)}, bf16[720,256]{1,0:T(8,128)(2,1)S(1)}, u32[]{:S(2)}, u32[]{:S(2)}) collective-permute-start(bf16[720,256]{1,0:T(8,128)(2,1)S(1)} %broadcast_select_fusion), channel_id=1, source_target_pairs={{0,1},{1,0},{2,3},{3,2},{4,5},{5,4},{6,7},{7,6},{8,9},{9,8},{10,11... | collective-permute-start | bytes 1105928 | tf_op jit(solution)/shard_map/ppermute | solution.py:632
  21.0 7.0 %collective-permute-done.2.x3.c1 = bf16[720,256]{1,0:T(8,128)(2,1)S(1)} collective-permute-done((bf16[720,256]{1,0:T(8,128)(2,1)S(1)}, bf16[720,256]{1,0:T(8,128)(2,1)S(1)}, u32[]{:S(2)}, u32[]{:S(2)}) %collective-permute-start.2) | collective-permute-done | bytes 368672 | tf_op jit(solution)/shard_map/ppermute | solution.py:632
  32.4 7.2 %collective-permute-done.4.x5 = bf16[720,256]{1,0:T(8,128)(2,1)S(1)} collective-permute-done((bf16[720,256]{1,0:T(8,128)(2,1)S(1)}, bf16[720,256]{1,0:T(8,128)(2,1)S(1)}, u32[]{:S(2)}, u32[]{:S(2)}) %collective-permute-start.4) | collective-permute-done | bytes 368672 | tf_op jit(solution)/shard_map/ppermute | solution.py:632
  43.5 12.2 %shard_map.246 = (bf16[704,256]{1,0:T(8,128)(2,1)}, bf16[704,256]{1,0:T(8,128)(2,1)}, bf16[704,256]{1,0:T(8,128)(2,1)}, bf16[704,256]{1,0:T(8,128)(2,1)}, bf16[7...) custom-call(s32[4]{0:T(128)} %pad_add_fusion.info_ref, ...), custom_call_target="tpu_custom_call" | custom-call | flops 3229614080 | bytes 14000000 | tf_op jit(solution)/shard_map/pallas_call | solution.py:612
  56.8 3.9 %collective-permute-done.8.c6 = bf16[720,256]{1,0:T(8,128)(2,1)S(1)} collective-permute-done((bf16[720,256]{1,0:T(8,128)(2,1)S(1)}, bf16[720,256]{1,0:T(8,128)(2,1)S(1)}, u32[]{:S(2)}, u32[]{:S(2)}) %collective-permute-start.8) | collective-permute-done | bytes 368672 | tf_op jit(solution)/shard_map/ppermute | solution.py:632
  66.2 6.7 %collective-permute-done.9 = bf16[704,256]{1,0:T(8,128)(2,1)S(1)} collective-permute-done((bf16[704,256]{1,0:T(8,128)(2,1)}, bf16[704,256]{1,0:T(8,128)(2,1)S(1)}, u32[]{:S(2)}, u32[]{:S(2)}) %collective-permute-start.9) | collective-permute-done | bytes 360480 | tf_op jit(solution)/shard_map/ppermute | solution.py:632
  74.2 5.4 %collective-permute-start.11 = (bf16[704,256]{1,0:T(8,128)(2,1)S(1)}, bf16[704,256]{1,0:T(8,128)(2,1)S(1)}, u32[]{:S(2)}, u32[]{:S(2)}) collective-permute-start(bf16[704,256]{1,0:T(8,128)(2,1)S(1)} %add_convert_fusion.9), channel_id=1, source_target_pairs={{0,1},{1,0},{2,3},{3,2},{4,5},{5,4},{6,7},{7,6},{8,9},{9,8},{10,11... | collective-permute-start | bytes 1081352 | tf_op jit(solution)/shard_map/ppermute | solution.py:632
  80.6 6.7 %collective-permute-done.11 = bf16[704,256]{1,0:T(8,128)(2,1)S(1)} collective-permute-done((bf16[704,256]{1,0:T(8,128)(2,1)S(1)}, bf16[704,256]{1,0:T(8,128)(2,1)S(1)}, u32[]{:S(2)}, u32[]{:S(2)}) %collective-permute-start.11) | collective-permute-done | bytes 360480 | tf_op jit(solution)/shard_map/ppermute | solution.py:632
  88.2 6.9 %collective-permute-start.14 = (bf16[704,256]{1,0:T(8,128)(2,1)S(1)}, bf16[704,256]{1,0:T(8,128)(2,1)S(1)}, u32[]{:S(2)}, u32[]{:S(2)}) collective-permute-start(bf16[704,256]{1,0:T(8,128)(2,1)S(1)} %get-tuple-element.196.m0), channel_id=1, source_target_pairs={{0,1},{1,0},{2,3},{3,2},{4,5},{5,4},{6,7},{7,6},{8,9},{9,8},{10,11... | collective-permute-start | bytes 1081352 | tf_op jit(solution)/shard_map/ppermute | solution.py:632
  96.5 5.7 %collective-permute-done.14.m1 = bf16[704,256]{1,0:T(8,128)(2,1)S(1)} collective-permute-done((bf16[704,256]{1,0:T(8,128)(2,1)S(1)}, bf16[704,256]{1,0:T(8,128)(2,1)S(1)}, u32[]{:S(2)}, u32[]{:S(2)}) %collective-permute-start.14) | collective-permute-done | bytes 360480 | tf_op jit(solution)/shard_map/ppermute | solution.py:632
  104.2 6.1 %collective-permute-done.16.m3 = bf16[704,256]{1,0:T(8,128)(2,1)S(1)} collective-permute-done((bf16[704,256]{1,0:T(8,128)(2,1)S(1)}, bf16[704,256]{1,0:T(8,128)(2,1)S(1)}, u32[]{:S(2)}, u32[]{:S(2)}) %collective-permute-start.16) | collective-permute-done | bytes 360480 | tf_op jit(solution)/shard_map/ppermute | solution.py:632
  110.3 10.2 %collective-permute-done.18.m5 = bf16[704,256]{1,0:T(8,128)(2,1)S(1)} collective-permute-done((bf16[704,256]{1,0:T(8,128)(2,1)S(1)}, bf16[704,256]{1,0:T(8,128)(2,1)S(1)}, u32[]{:S(2)}, u32[]{:S(2)}) %collective-permute-start.18) | collective-permute-done | bytes 360480 | tf_op jit(solution)/shard_map/ppermute | solution.py:632
  120.5 10.3 %shard_map.247 = (bf16[704,256]{1,0:T(8,128)(2,1)S(1)}, bf16[704,256]{1,0:T(8,128)(2,1)S(1)}, bf16[704,256]{1,0:T(8,128)(2,1)S(1)}, bf16[704,256]{1,0:T(8,128)(2...) custom-call(s32[4]{0:T(128)S(1)} %copy-done.6, ...), custom_call_target="tpu_custom_call" | custom-call | flops 5536481280 | bytes 16000000 | tf_op jit(solution)/shard_map/pallas_call | solution.py:612
  139.9 7.4 %shard_map.248 = (bf16[704,256]{1,0:T(8,128)(2,1)S(1)}, bf16[704,256]{1,0:T(8,128)(2,1)S(1)}, bf16[704,256]{1,0:T(8,128)(2,1)S(1)}, bf16[704,256]{1,0:T(8,128)(2...) custom-call(s32[4]{0:T(128)S(1)} %copy-done.6, ...), custom_call_target="tpu_custom_call" | custom-call | flops 4429185024 | bytes 14000000 | tf_op jit(solution)/shard_map/pallas_call | solution.py:612
  153.6 7.3 %collective-permute-done.22 = bf16[704,256]{1,0:T(8,128)(2,1)S(1)} collective-permute-done((bf16[704,256]{1,0:T(8,128)(2,1)S(1)}, bf16[704,256]{1,0:T(8,128)(2,1)S(1)}, u32[]{:S(2)}, u32[]{:S(2)}) %collective-permute-start.22) | collective-permute-done | bytes 360480 | tf_op jit(solution)/shard_map/ppermute | solution.py:632
  167.3 6.4 %collective-permute-done.27.got_on_x = bf16[128,1152]{1,0:T(8,128)(2,1)S(1)} collective-permute-done((bf16[128,1152]{1,0:T(8,128)(2,1)S(1)}, bf16[128,1152]{1,0:T(8,128)(2,1)S(1)}, u32[]{:S(2)}, u32[]{:S(2)}) %collective-permute-start.27) | collective-permute-done | bytes 294944 | tf_op jit(solution)/shard_map/ppermute | solution.py:675
  181.7 5.6 %collective-permute-done.33.got_y = bf16[128,1152]{1,0:T(8,128)(2,1)S(1)} collective-permute-done((bf16[128,1152]{1,0:T(8,128)(2,1)S(1)}, bf16[128,1152]{1,0:T(8,128)(2,1)S(1)}, u32[]{:S(2)}, u32[]{:S(2)}) %collective-permute-start.33) | collective-permute-done | bytes 294944 | tf_op jit(solution)/shard_map/ppermute | solution.py:675
  192.3 4.7 %collective-permute-start.35 = (bf16[704,256]{1,0:T(8,128)(2,1)S(1)}, bf16[704,256]{1,0:T(8,128)(2,1)S(1)}, u32[]{:S(2)}, u32[]{:S(2)}) collective-permute-start(bf16[704,256]{1,0:T(8,128)(2,1)S(1)} %broadcast_select_fusion.1), channel_id=1, source_target_pairs={{0,1},{1,0},{2,3},{3,2},{4,5},{5,4},{6,7},{7,6},{8,9},{9,8},{10,11... | collective-permute-start | bytes 1081352 | tf_op jit(solution)/shard_map/ppermute | solution.py:632
  199.1 6.3 %collective-permute-done.37 = bf16[128,1152]{1,0:T(8,128)(2,1)S(1)} collective-permute-done((bf16[128,1152]{1,0:T(8,128)(2,1)S(1)}, bf16[128,1152]{1,0:T(8,128)(2,1)S(1)}, u32[]{:S(2)}, u32[]{:S(2)}) %collective-permute-start.37) | collective-permute-done | bytes 294944 | tf_op jit(solution)/shard_map/ppermute | solution.py:675
  212.2 26.1 %shard_map.252 = (bf16[704,256]{1,0:T(8,128)(2,1)S(1)}, bf16[704,256]{1,0:T(8,128)(2,1)S(1)}, bf16[704,256]{1,0:T(8,128)(2,1)S(1)}, bf16[704,256]{1,0:T(8,128)(2...) custom-call(s32[4]{0:T(128)S(1)} %copy-done.6, ...), custom_call_target="tpu_custom_call" | custom-call | flops 6966738944 | bytes 20000000 | tf_op jit(solution)/shard_map/pallas_call | solution.py:612
  263.1 5.3 %collective-permute-start.56 = (bf16[704,256]{1,0:T(8,128)(2,1)S(1)}, bf16[704,256]{1,0:T(8,128)(2,1)S(1)}, u32[]{:S(2)}, u32[]{:S(2)}) collective-permute-start(bf16[704,256]{1,0:T(8,128)(2,1)S(1)} %get-tuple-element.304), channel_id=1, source_target_pairs={{0,1},{3,2},{4,5},{7,6},{8,9},{11,10},{12,13},{15,14},{16,17},{19,... | collective-permute-start | bytes 1081352 | tf_op jit(solution)/shard_map/ppermute | solution.py:632
  270.3 4.0 %collective-permute-done.52 = bf16[208,512]{1,0:T(8,128)(2,1)S(1)} collective-permute-done((bf16[208,512]{1,0:T(8,128)(2,1)S(1)}, bf16[208,512]{1,0:T(8,128)(2,1)S(1)}, u32[]{:S(2)}, u32[]{:S(2)}) %collective-permute-start.52) | collective-permute-done | bytes 213024 | tf_op jit(solution)/shard_map/ppermute | solution.py:675
  281.1 4.9 %shard_map.258 = (f32[1024,768]{1,0:T(8,128)}, f32[1024,768]{1,0:T(8,128)}, f32[768,1024]{1,0:T(8,128)}) custom-call(s32[4]{0:T(128)S(1)} %copy-done.6, bf16[2,128,1152]{2,1,0:T(8,128)(2,1)S(1)} %pad_maximum_fusion.refs_0_, bf16[2,128,1152]{2,1,0:T(8,128)(2,1)S(1)} %collective-permute-done.41.refs_1_, bf16[2,128,1152]{2,1,0:T(8,128)(2,1)S(1)} %pad_maximum_fusion.1.refs_2_, ...), custom_call_target="tpu_custom_call" | custom-call | bytes 14000000 | tf_op jit(solution)/shard_map/pallas_call | solution.py:612
  (239 shorter events, 116.8 us)
Async XLA Ops:
  39.7 16.1 %collective-permute-start.6 = (bf16[720,256]{1,0:T(8,128)(2,1)S(1)}, bf16[720,256]{1,0:T(8,128)(2,1)S(1)}, u32[]{:S(2)}, u32[]{:S(2)}) collective-permute-start(bf16[720,256]{1,0:T(8,128)(2,1)S(1)} %concatenate.9.c0), channel_id=1, source_target_pairs={{1,2},{2,1},{5,6},{6,5},{9,10},{10,9},{13,14},{14,13},{17,18},{18,... | collective-permute-start | bytes 1105928 | tf_op jit(solution)/shard_map/ppermute | solution.py:632
  40.4 16.5 %collective-permute-start.7 = (bf16[720,256]{1,0:T(8,128)(2,1)S(1)}, bf16[720,256]{1,0:T(8,128)(2,1)S(1)}, u32[]{:S(2)}, u32[]{:S(2)}) collective-permute-start(bf16[720,256]{1,0:T(8,128)(2,1)S(1)} %concatenate.9.c0), channel_id=1, source_target_pairs={{1,0},{2,3},{5,4},{6,7},{9,8},{10,11},{13,12},{14,15},{17,16},{18,... | collective-permute-start | bytes 1105928 | tf_op jit(solution)/shard_map/ppermute | solution.py:632
  41.7 19.1 %collective-permute-start.8 = (bf16[720,256]{1,0:T(8,128)(2,1)S(1)}, bf16[720,256]{1,0:T(8,128)(2,1)S(1)}, u32[]{:S(2)}, u32[]{:S(2)}) collective-permute-start(bf16[720,256]{1,0:T(8,128)(2,1)S(1)} %collective-permute-done.5.c5), channel_id=1, source_target_pairs={{1,0},{2,3},{5,4},{6,7},{9,8},{10,11},{13,12},{14,15},{17,16},{18,... | collective-permute-start | bytes 1105928 | tf_op jit(solution)/shard_map/ppermute | solution.py:632
  66.0 13.6 %collective-permute-start.12 = (bf16[704,256]{1,0:T(8,128)(2,1)S(1)}, bf16[704,256]{1,0:T(8,128)(2,1)S(1)}, u32[]{:S(2)}, u32[]{:S(2)}) collective-permute-start(bf16[704,256]{1,0:T(8,128)(2,1)S(1)} %slice_select_fusion), channel_id=1, source_target_pairs={{0,1},{1,0},{2,3},{3,2},{4,5},{5,4},{6,7},{7,6},{8,9},{9,8},{10,11... | collective-permute-start | bytes 1081352 | tf_op jit(solution)/shard_map/ppermute | solution.py:632
  74.2 13.1 %collective-permute-start.11 = (bf16[704,256]{1,0:T(8,128)(2,1)S(1)}, bf16[704,256]{1,0:T(8,128)(2,1)S(1)}, u32[]{:S(2)}, u32[]{:S(2)}) collective-permute-start(bf16[704,256]{1,0:T(8,128)(2,1)S(1)} %add_convert_fusion.9), channel_id=1, source_target_pairs={{0,1},{1,0},{2,3},{3,2},{4,5},{5,4},{6,7},{7,6},{8,9},{9,8},{10,11... | collective-permute-start | bytes 1081352 | tf_op jit(solution)/shard_map/ppermute | solution.py:632
  88.2 14.0 %collective-permute-start.14 = (bf16[704,256]{1,0:T(8,128)(2,1)S(1)}, bf16[704,256]{1,0:T(8,128)(2,1)S(1)}, u32[]{:S(2)}, u32[]{:S(2)}) collective-permute-start(bf16[704,256]{1,0:T(8,128)(2,1)S(1)} %get-tuple-element.196.m0), channel_id=1, source_target_pairs={{0,1},{1,0},{2,3},{3,2},{4,5},{5,4},{6,7},{7,6},{8,9},{9,8},{10,11... | collective-permute-start | bytes 1081352 | tf_op jit(solution)/shard_map/ppermute | solution.py:632
  95.2 15.1 %collective-permute-start.16 = (bf16[704,256]{1,0:T(8,128)(2,1)S(1)}, bf16[704,256]{1,0:T(8,128)(2,1)S(1)}, u32[]{:S(2)}, u32[]{:S(2)}) collective-permute-start(bf16[704,256]{1,0:T(8,128)(2,1)S(1)} %collective-permute-done.15.m2), channel_id=1, source_target_pairs={{1,0},{2,3},{5,4},{6,7},{9,8},{10,11},{13,12},{14,15},{17,16},{18,... | collective-permute-start | bytes 1081352 | tf_op jit(solution)/shard_map/ppermute | solution.py:632
  102.9 17.6 %collective-permute-start.18 = (bf16[704,256]{1,0:T(8,128)(2,1)S(1)}, bf16[704,256]{1,0:T(8,128)(2,1)S(1)}, u32[]{:S(2)}, u32[]{:S(2)}) collective-permute-start(bf16[704,256]{1,0:T(8,128)(2,1)S(1)} %collective-permute-done.14.m1), channel_id=1, source_target_pairs={{2,0},{1,3},{6,4},{5,7},{10,8},{9,11},{14,12},{13,15},{18,16},{17,... | collective-permute-start | bytes 1081352 | tf_op jit(solution)/shard_map/ppermute | solution.py:632
  131.8 15.5 %collective-permute-start.19 = (bf16[704,256]{1,0:T(8,128)(2,1)S(1)}, bf16[704,256]{1,0:T(8,128)(2,1)S(1)}, u32[]{:S(2)}, u32[]{:S(2)}) collective-permute-start(bf16[704,256]{1,0:T(8,128)(2,1)S(1)} %get-tuple-element.203), channel_id=1, source_target_pairs={{0,2},{3,1},{4,6},{7,5},{8,10},{11,9},{12,14},{15,13},{16,18},{19,... | collective-permute-start | bytes 1081352 | tf_op jit(solution)/shard_map/ppermute | solution.py:632
  133.3 14.0 %collective-permute-start.20 = (bf16[704,256]{1,0:T(8,128)(2,1)S(1)}, bf16[704,256]{1,0:T(8,128)(2,1)S(1)}, u32[]{:S(2)}, u32[]{:S(2)}) collective-permute-start(bf16[704,256]{1,0:T(8,128)(2,1)S(1)} %get-tuple-element.203), channel_id=1, source_target_pairs={{1,2},{2,1},{5,6},{6,5},{9,10},{10,9},{13,14},{14,13},{17,18},{18,... | collective-permute-start | bytes 1081352 | tf_op jit(solution)/shard_map/ppermute | solution.py:632
  134.0 13.3 %collective-permute-start.21 = (bf16[704,256]{1,0:T(8,128)(2,1)S(1)}, bf16[704,256]{1,0:T(8,128)(2,1)S(1)}, u32[]{:S(2)}, u32[]{:S(2)}) collective-permute-start(bf16[704,256]{1,0:T(8,128)(2,1)S(1)} %get-tuple-element.204), channel_id=1, source_target_pairs={{0,1},{3,2},{4,5},{7,6},{8,9},{11,10},{12,13},{15,14},{16,17},{19,... | collective-permute-start | bytes 1081352 | tf_op jit(solution)/shard_map/ppermute | solution.py:632
  148.4 12.5 %collective-permute-start.22 = (bf16[704,256]{1,0:T(8,128)(2,1)S(1)}, bf16[704,256]{1,0:T(8,128)(2,1)S(1)}, u32[]{:S(2)}, u32[]{:S(2)}) collective-permute-start(bf16[704,256]{1,0:T(8,128)(2,1)S(1)} %add_convert_fusion.7), channel_id=1, source_target_pairs={{0,1},{1,0},{2,3},{3,2},{4,5},{5,4},{6,7},{7,6},{8,9},{9,8},{10,11... | collective-permute-start | bytes 1081352 | tf_op jit(solution)/shard_map/ppermute | solution.py:632
  161.1 13.2 %collective-permute-start.25 = (bf16[704,256]{1,0:T(8,128)(2,1)S(1)}, bf16[704,256]{1,0:T(8,128)(2,1)S(1)}, u32[]{:S(2)}, u32[]{:S(2)}) collective-permute-start(bf16[704,256]{1,0:T(8,128)(2,1)S(1)} %fusion.3.g0), channel_id=1, source_target_pairs={{0,1},{1,0},{2,3},{3,2},{4,5},{5,4},{6,7},{7,6},{8,9},{9,8},{10,11... | collective-permute-start | bytes 1081352 | tf_op jit(solution)/shard_map/ppermute | solution.py:632
  166.8 13.5 %collective-permute-start.31 = (bf16[128,1152]{1,0:T(8,128)(2,1)S(1)}, bf16[128,1152]{1,0:T(8,128)(2,1)S(1)}, u32[]{:S(2)}, u32[]{:S(2)}) collective-permute-start(bf16[128,1152]{1,0:T(8,128)(2,1)S(1)} %get-tuple-element.239), channel_id=1, source_target_pairs={{0,8},{4,12},{8,0},{12,4},{16,24},{20,28},{24,16},{28,20},{1,9},{5... | collective-permute-start | bytes 884744 | tf_op jit(solution)/shard_map/ppermute | solution.py:675
  174.4 16.8 %collective-permute-start.29 = (bf16[704,256]{1,0:T(8,128)(2,1)S(1)}, bf16[704,256]{1,0:T(8,128)(2,1)S(1)}, u32[]{:S(2)}, u32[]{:S(2)}) collective-permute-start(bf16[704,256]{1,0:T(8,128)(2,1)S(1)} %broadcast_select_fusion.2), channel_id=1, source_target_pairs={{0,1},{1,0},{2,3},{3,2},{4,5},{5,4},{6,7},{7,6},{8,9},{9,8},{10,11... | collective-permute-start | bytes 1081352 | tf_op jit(solution)/shard_map/ppermute | solution.py:632
  177.4 13.8 %collective-permute-start.30 = (bf16[704,256]{1,0:T(8,128)(2,1)S(1)}, bf16[704,256]{1,0:T(8,128)(2,1)S(1)}, u32[]{:S(2)}, u32[]{:S(2)}) collective-permute-start(bf16[704,256]{1,0:T(8,128)(2,1)S(1)} %collective-permute-done.25.g1), channel_id=1, source_target_pairs={{1,2},{2,1},{5,6},{6,5},{9,10},{10,9},{13,14},{14,13},{17,18},{18,... | collective-permute-start | bytes 1081352 | tf_op jit(solution)/shard_map/ppermute | solution.py:632
  191.4 16.5 %collective-permute-start.36 = (bf16[704,256]{1,0:T(8,128)(2,1)S(1)}, bf16[704,256]{1,0:T(8,128)(2,1)S(1)}, u32[]{:S(2)}, u32[]{:S(2)}) collective-permute-start(bf16[704,256]{1,0:T(8,128)(2,1)S(1)} %add_convert_fusion.5), channel_id=1, source_target_pairs={{1,2},{2,1},{5,6},{6,5},{9,10},{10,9},{13,14},{14,13},{17,18},{18,... | collective-permute-start | bytes 1081352 | tf_op jit(solution)/shard_map/ppermute | solution.py:632
  192.3 15.6 %collective-permute-start.35 = (bf16[704,256]{1,0:T(8,128)(2,1)S(1)}, bf16[704,256]{1,0:T(8,128)(2,1)S(1)}, u32[]{:S(2)}, u32[]{:S(2)}) collective-permute-start(bf16[704,256]{1,0:T(8,128)(2,1)S(1)} %broadcast_select_fusion.1), channel_id=1, source_target_pairs={{0,1},{1,0},{2,3},{3,2},{4,5},{5,4},{6,7},{7,6},{8,9},{9,8},{10,11... | collective-permute-start | bytes 1081352 | tf_op jit(solution)/shard_map/ppermute | solution.py:632
  208.0 30.4 %collective-permute-start.42 = (bf16[2,128,1152]{2,1,0:T(8,128)(2,1)S(1)}, bf16[2,128,1152]{2,1,0:T(8,128)(2,1)S(1)}, u32[]{:S(2)}, u32[]{:S(2)}) collective-permute-start(bf16[2,128,1152]{2,1,0:T(8,128)(2,1)S(1)} %pad_maximum_fusion.1.refs_2_), channel_id=1, source_target_pairs={{0,16},{4,20},{8,24},{12,28},{16,0},{20,4},{24,8},{28,12},{1,17},{... | collective-permute-start | bytes 1769480 | tf_op jit(solution)/shard_map/ppermute | solution.py:675
  208.2 30.1 %collective-permute-start.41 = (bf16[2,128,1152]{2,1,0:T(8,128)(2,1)S(1)}, bf16[2,128,1152]{2,1,0:T(8,128)(2,1)S(1)}, u32[]{:S(2)}, u32[]{:S(2)}) collective-permute-start(bf16[2,128,1152]{2,1,0:T(8,128)(2,1)S(1)} %pad_maximum_fusion.refs_0_), channel_id=1, source_target_pairs={{0,8},{4,12},{8,0},{12,4},{16,24},{20,28},{24,16},{28,20},{1,9},{5... | collective-permute-start | bytes 1769480 | tf_op jit(solution)/shard_map/ppermute | solution.py:675
  209.2 29.2 %collective-permute-start.40 = (bf16[704,256]{1,0:T(8,128)(2,1)S(1)}, bf16[704,256]{1,0:T(8,128)(2,1)S(1)}, u32[]{:S(2)}, u32[]{:S(2)}) collective-permute-start(bf16[704,256]{1,0:T(8,128)(2,1)S(1)} %add_convert_fusion.3), channel_id=1, source_target_pairs={{1,2},{2,1},{5,6},{6,5},{9,10},{10,9},{13,14},{14,13},{17,18},{18,... | collective-permute-start | bytes 1081352 | tf_op jit(solution)/shard_map/ppermute | solution.py:632
  209.9 28.4 %collective-permute-start.39 = (bf16[704,256]{1,0:T(8,128)(2,1)S(1)}, bf16[704,256]{1,0:T(8,128)(2,1)S(1)}, u32[]{:S(2)}, u32[]{:S(2)}) collective-permute-start(bf16[704,256]{1,0:T(8,128)(2,1)S(1)} %add_convert_fusion.4), channel_id=1, source_target_pairs={{0,1},{1,0},{2,3},{3,2},{4,5},{5,4},{6,7},{7,6},{8,9},{9,8},{10,11... | collective-permute-start | bytes 1081352 | tf_op jit(solution)/shard_map/ppermute | solution.py:632
  256.8 13.5 %collective-permute-start.54 = (bf16[704,256]{1,0:T(8,128)(2,1)S(1)}, bf16[704,256]{1,0:T(8,128)(2,1)S(1)}, u32[]{:S(2)}, u32[]{:S(2)}) collective-permute-start(bf16[704,256]{1,0:T(8,128)(2,1)S(1)} %get-tuple-element.303), channel_id=1, source_target_pairs={{0,2},{3,1},{4,6},{7,5},{8,10},{11,9},{12,14},{15,13},{16,18},{19,... | collective-permute-start | bytes 1081352 | tf_op jit(solution)/shard_map/ppermute | solution.py:632
  275.3 14.0 %collective-permute-start.58 = (bf16[2,208,512]{2,1,0:T(8,128)(2,1)S(1)}, bf16[2,208,512]{2,1,0:T(8,128)(2,1)S(1)}, u32[]{:S(2)}, u32[]{:S(2)}) collective-permute-start(bf16[2,208,512]{2,1,0:T(8,128)(2,1)S(1)} %pad_maximum_fusion.3.refs_2_), channel_id=1, source_target_pairs={{0,16},{4,20},{8,24},{12,28},{16,0},{20,4},{24,8},{28,12},{1,17},{... | collective-permute-start | bytes 1277960 | tf_op jit(solution)/shard_map/ppermute | solution.py:675
  (85 other events, 1043.5 us)

commit v5 on v4

--- a/solution.py
+++ b/solution.py
@@ -15,7 +15,7 @@
 ROWS = 64
 TAIL = 16
 FULL_BYTES = 60 * 1024 * 1024
-VMEM_BYTES = 40 * 1024 * 1024
+VMEM_BYTES = 44 * 1024 * 1024
 SMALL_BYTES = 24 * 1024 * 1024
 
 bf16 = jnp.bfloat16

time: 302 us -> 301 us (level)
    unnamed x80 -> x68, local copies, waits for them, and re-layouts: 6.32 us -> 4.1 us
where the time goes in v5:
time: 301 us; the launch traced here: 296 us
  waiting for transfers between devices  112 us (37%)
  starting transfers between devices  94.3 us (31%)
  Pallas kernels  73.3 us (24%)
  other arithmetic  8.09 us (3%)
  local copies, waits for them, and re-layouts  5.62 us (2%)
    ppermute x39, waiting for transfers between devices, send(): return lax.ppermute(rows, 'tensor', pairs)  78.7 us
    pallas_call x15, Pallas kernels, call(): pl.pallas_call(body, out_shape=[jax.ShapeDtypeStruct(s, d) for s, d, _ in...  73.3 us
    ppermute x39, starting transfers between devices, send(): return lax.ppermute(rows, 'tensor', pairs)  72.8 us
    ppermute x30, waiting for transfers between devices, swap(): return lax.ppermute(values, 'dp', [(i, i ^ bit) for i in range(8)])  33.6 us
    ppermute x30, starting transfers between devices, swap(): return lax.ppermute(values, 'dp', [(i, i ^ bit) for i in range(8)])  21.5 us
  transfers between devices with their start and end apart: 69, of which 26 were waited for; matrix products, arithmetic and copies ran while one was open for 3% of the time, Pallas kernels for 19%

profile of v5, /device:TPU:0, one launch (start us, length us, event | category | flops | bytes accessed | tf_op | source)
XLA Modules:
  0.0 296.2 jit_solution(14984126637614676005)
XLA Ops:
  8.5 6.9 %collective-permute-done.x1 = bf16[720,256]{1,0:T(8,128)(2,1)S(1)} collective-permute-done((bf16[720,256]{1,0:T(8,128)(2,1)S(1)}, bf16[720,256]{1,0:T(8,128)(2,1)S(1)}, u32[]{:S(2)}, u32[]{:S(2)}) %collective-permute-start) | collective-permute-done | bytes 368672 | tf_op jit(solution)/shard_map/ppermute | solution.py:632
  15.4 4.8 %collective-permute-start.2 = (bf16[720,256]{1,0:T(8,128)(2,1)S(1)}, bf16[720,256]{1,0:T(8,128)(2,1)S(1)}, u32[]{:S(2)}, u32[]{:S(2)}) collective-permute-start(bf16[720,256]{1,0:T(8,128)(2,1)S(1)} %broadcast_select_fusion), channel_id=1, source_target_pairs={{0,1},{1,0},{2,3},{3,2},{4,5},{5,4},{6,7},{7,6},{8,9},{9,8},{10,11... | collective-permute-start | bytes 1105928 | tf_op jit(solution)/shard_map/ppermute | solution.py:632
  21.0 7.0 %collective-permute-done.2.x3.c1 = bf16[720,256]{1,0:T(8,128)(2,1)S(1)} collective-permute-done((bf16[720,256]{1,0:T(8,128)(2,1)S(1)}, bf16[720,256]{1,0:T(8,128)(2,1)S(1)}, u32[]{:S(2)}, u32[]{:S(2)}) %collective-permute-start.2) | collective-permute-done | bytes 368672 | tf_op jit(solution)/shard_map/ppermute | solution.py:632
  32.4 7.2 %collective-permute-done.4.x5 = bf16[720,256]{1,0:T(8,128)(2,1)S(1)} collective-permute-done((bf16[720,256]{1,0:T(8,128)(2,1)S(1)}, bf16[720,256]{1,0:T(8,128)(2,1)S(1)}, u32[]{:S(2)}, u32[]{:S(2)}) %collective-permute-start.4) | collective-permute-done | bytes 368672 | tf_op jit(solution)/shard_map/ppermute | solution.py:632
  43.5 12.2 %shard_map.246 = (bf16[704,256]{1,0:T(8,128)(2,1)}, bf16[704,256]{1,0:T(8,128)(2,1)}, bf16[704,256]{1,0:T(8,128)(2,1)}, bf16[704,256]{1,0:T(8,128)(2,1)}, bf16[7...) custom-call(s32[4]{0:T(128)} %pad_add_fusion.info_ref, ...), custom_call_target="tpu_custom_call" | custom-call | flops 3229614080 | bytes 14000000 | tf_op jit(solution)/shard_map/pallas_call | solution.py:612
  56.8 3.9 %collective-permute-done.8.c6 = bf16[720,256]{1,0:T(8,128)(2,1)S(1)} collective-permute-done((bf16[720,256]{1,0:T(8,128)(2,1)S(1)}, bf16[720,256]{1,0:T(8,128)(2,1)S(1)}, u32[]{:S(2)}, u32[]{:S(2)}) %collective-permute-start.8) | collective-permute-done | bytes 368672 | tf_op jit(solution)/shard_map/ppermute | solution.py:632
  66.3 6.7 %collective-permute-done.9 = bf16[704,256]{1,0:T(8,128)(2,1)S(1)} collective-permute-done((bf16[704,256]{1,0:T(8,128)(2,1)}, bf16[704,256]{1,0:T(8,128)(2,1)S(1)}, u32[]{:S(2)}, u32[]{:S(2)}) %collective-permute-start.9) | collective-permute-done | bytes 360480 | tf_op jit(solution)/shard_map/ppermute | solution.py:632
  74.2 5.4 %collective-permute-start.11 = (bf16[704,256]{1,0:T(8,128)(2,1)S(1)}, bf16[704,256]{1,0:T(8,128)(2,1)S(1)}, u32[]{:S(2)}, u32[]{:S(2)}) collective-permute-start(bf16[704,256]{1,0:T(8,128)(2,1)S(1)} %add_convert_fusion.9), channel_id=1, source_target_pairs={{0,1},{1,0},{2,3},{3,2},{4,5},{5,4},{6,7},{7,6},{8,9},{9,8},{10,11... | collective-permute-start | bytes 1081352 | tf_op jit(solution)/shard_map/ppermute | solution.py:632
  80.6 6.7 %collective-permute-done.11 = bf16[704,256]{1,0:T(8,128)(2,1)S(1)} collective-permute-done((bf16[704,256]{1,0:T(8,128)(2,1)S(1)}, bf16[704,256]{1,0:T(8,128)(2,1)S(1)}, u32[]{:S(2)}, u32[]{:S(2)}) %collective-permute-start.11) | collective-permute-done | bytes 360480 | tf_op jit(solution)/shard_map/ppermute | solution.py:632
  88.3 6.8 %collective-permute-start.14 = (bf16[704,256]{1,0:T(8,128)(2,1)S(1)}, bf16[704,256]{1,0:T(8,128)(2,1)S(1)}, u32[]{:S(2)}, u32[]{:S(2)}) collective-permute-start(bf16[704,256]{1,0:T(8,128)(2,1)S(1)} %get-tuple-element.196.m0), channel_id=1, source_target_pairs={{0,1},{1,0},{2,3},{3,2},{4,5},{5,4},{6,7},{7,6},{8,9},{9,8},{10,11... | collective-permute-start | bytes 1081352 | tf_op jit(solution)/shard_map/ppermute | solution.py:632
  96.3 5.7 %collective-permute-done.14.m1 = bf16[704,256]{1,0:T(8,128)(2,1)S(1)} collective-permute-done((bf16[704,256]{1,0:T(8,128)(2,1)S(1)}, bf16[704,256]{1,0:T(8,128)(2,1)S(1)}, u32[]{:S(2)}, u32[]{:S(2)}) %collective-permute-start.14) | collective-permute-done | bytes 360480 | tf_op jit(solution)/shard_map/ppermute | solution.py:632
  104.1 6.1 %collective-permute-done.16.m3 = bf16[704,256]{1,0:T(8,128)(2,1)S(1)} collective-permute-done((bf16[704,256]{1,0:T(8,128)(2,1)S(1)}, bf16[704,256]{1,0:T(8,128)(2,1)S(1)}, u32[]{:S(2)}, u32[]{:S(2)}) %collective-permute-start.16) | collective-permute-done | bytes 360480 | tf_op jit(solution)/shard_map/ppermute | solution.py:632
  110.2 10.2 %collective-permute-done.18.m5 = bf16[704,256]{1,0:T(8,128)(2,1)S(1)} collective-permute-done((bf16[704,256]{1,0:T(8,128)(2,1)S(1)}, bf16[704,256]{1,0:T(8,128)(2,1)S(1)}, u32[]{:S(2)}, u32[]{:S(2)}) %collective-permute-start.18) | collective-permute-done | bytes 360480 | tf_op jit(solution)/shard_map/ppermute | solution.py:632
  120.4 11.1 %shard_map.247 = (bf16[704,256]{1,0:T(8,128)(2,1)S(1)}, bf16[704,256]{1,0:T(8,128)(2,1)S(1)}, bf16[704,256]{1,0:T(8,128)(2,1)S(1)}, bf16[704,256]{1,0:T(8,128)(2...) custom-call(s32[4]{0:T(128)S(1)} %copy-done.7, ...), custom_call_target="tpu_custom_call" | custom-call | flops 5536481280 | bytes 16000000 | tf_op jit(solution)/shard_map/pallas_call | solution.py:612
  138.3 8.6 %shard_map.248 = (bf16[704,256]{1,0:T(8,128)(2,1)S(1)}, bf16[704,256]{1,0:T(8,128)(2,1)S(1)}, bf16[704,256]{1,0:T(8,128)(2,1)S(1)}, bf16[704,256]{1,0:T(8,128)(2...) custom-call(s32[4]{0:T(128)S(1)} %copy-done.7, bf16[704,1024]{1,0:T(8,128)(2,1)S(1)} %get-tuple-element.205.n2_hbm, ...), custom_call_target="tpu_custom_call" | custom-call | flops 4429185024 | bytes 14000000 | tf_op jit(solution)/shard_map/pallas_call | solution.py:612
  153.2 7.3 %collective-permute-done.22 = bf16[704,256]{1,0:T(8,128)(2,1)S(1)} collective-permute-done((bf16[704,256]{1,0:T(8,128)(2,1)S(1)}, bf16[704,256]{1,0:T(8,128)(2,1)S(1)}, u32[]{:S(2)}, u32[]{:S(2)}) %collective-permute-start.22) | collective-permute-done | bytes 360480 | tf_op jit(solution)/shard_map/ppermute | solution.py:632
  166.9 6.4 %collective-permute-done.27.got_on_x = bf16[128,1152]{1,0:T(8,128)(2,1)S(1)} collective-permute-done((bf16[128,1152]{1,0:T(8,128)(2,1)S(1)}, bf16[128,1152]{1,0:T(8,128)(2,1)S(1)}, u32[]{:S(2)}, u32[]{:S(2)}) %collective-permute-start.27) | collective-permute-done | bytes 294944 | tf_op jit(solution)/shard_map/ppermute | solution.py:675
  181.3 5.6 %collective-permute-done.33.got_y = bf16[128,1152]{1,0:T(8,128)(2,1)S(1)} collective-permute-done((bf16[128,1152]{1,0:T(8,128)(2,1)S(1)}, bf16[128,1152]{1,0:T(8,128)(2,1)S(1)}, u32[]{:S(2)}, u32[]{:S(2)}) %collective-permute-start.33) | collective-permute-done | bytes 294944 | tf_op jit(solution)/shard_map/ppermute | solution.py:675
  191.9 4.6 %collective-permute-start.35 = (bf16[704,256]{1,0:T(8,128)(2,1)S(1)}, bf16[704,256]{1,0:T(8,128)(2,1)S(1)}, u32[]{:S(2)}, u32[]{:S(2)}) collective-permute-start(bf16[704,256]{1,0:T(8,128)(2,1)S(1)} %broadcast_select_fusion.1), channel_id=1, source_target_pairs={{0,1},{1,0},{2,3},{3,2},{4,5},{5,4},{6,7},{7,6},{8,9},{9,8},{10,11... | collective-permute-start | bytes 1081352 | tf_op jit(solution)/shard_map/ppermute | solution.py:632
  198.5 6.3 %collective-permute-done.37 = bf16[128,1152]{1,0:T(8,128)(2,1)S(1)} collective-permute-done((bf16[128,1152]{1,0:T(8,128)(2,1)S(1)}, bf16[128,1152]{1,0:T(8,128)(2,1)S(1)}, u32[]{:S(2)}, u32[]{:S(2)}) %collective-permute-start.37) | collective-permute-done | bytes 294944 | tf_op jit(solution)/shard_map/ppermute | solution.py:675
  211.7 25.5 %shard_map.252 = (bf16[704,256]{1,0:T(8,128)(2,1)S(1)}, bf16[704,256]{1,0:T(8,128)(2,1)S(1)}, bf16[704,256]{1,0:T(8,128)(2,1)S(1)}, bf16[704,256]{1,0:T(8,128)(2...) custom-call(s32[4]{0:T(128)S(1)} %copy-done.7, ...), custom_call_target="tpu_custom_call" | custom-call | flops 6966738944 | bytes 20000000 | tf_op jit(solution)/shard_map/pallas_call | solution.py:612
  261.9 5.3 %collective-permute-start.56 = (bf16[704,256]{1,0:T(8,128)(2,1)S(1)}, bf16[704,256]{1,0:T(8,128)(2,1)S(1)}, u32[]{:S(2)}, u32[]{:S(2)}) collective-permute-start(bf16[704,256]{1,0:T(8,128)(2,1)S(1)} %get-tuple-element.304), channel_id=1, source_target_pairs={{0,1},{3,2},{4,5},{7,6},{8,9},{11,10},{12,13},{15,14},{16,17},{19,... | collective-permute-start | bytes 1081352 | tf_op jit(solution)/shard_map/ppermute | solution.py:632
  269.2 4.0 %collective-permute-done.52 = bf16[208,512]{1,0:T(8,128)(2,1)S(1)} collective-permute-done((bf16[208,512]{1,0:T(8,128)(2,1)S(1)}, bf16[208,512]{1,0:T(8,128)(2,1)S(1)}, u32[]{:S(2)}, u32[]{:S(2)}) %collective-permute-start.52) | collective-permute-done | bytes 213024 | tf_op jit(solution)/shard_map/ppermute | solution.py:675
  280.0 4.9 %shard_map.258 = (f32[1024,768]{1,0:T(8,128)}, f32[1024,768]{1,0:T(8,128)}, f32[768,1024]{1,0:T(8,128)}) custom-call(s32[4]{0:T(128)S(1)} %copy-done.7, bf16[2,128,1152]{2,1,0:T(8,128)(2,1)S(1)} %pad_maximum_fusion.refs_0_, bf16[2,128,1152]{2,1,0:T(8,128)(2,1)S(1)} %collective-permute-done.41.refs_1_, bf16[2,128,1152]{2,1,0:T(8,128)(2,1)S(1)} %pad_maximum_fusion.1.refs_2_, ...), custom_call_target="tpu_custom_call" | custom-call | bytes 14000000 | tf_op jit(solution)/shard_map/pallas_call | solution.py:612
  (227 shorter events, 114.5 us)
Async XLA Ops:
  15.4 12.5 %collective-permute-start.2 = (bf16[720,256]{1,0:T(8,128)(2,1)S(1)}, bf16[720,256]{1,0:T(8,128)(2,1)S(1)}, u32[]{:S(2)}, u32[]{:S(2)}) collective-permute-start(bf16[720,256]{1,0:T(8,128)(2,1)S(1)} %broadcast_select_fusion), channel_id=1, source_target_pairs={{0,1},{1,0},{2,3},{3,2},{4,5},{5,4},{6,7},{7,6},{8,9},{9,8},{10,11... | collective-permute-start | bytes 1105928 | tf_op jit(solution)/shard_map/ppermute | solution.py:632
  39.7 16.1 %collective-permute-start.6 = (bf16[720,256]{1,0:T(8,128)(2,1)S(1)}, bf16[720,256]{1,0:T(8,128)(2,1)S(1)}, u32[]{:S(2)}, u32[]{:S(2)}) collective-permute-start(bf16[720,256]{1,0:T(8,128)(2,1)S(1)} %concatenate.9.c0), channel_id=1, source_target_pairs={{1,2},{2,1},{5,6},{6,5},{9,10},{10,9},{13,14},{14,13},{17,18},{18,... | collective-permute-start | bytes 1105928 | tf_op jit(solution)/shard_map/ppermute | solution.py:632
  40.4 16.5 %collective-permute-start.7 = (bf16[720,256]{1,0:T(8,128)(2,1)S(1)}, bf16[720,256]{1,0:T(8,128)(2,1)S(1)}, u32[]{:S(2)}, u32[]{:S(2)}) collective-permute-start(bf16[720,256]{1,0:T(8,128)(2,1)S(1)} %concatenate.9.c0), channel_id=1, source_target_pairs={{1,0},{2,3},{5,4},{6,7},{9,8},{10,11},{13,12},{14,15},{17,16},{18,... | collective-permute-start | bytes 1105928 | tf_op jit(solution)/shard_map/ppermute | solution.py:632
  41.7 19.1 %collective-permute-start.8 = (bf16[720,256]{1,0:T(8,128)(2,1)S(1)}, bf16[720,256]{1,0:T(8,128)(2,1)S(1)}, u32[]{:S(2)}, u32[]{:S(2)}) collective-permute-start(bf16[720,256]{1,0:T(8,128)(2,1)S(1)} %collective-permute-done.5.c5), channel_id=1, source_target_pairs={{1,0},{2,3},{5,4},{6,7},{9,8},{10,11},{13,12},{14,15},{17,16},{18,... | collective-permute-start | bytes 1105928 | tf_op jit(solution)/shard_map/ppermute | solution.py:632
  66.0 13.6 %collective-permute-start.12 = (bf16[704,256]{1,0:T(8,128)(2,1)S(1)}, bf16[704,256]{1,0:T(8,128)(2,1)S(1)}, u32[]{:S(2)}, u32[]{:S(2)}) collective-permute-start(bf16[704,256]{1,0:T(8,128)(2,1)S(1)} %slice_select_fusion), channel_id=1, source_target_pairs={{0,1},{1,0},{2,3},{3,2},{4,5},{5,4},{6,7},{7,6},{8,9},{9,8},{10,11... | collective-permute-start | bytes 1081352 | tf_op jit(solution)/shard_map/ppermute | solution.py:632
  74.2 13.1 %collective-permute-start.11 = (bf16[704,256]{1,0:T(8,128)(2,1)S(1)}, bf16[704,256]{1,0:T(8,128)(2,1)S(1)}, u32[]{:S(2)}, u32[]{:S(2)}) collective-permute-start(bf16[704,256]{1,0:T(8,128)(2,1)S(1)} %add_convert_fusion.9), channel_id=1, source_target_pairs={{0,1},{1,0},{2,3},{3,2},{4,5},{5,4},{6,7},{7,6},{8,9},{9,8},{10,11... | collective-permute-start | bytes 1081352 | tf_op jit(solution)/shard_map/ppermute | solution.py:632
  88.3 13.8 %collective-permute-start.14 = (bf16[704,256]{1,0:T(8,128)(2,1)S(1)}, bf16[704,256]{1,0:T(8,128)(2,1)S(1)}, u32[]{:S(2)}, u32[]{:S(2)}) collective-permute-start(bf16[704,256]{1,0:T(8,128)(2,1)S(1)} %get-tuple-element.196.m0), channel_id=1, source_target_pairs={{0,1},{1,0},{2,3},{3,2},{4,5},{5,4},{6,7},{7,6},{8,9},{9,8},{10,11... | collective-permute-start | bytes 1081352 | tf_op jit(solution)/shard_map/ppermute | solution.py:632
  95.0 15.1 %collective-permute-start.16 = (bf16[704,256]{1,0:T(8,128)(2,1)S(1)}, bf16[704,256]{1,0:T(8,128)(2,1)S(1)}, u32[]{:S(2)}, u32[]{:S(2)}) collective-permute-start(bf16[704,256]{1,0:T(8,128)(2,1)S(1)} %collective-permute-done.15.m2), channel_id=1, source_target_pairs={{1,0},{2,3},{5,4},{6,7},{9,8},{10,11},{13,12},{14,15},{17,16},{18,... | collective-permute-start | bytes 1081352 | tf_op jit(solution)/shard_map/ppermute | solution.py:632
  102.8 17.6 %collective-permute-start.18 = (bf16[704,256]{1,0:T(8,128)(2,1)S(1)}, bf16[704,256]{1,0:T(8,128)(2,1)S(1)}, u32[]{:S(2)}, u32[]{:S(2)}) collective-permute-start(bf16[704,256]{1,0:T(8,128)(2,1)S(1)} %collective-permute-done.14.m1), channel_id=1, source_target_pairs={{2,0},{1,3},{6,4},{5,7},{10,8},{9,11},{14,12},{13,15},{18,16},{17,... | collective-permute-start | bytes 1081352 | tf_op jit(solution)/shard_map/ppermute | solution.py:632
  131.4 15.5 %collective-permute-start.19 = (bf16[704,256]{1,0:T(8,128)(2,1)S(1)}, bf16[704,256]{1,0:T(8,128)(2,1)S(1)}, u32[]{:S(2)}, u32[]{:S(2)}) collective-permute-start(bf16[704,256]{1,0:T(8,128)(2,1)S(1)} %get-tuple-element.203), channel_id=1, source_target_pairs={{0,2},{3,1},{4,6},{7,5},{8,10},{11,9},{12,14},{15,13},{16,18},{19,... | collective-permute-start | bytes 1081352 | tf_op jit(solution)/shard_map/ppermute | solution.py:632
  132.9 14.0 %collective-permute-start.20 = (bf16[704,256]{1,0:T(8,128)(2,1)S(1)}, bf16[704,256]{1,0:T(8,128)(2,1)S(1)}, u32[]{:S(2)}, u32[]{:S(2)}) collective-permute-start(bf16[704,256]{1,0:T(8,128)(2,1)S(1)} %get-tuple-element.203), channel_id=1, source_target_pairs={{1,2},{2,1},{5,6},{6,5},{9,10},{10,9},{13,14},{14,13},{17,18},{18,... | collective-permute-start | bytes 1081352 | tf_op jit(solution)/shard_map/ppermute | solution.py:632
  133.6 13.3 %collective-permute-start.21 = (bf16[704,256]{1,0:T(8,128)(2,1)S(1)}, bf16[704,256]{1,0:T(8,128)(2,1)S(1)}, u32[]{:S(2)}, u32[]{:S(2)}) collective-permute-start(bf16[704,256]{1,0:T(8,128)(2,1)S(1)} %get-tuple-element.204), channel_id=1, source_target_pairs={{0,1},{3,2},{4,5},{7,6},{8,9},{11,10},{12,13},{15,14},{16,17},{19,... | collective-permute-start | bytes 1081352 | tf_op jit(solution)/shard_map/ppermute | solution.py:632
  160.8 13.2 %collective-permute-start.25 = (bf16[704,256]{1,0:T(8,128)(2,1)S(1)}, bf16[704,256]{1,0:T(8,128)(2,1)S(1)}, u32[]{:S(2)}, u32[]{:S(2)}) collective-permute-start(bf16[704,256]{1,0:T(8,128)(2,1)S(1)} %fusion.3.g0), channel_id=1, source_target_pairs={{0,1},{1,0},{2,3},{3,2},{4,5},{5,4},{6,7},{7,6},{8,9},{9,8},{10,11... | collective-permute-start | bytes 1081352 | tf_op jit(solution)/shard_map/ppermute | solution.py:632
  166.4 13.4 %collective-permute-start.31 = (bf16[128,1152]{1,0:T(8,128)(2,1)S(1)}, bf16[128,1152]{1,0:T(8,128)(2,1)S(1)}, u32[]{:S(2)}, u32[]{:S(2)}) collective-permute-start(bf16[128,1152]{1,0:T(8,128)(2,1)S(1)} %get-tuple-element.239), channel_id=1, source_target_pairs={{0,8},{4,12},{8,0},{12,4},{16,24},{20,28},{24,16},{28,20},{1,9},{5... | collective-permute-start | bytes 884744 | tf_op jit(solution)/shard_map/ppermute | solution.py:675
  174.0 16.8 %collective-permute-start.29 = (bf16[704,256]{1,0:T(8,128)(2,1)S(1)}, bf16[704,256]{1,0:T(8,128)(2,1)S(1)}, u32[]{:S(2)}, u32[]{:S(2)}) collective-permute-start(bf16[704,256]{1,0:T(8,128)(2,1)S(1)} %broadcast_select_fusion.2), channel_id=1, source_target_pairs={{0,1},{1,0},{2,3},{3,2},{4,5},{5,4},{6,7},{7,6},{8,9},{9,8},{10,11... | collective-permute-start | bytes 1081352 | tf_op jit(solution)/shard_map/ppermute | solution.py:632
  177.0 13.8 %collective-permute-start.30 = (bf16[704,256]{1,0:T(8,128)(2,1)S(1)}, bf16[704,256]{1,0:T(8,128)(2,1)S(1)}, u32[]{:S(2)}, u32[]{:S(2)}) collective-permute-start(bf16[704,256]{1,0:T(8,128)(2,1)S(1)} %collective-permute-done.25.g1), channel_id=1, source_target_pairs={{1,2},{2,1},{5,6},{6,5},{9,10},{10,9},{13,14},{14,13},{17,18},{18,... | collective-permute-start | bytes 1081352 | tf_op jit(solution)/shard_map/ppermute | solution.py:632
  191.0 16.4 %collective-permute-start.36 = (bf16[704,256]{1,0:T(8,128)(2,1)S(1)}, bf16[704,256]{1,0:T(8,128)(2,1)S(1)}, u32[]{:S(2)}, u32[]{:S(2)}) collective-permute-start(bf16[704,256]{1,0:T(8,128)(2,1)S(1)} %add_convert_fusion.5), channel_id=1, source_target_pairs={{1,2},{2,1},{5,6},{6,5},{9,10},{10,9},{13,14},{14,13},{17,18},{18,... | collective-permute-start | bytes 1081352 | tf_op jit(solution)/shard_map/ppermute | solution.py:632
  191.9 15.5 %collective-permute-start.35 = (bf16[704,256]{1,0:T(8,128)(2,1)S(1)}, bf16[704,256]{1,0:T(8,128)(2,1)S(1)}, u32[]{:S(2)}, u32[]{:S(2)}) collective-permute-start(bf16[704,256]{1,0:T(8,128)(2,1)S(1)} %broadcast_select_fusion.1), channel_id=1, source_target_pairs={{0,1},{1,0},{2,3},{3,2},{4,5},{5,4},{6,7},{7,6},{8,9},{9,8},{10,11... | collective-permute-start | bytes 1081352 | tf_op jit(solution)/shard_map/ppermute | solution.py:632
  207.4 29.8 %collective-permute-start.42 = (bf16[2,128,1152]{2,1,0:T(8,128)(2,1)S(1)}, bf16[2,128,1152]{2,1,0:T(8,128)(2,1)S(1)}, u32[]{:S(2)}, u32[]{:S(2)}) collective-permute-start(bf16[2,128,1152]{2,1,0:T(8,128)(2,1)S(1)} %pad_maximum_fusion.1.refs_2_), channel_id=1, source_target_pairs={{0,16},{4,20},{8,24},{12,28},{16,0},{20,4},{24,8},{28,12},{1,17},{... | collective-permute-start | bytes 1769480 | tf_op jit(solution)/shard_map/ppermute | solution.py:675
  207.7 29.5 %collective-permute-start.41 = (bf16[2,128,1152]{2,1,0:T(8,128)(2,1)S(1)}, bf16[2,128,1152]{2,1,0:T(8,128)(2,1)S(1)}, u32[]{:S(2)}, u32[]{:S(2)}) collective-permute-start(bf16[2,128,1152]{2,1,0:T(8,128)(2,1)S(1)} %pad_maximum_fusion.refs_0_), channel_id=1, source_target_pairs={{0,8},{4,12},{8,0},{12,4},{16,24},{20,28},{24,16},{28,20},{1,9},{5... | collective-permute-start | bytes 1769480 | tf_op jit(solution)/shard_map/ppermute | solution.py:675
  208.6 28.6 %collective-permute-start.40 = (bf16[704,256]{1,0:T(8,128)(2,1)S(1)}, bf16[704,256]{1,0:T(8,128)(2,1)S(1)}, u32[]{:S(2)}, u32[]{:S(2)}) collective-permute-start(bf16[704,256]{1,0:T(8,128)(2,1)S(1)} %add_convert_fusion.3), channel_id=1, source_target_pairs={{1,2},{2,1},{5,6},{6,5},{9,10},{10,9},{13,14},{14,13},{17,18},{18,... | collective-permute-start | bytes 1081352 | tf_op jit(solution)/shard_map/ppermute | solution.py:632
  209.5 27.6 %collective-permute-start.39 = (bf16[704,256]{1,0:T(8,128)(2,1)S(1)}, bf16[704,256]{1,0:T(8,128)(2,1)S(1)}, u32[]{:S(2)}, u32[]{:S(2)}) collective-permute-start(bf16[704,256]{1,0:T(8,128)(2,1)S(1)} %add_convert_fusion.4), channel_id=1, source_target_pairs={{0,1},{1,0},{2,3},{3,2},{4,5},{5,4},{6,7},{7,6},{8,9},{9,8},{10,11... | collective-permute-start | bytes 1081352 | tf_op jit(solution)/shard_map/ppermute | solution.py:632
  255.7 13.5 %collective-permute-start.54 = (bf16[704,256]{1,0:T(8,128)(2,1)S(1)}, bf16[704,256]{1,0:T(8,128)(2,1)S(1)}, u32[]{:S(2)}, u32[]{:S(2)}) collective-permute-start(bf16[704,256]{1,0:T(8,128)(2,1)S(1)} %get-tuple-element.303), channel_id=1, source_target_pairs={{0,2},{3,1},{4,6},{7,5},{8,10},{11,9},{12,14},{15,13},{16,18},{19,... | collective-permute-start | bytes 1081352 | tf_op jit(solution)/shard_map/ppermute | solution.py:632
  274.2 14.0 %collective-permute-start.58 = (bf16[2,208,512]{2,1,0:T(8,128)(2,1)S(1)}, bf16[2,208,512]{2,1,0:T(8,128)(2,1)S(1)}, u32[]{:S(2)}, u32[]{:S(2)}) collective-permute-start(bf16[2,208,512]{2,1,0:T(8,128)(2,1)S(1)} %pad_maximum_fusion.3.refs_2_), channel_id=1, source_target_pairs={{0,16},{4,20},{8,24},{12,28},{16,0},{20,4},{24,8},{28,12},{1,17},{... | collective-permute-start | bytes 1277960 | tf_op jit(solution)/shard_map/ppermute | solution.py:675
  (79 other events, 794.6 us)
